TPU v7x, 32 devices: a whole 2x2x4 slice. The times are simulated.
32 devices in a mesh: group: 2 (over y), row: 4 (over z), col: 2 (over x), sub: 2 (over core).
Axes of the slice: x: 2, y: 2, z: 4, core: 2. Of those that a mesh axis runs over, the one named last changes fastest.
Arguments:
- traces: bfloat16 [8, 5120, 16384], P(('group', 'sub'), 'col', 'row'), parts along dimension 0, may hold values from -200 to 200
- quality_mask: int32 [5120], P('col'), may hold values 0 or 1
- band_bins: int32 [128], replicated, may hold values from 17 to 163, as said below
Outputs:
- correlation: float32 [8, 5120, 5120], P('group', 'row', ('col', 'sub')), parts along dimension 0
There are 2 independent parts, one for each index of `group`. A program takes and returns all parts, laid end to end along the dimension named above; an argument that names none is the same for every part. Nothing has to cross between parts.
Inputs may be any that keep to these rules, and one draw needn't show every extreme that they name: `band_bins`: 128 distinct bin numbers; the lowest and the highest bin of the band are among them.
All inputs are finite; a program needn't handle non-finite values. No bound on the sum of `quality_mask` on one device may be relied on, other than what follows from the above.
Results may differ from a plain program's by a relative error of at most 0.0053.
Values may be sent and summed in bfloat16 or wider, within the bound.
No kernel may reach another device: no remote copies, remote signals or barrier semaphores. Data moves between devices by JAX's collectives and lax.ppermute only.
A program may use at most 320 MiB of HBM per device.

v0:
```python
import math

import jax
import jax.numpy as jnp
from jax import lax
from jax.sharding import PartitionSpec as P

W = 16384
LAGS = 4
LAG_STEP = 50


TWO_PI = 2.0 * math.pi


def band_table(sample_times, bin_ids, length):
    window_taper = 0.5 - 0.5 * jnp.cos(TWO_PI / length * sample_times.astype(jnp.float32))
    phase_index = sample_times[:, None] * bin_ids[None, :] % length
    angles = TWO_PI / length * phase_index.astype(jnp.float32)
    cosine = window_taper[:, None] * jnp.cos(angles)
    sine_part = -window_taper[:, None] * jnp.sin(angles)
    return jnp.concatenate([cosine, sine_part], axis=1).astype(jnp.bfloat16)


def whiten(spectra, quality):
    nbins = spectra.shape[-1] // 2
    real_part = spectra[..., :nbins]
    imag_part = spectra[..., nbins:]
    band_rms = jnp.sqrt(jnp.mean(spectra * spectra, axis=-1, keepdims=True) + 1e-05)
    magnitude = jnp.sqrt(real_part * real_part + imag_part * imag_part)
    divisor = jnp.maximum(magnitude, 0.25 * band_rms)
    scaled = jnp.concatenate([real_part / divisor, imag_part / divisor], axis=-1)
    return (quality.astype(jnp.float32)[:, None] * scaled).astype(jnp.bfloat16)


def rotate(white, bin_ids, lag_shift, length):
    nbins = white.shape[-1] // 2
    phase_index = bin_ids * lag_shift % length
    angles = TWO_PI / length * phase_index.astype(jnp.float32)
    cosine = jnp.cos(angles)
    sine_part = jnp.sin(angles)
    real_part = white[..., :nbins].astype(jnp.float32)
    imag_part = white[..., nbins:].astype(jnp.float32)
    turned = jnp.concatenate(
        [real_part * cosine + imag_part * sine_part, imag_part * cosine - real_part * sine_part],
        axis=-1,
    )
    return turned.astype(jnp.bfloat16)


def pair_products(row_spectra, column_spectra, bin_ids, length):
    results = []
    for lag_index in range(LAGS):
        lag_shift = (lag_index - LAGS // 2) * LAG_STEP
        rotated = rotate(row_spectra, bin_ids, lag_shift, length)
        results.append(
            jnp.einsum("wpk,wqk->pq", rotated, column_spectra, preferred_element_type=jnp.float32)
        )
    return jnp.stack(results)


def local(traces, quality_mask, band_bins):
    nbins = band_bins.shape[0]
    windows_here = traces.shape[0]
    samples_here = traces.shape[2]
    sample_times = lax.axis_index("row") * samples_here + jnp.arange(samples_here, dtype=jnp.int32)
    table = band_table(sample_times, band_bins, W)
    partial_value = jnp.einsum("wct,tk->wck", traces, table, preferred_element_type=jnp.float32)
    spectra_all = lax.psum(partial_value, "row")
    column_spectra = whiten(spectra_all, quality_mask)
    local_channels = traces.shape[1] // lax.axis_size("row")
    white = lax.dynamic_slice_in_dim(
        column_spectra, lax.axis_index("row") * local_channels, local_channels, 1
    )
    row_spectra = lax.all_gather(white, "col", axis=1, tiled=True)
    scale = 1.0 / math.sqrt(lax.axis_size("sub") * windows_here * nbins)
    partial_products = pair_products(row_spectra, column_spectra, band_bins, W)
    summed = lax.psum_scatter(partial_products, "sub", scatter_dimension=2, tiled=True)
    return summed * scale


def solution(mesh):
    in_specs = (P(("group", "sub"), "col", "row"), P("col"), P())
    out_specs = P("group", "row", ("col", "sub"))
    return jax.shard_map(local, mesh=mesh, in_specs=in_specs, out_specs=out_specs, check_vma=False)
```

profile of v0, /device:TPU:0, one launch (start us, length us, event | category | flops | bytes accessed | tf_op | source)
XLA Modules:
  0.0 412.2 jit_solution(8185256579321833247)
XLA Ops:
  6.5 0.0 all-reduce.2.cloned.1.call-start
  6.5 0.1 multiply_subtract_fusion
  6.6 9.4 %multiply_convert_fusion.1 = (bf16[4096,128]{0,1:T(8,128)(2,1)S(1)}, bf16[4096,128]{0,1:T(8,128)(2,1)S(1)}) fusion(s32[128]{0:T(128)} %param.5, s32[4096]{0:T(1024)S(1)} %iota_add_fusion, f32[4096]{0:T(1024)S(1)} %get-tuple-element.29, f32[4096]{0:T(1024)S(1)} %get-tuple-element.30), kind=kLoop, calls=%fused_computation.41 | loop fusion | flops 9437184 | bytes 2146816 | tf_op jit(solution)/shard_map/convert.8
  16.0 19.4 %convolution_bitcast_fusion.4 = f32[2,2560,256]{1,2,0:T(8,128)} fusion(bf16[2,2560,4096]{2,1,0:T(8,128)(2,1)} %param.3, bf16[4096,128]{0,1:T(8,128)(2,1)S(1)} %get-tuple-element.24, bf16[4096,128]{0,1:T(8,128)(2,1)S(1)} %get-tuple-element.23), kind=kOutput, calls=%fused_computation.9 | convolution fusion | flops 10741612544 | bytes 49283072 | tf_op jit(solution)/shard_map/wct,tk->wck/dot_general | solution.py:68
  35.4 0.0 copy-start.2
  35.4 0.0 all-reduce.2.cloned.1.call-update
  35.4 0.0 all-gather.2.cloned.1.call-start
  35.5 0.6 copy-done.2
  36.1 191.1 %all-reduce.2.cloned.1.call-done = f32[2,2560,256]{1,2,0:T(8,128)} async-done(((f32[2,2560,256]{1,2,0:T(8,128)}), f32[2,2560,256]{1,2,0:T(8,128)}) %all-reduce.2.cloned.1.call-update) | async-done | bytes 5242896 | tf_op jit(solution)/shard_map/psum | solution.py:69
  227.2 3.1 multiply_reduce_fusion
  230.4 0.9 copy-done
  231.2 1.2 fusion.2
  232.4 0.0 copy-start.3
  232.4 0.6 fusion
  233.0 0.9 constant_dynamic-slice_fusion
  233.9 0.0 all-gather.2.cloned.1.call-update
  233.9 0.2 reduce-scatter.2.cloned.1.call-start
  234.2 0.0 copy-done.3
  234.2 0.1 fusion.49
  234.4 22.9 %all-gather.2.cloned.1.call-done = bf16[2,1280,256]{1,2,0:T(8,128)(2,1)} async-done(((bf16[2,640,256]{1,2,0:T(8,128)(2,1)}), bf16[2,1280,256]{1,2,0:T(8,128)(2,1)}) %all-gather.2.cloned.1.call-update) | async-done | bytes 1310736 | tf_op jit(solution)/shard_map/all_gather | solution.py:75
  257.3 2.5 fusion.9
  259.9 0.0 copy-start.1
  259.9 6.7 %convolution_bitcast_fusion.3 = f32[1,1280,2560]{2,1,0:T(8,128)} fusion(bf16[2,2560,256]{1,2,0:T(8,128)(2,1)S(1)} %fusion, bf16[2,1280,128]{1,2,0:T(8,128)(2,1)S(1)} %get-tuple-element.14, bf16[2,1280,128]{1,2,0:T(8,128)(2,1)S(1)} %get-tuple-element.13), kind=kOutput, calls=%fused_computation.5 | convolution fusion | flops 3358064640 | bytes 17039360 | tf_op jit(solution)/shard_map/wpk,wqk->pq/dot_general | solution.py:57
  266.5 0.0 copy-done.1
  266.5 0.5 fusion.13
  267.1 6.5 %convolution_bitcast_fusion.2 = f32[1,1280,2560]{2,1,0:T(8,128)} fusion(bf16[2,2560,256]{1,2,0:T(8,128)(2,1)S(1)} %fusion, bf16[2,1280,128]{1,2,0:T(8,128)(2,1)S(1)} %get-tuple-element.16, bf16[2,1280,128]{1,2,0:T(8,128)(2,1)S(1)} %get-tuple-element.15), kind=kOutput, calls=%fused_computation.4 | convolution fusion | flops 3358064640 | bytes 17039360 | tf_op jit(solution)/shard_map/wpk,wqk->pq/dot_general | solution.py:57
  273.6 6.8 %convolution_bitcast_fusion = f32[1,1280,2560]{2,1,0:T(8,128)} fusion(bf16[2,2560,256]{1,2,0:T(8,128)(2,1)S(1)} %fusion, bf16[2,1280,128]{1,2,0:T(8,128)(2,1)S(1)} %get-tuple-element.19, bf16[2,1280,128]{1,2,0:T(8,128)(2,1)S(1)} %get-tuple-element.20), kind=kOutput, calls=%fused_computation.2 | convolution fusion | flops 3358064640 | bytes 17039360 | tf_op jit(solution)/shard_map/wpk,wqk->pq/dot_general | solution.py:57
  280.4 6.6 %convolution_bitcast_fusion.1 = f32[1,1280,2560]{2,1,0:T(8,128)} fusion(bf16[2,2560,256]{1,2,0:T(8,128)(2,1)S(1)} %fusion, bf16[2,1280,128]{1,2,0:T(8,128)(2,1)S(1)} %get-tuple-element.21, bf16[2,1280,128]{1,2,0:T(8,128)(2,1)S(1)} %get-tuple-element.22), kind=kOutput, calls=%fused_computation.3 | convolution fusion | flops 3358064640 | bytes 17039360 | tf_op jit(solution)/shard_map/wpk,wqk->pq/dot_general | solution.py:57
  287.1 34.9 %pad_maximum_fusion = f32[4,1280,2560]{2,1,0:T(8,128)} fusion(f32[1,1280,2560]{2,1,0:T(8,128)} %convolution_bitcast_fusion, f32[1,1280,2560]{2,1,0:T(8,128)} %convolution_bitcast_fusion.1, f32[1,1280,2560]{2,1,0:T(8,128)} %convolution_bitcast_fusion.2, f32[1,1280,2560]{2,1,0:T(8,128)} %convolution_bitcast_fusion.3), kind=kLoop, calls=%fused_computation | loop fusion | flops 39321600 | bytes 104857600 | tf_op jit(solution)/shard_map/stack | solution.py:59
  322.0 0.0 reduce-scatter.2.cloned.1.call-update
  322.0 65.9 %reduce-scatter.2.cloned.1.call-done = f32[4,1280,1280]{2,1,0:T(8,128)} async-done(((f32[4,1280,2560]{2,1,0:T(8,128)}), f32[4,1280,1280]{2,1,0:T(8,128)}) %reduce-scatter.2.cloned.1.call-update) | async-done | bytes 26214416 | tf_op jit(solution)/shard_map/reduce_scatter | solution.py:78
  387.9 17.8 %broadcast_multiply_fusion = f32[4,1280,1280]{2,1,0:T(8,128)} fusion(f32[4,1280,1280]{2,1,0:T(8,128)} %reduce-scatter.2.cloned.1.call-done), kind=kLoop, calls=%fused_computation.1 | loop fusion | flops 6553600 | bytes 52428800 | tf_op jit(solution)/shard_map/mul | solution.py:79
  (7 shorter events, 0.2 us)
Async XLA Ops:
  6.5 220.7 %all-reduce.2.cloned.1.call-start = ((), (), s32[]{:S(2)}) async-start(), calls=%async_computation.1 | async-start | bytes 10485760 | tf_op jit(solution)/shard_map/psum | solution.py:69
  35.4 0.7 copy-start.2
  35.4 221.9 %all-gather.2.cloned.1.call-start = ((), (), s32[]{:S(2)}) async-start(), calls=%async_computation.2 | async-start | bytes 1966080 | tf_op jit(solution)/shard_map/all_gather | solution.py:75
  227.2 4.0 copy-start
  232.4 1.7 copy-start.3
  233.9 154.0 %reduce-scatter.2.cloned.1.call-start = ((), (), s32[]{:S(2)}) async-start(), calls=%async_computation.3 | async-start | bytes 78643200 | tf_op jit(solution)/shard_map/reduce_scatter | solution.py:78
  259.9 6.7 %copy-start.1 = (bf16[2,1280,256]{1,2,0:T(8,128)(2,1)S(1)}, bf16[2,1280,256]{1,2,0:T(8,128)(2,1)}, u32[]{:S(2)}) copy-start(bf16[2,1280,256]{1,2,0:T(8,128)(2,1)} %all-gather.2.cloned.1.call-done) | copy-start | bytes 3932164
Sparse Core Ops, SparseCore 0:
  35.5 191.6 all-reduce.1
  234.1 23.2 all-gather.1
  322.2 65.7 reduce-scatter.1
where the time goes:
time: 413 us; the launch traced here: 412 us
  waiting for transfers between devices  280 us (68%)
  other arithmetic  70.1 us (17%)
  matrix products  46.1 us (11%)
  between operations  13.2 us (3%)
    psum x1, waiting for transfers between devices, local(): spectra_all = lax.psum(partial_value, 'row')  191 us
    reduce_scatter x1, waiting for transfers between devices, local(): lax.psum_scatter(partial_products, 'sub', scatter_dimension=2, tiled=True)  65.9 us
    another operation x1, other arithmetic, pair_products(): return jnp.stack(results)  34.9 us
    dot_general x4, matrix products, pair_products(): jnp.einsum('wpk,wqk->pq', rotated, column_spectra, preferred_element_type...  26.7 us
    all_gather x1, waiting for transfers between devices, local(): row_spectra = lax.all_gather(white, 'col', axis=1, tiled=True)  22.9 us
    dot_general x1, matrix products, local(): jnp.einsum('wct,tk->wck', traces, table, preferred_element_type=jnp.float32)  19.4 us
    mul x1, other arithmetic, local(): return summed * scale  17.8 us
    another operation x3, other arithmetic  12.4 us
  transfers between devices with their start and end apart: 3, of which 3 were waited for; matrix products, arithmetic and copies ran while one was open for 0% of the time, Pallas kernels for 0%

commit v1 on v0

v1 whole, which is shorter than its diff:
```python
import functools
import math

import jax
import jax.numpy as jnp
from jax import lax
from jax.experimental import pallas as pl
from jax.experimental.pallas import tpu as pltpu
from jax.sharding import PartitionSpec as P

W = 16384
LAGS = 4
LAG_STEP = 50
TWO_PI = 2.0 * math.pi

F32 = jnp.float32
BF16 = jnp.bfloat16
VMEM_LIMIT = 56 * 1024 * 1024
FINE = 64


def band_table(sample_times, bin_ids, length):
    window_taper = 0.5 - 0.5 * jnp.cos(TWO_PI / length * sample_times.astype(F32))
    phase_index = sample_times[:, None] * bin_ids[None, :] % length
    angles = TWO_PI / length * phase_index.astype(F32)
    cosine = window_taper[:, None] * jnp.cos(angles)
    sine_part = -window_taper[:, None] * jnp.sin(angles)
    return jnp.concatenate([cosine, sine_part], axis=1).astype(BF16)


def whiten(spectra, quality):
    nbins = spectra.shape[-1] // 2
    real_part = spectra[..., :nbins]
    imag_part = spectra[..., nbins:]
    band_rms = jnp.sqrt(jnp.mean(spectra * spectra, axis=-1, keepdims=True) + 1e-05)
    magnitude = jnp.sqrt(real_part * real_part + imag_part * imag_part)
    divisor = jnp.maximum(magnitude, 0.25 * band_rms)
    scaled = jnp.concatenate([real_part / divisor, imag_part / divisor], axis=-1)
    return (quality.astype(F32)[:, None] * scaled).astype(BF16)


def rotate(white, bin_ids, lag_shift, length):
    nbins = white.shape[-1] // 2
    phase_index = bin_ids * lag_shift % length
    angles = TWO_PI / length * phase_index.astype(F32)
    cosine = jnp.cos(angles)
    sine_part = jnp.sin(angles)
    real_part = white[..., :nbins].astype(F32)
    imag_part = white[..., nbins:].astype(F32)
    turned = jnp.concatenate(
        [real_part * cosine + imag_part * sine_part, imag_part * cosine - real_part * sine_part],
        axis=-1,
    )
    return turned.astype(BF16)


def pair_products(row_spectra, column_spectra, bin_ids, length):
    results = []
    for lag_index in range(LAGS):
        lag_shift = (lag_index - LAGS // 2) * LAG_STEP
        rotated = rotate(row_spectra, bin_ids, lag_shift, length)
        results.append(
            jnp.einsum("wpk,wqk->pq", rotated, column_spectra, preferred_element_type=F32)
        )
    return jnp.stack(results)


def local_plain(traces, quality_mask, band_bins):
    nbins = band_bins.shape[0]
    windows_here = traces.shape[0]
    samples_here = traces.shape[2]
    sample_times = lax.axis_index("row") * samples_here + jnp.arange(samples_here, dtype=jnp.int32)
    table = band_table(sample_times, band_bins, W)
    partial_value = jnp.einsum("wct,tk->wck", traces, table, preferred_element_type=F32)
    spectra_all = lax.psum(partial_value, "row")
    column_spectra = whiten(spectra_all, quality_mask)
    local_channels = traces.shape[1] // lax.axis_size("row")
    white = lax.dynamic_slice_in_dim(
        column_spectra, lax.axis_index("row") * local_channels, local_channels, 1
    )
    row_spectra = lax.all_gather(white, "col", axis=1, tiled=True)
    scale = 1.0 / math.sqrt(lax.axis_size("sub") * windows_here * nbins)
    partial_products = pair_products(row_spectra, column_spectra, band_bins, W)
    summed = lax.psum_scatter(partial_products, "sub", scatter_dimension=2, tiled=True)
    return summed * scale


def fill_table(first_sample, bins_ref, table_ref, coarse_ref):
    nbins = bins_ref.shape[1]
    runs = table_ref.shape[0] // FINE
    bins = bins_ref[...]

    def turn(ids, times):
        angles = TWO_PI / W * ((ids * times) & (W - 1)).astype(F32)
        return jnp.cos(angles), jnp.sin(angles)

    fine_times = lax.broadcasted_iota(jnp.int32, (FINE, nbins), 0)
    coarse_times = first_sample + FINE * lax.broadcasted_iota(jnp.int32, (runs, nbins), 0)
    cos_f, sin_f = turn(bins, fine_times)
    cos_h, sin_h = turn(1, fine_times)
    for place, value in enumerate(turn(bins, coarse_times) + turn(1, coarse_times)):
        coarse_ref[place] = value

    @pl.loop(0, runs)
    def _(a):
        cos_c, sin_c, cos_g, sin_g = (coarse_ref[i, pl.ds(a, 1), :] for i in range(4))
        taper = 0.5 - 0.5 * (cos_g * cos_h - sin_g * sin_h)
        rows = pl.ds(pl.multiple_of(a * FINE, FINE), FINE)
        table_ref[rows, :nbins] = (taper * (cos_c * cos_f - sin_c * sin_f)).astype(BF16)
        table_ref[rows, nbins:] = (-taper * (sin_c * cos_f + cos_c * sin_f)).astype(BF16)


def spectra_kernel(with_table, split, block, where_ref, bins_or_table, traces_ref, *rest):
    if with_table:
        right_ref, left_ref, table_ref, right_buf, left_buf, sems, coarse_ref = rest
    else:
        right_ref, left_ref, right_buf, left_buf, sems = rest
        table_ref = bins_or_table
    windows = traces_ref.shape[0]
    right_start = pl.multiple_of(where_ref[1] * block, 128)
    left_start = pl.multiple_of(where_ref[2] * block + split, 128)
    copies = []
    for w in range(windows):
        copies.append(
            pltpu.make_async_copy(
                traces_ref.at[w, pl.ds(right_start, split), :], right_buf.at[w], sems.at[0, w]
            )
        )
        copies.append(
            pltpu.make_async_copy(
                traces_ref.at[w, pl.ds(left_start, block - split), :], left_buf.at[w], sems.at[1, w]
            )
        )
    for copy in copies:
        copy.start()
    if with_table:
        fill_table(where_ref[0], bins_or_table, table_ref, coarse_ref)
    width = table_ref.shape[1]
    for w in range(windows):
        for side, (buf, out) in enumerate(((right_buf, right_ref), (left_buf, left_ref))):
            copies[2 * w + side].wait()
            out[:, w * width : (w + 1) * width] = jnp.dot(
                buf[w], table_ref[...], preferred_element_type=F32
            ).astype(out.dtype)


def spectra_call(where, bins_or_table, traces, split, block, with_table, dtype):
    windows, _, samples = traces.shape
    nbins = bins_or_table.shape[1] if with_table else bins_or_table.shape[1] // 2
    lanes = windows * 2 * nbins
    vmem = pl.BlockSpec(memory_space=pltpu.VMEM)
    out_shape = [
        jax.ShapeDtypeStruct((split, lanes), dtype),
        jax.ShapeDtypeStruct((block - split, lanes), dtype),
    ]
    scratch = [
        pltpu.VMEM((windows, split, samples), BF16),
        pltpu.VMEM((windows, block - split, samples), BF16),
        pltpu.SemaphoreType.DMA((2, windows)),
    ]
    if with_table:
        out_shape.append(jax.ShapeDtypeStruct((samples, 2 * nbins), BF16))
        scratch.append(pltpu.VMEM((4, samples // FINE, nbins), F32))
    return pl.pallas_call(
        functools.partial(spectra_kernel, with_table, split, block),
        out_shape=out_shape,
        in_specs=[
            pl.BlockSpec(memory_space=pltpu.SMEM),
            vmem,
            pl.BlockSpec(memory_space=pl.ANY),
        ],
        out_specs=[vmem] * len(out_shape),
        scratch_shapes=scratch,
        compiler_params=pltpu.CompilerParams(vmem_limit_bytes=VMEM_LIMIT),
        cost_estimate=pl.CostEstimate(
            flops=2 * block * lanes * samples,
            bytes_accessed=2 * windows * block * samples + 4 * block * lanes,
            transcendentals=0,
        ),
        name="spectra",
    )(where, bins_or_table, traces)


def whiten_kernel(got_r, got_l, own_r, own_l, quality, white, white_r, white_l):
    split = got_r.shape[0]
    lanes = got_r.shape[1]
    nbins = lanes // 4
    for got, own, out, first in ((got_r, own_r, white_r, 0), (got_l, own_l, white_l, split)):
        rows = got.shape[0]
        mask = quality[first : first + rows, :]
        for w in range(2):
            low = w * 2 * nbins
            real = got[:, low : low + nbins].astype(F32) + own[:, low : low + nbins]
            high = low + nbins
            imag = got[:, high : high + nbins].astype(F32) + own[:, high : high + nbins]
            power = real * real + imag * imag
            mean = jnp.sum(power, axis=1, keepdims=True) * (0.5 / nbins)
            factor = mask * jnp.minimum(lax.rsqrt(power), 4.0 * lax.rsqrt(mean + 1e-05))
            real = (real * factor).astype(BF16)
            imag = (imag * factor).astype(BF16)
            out[:, low : low + nbins] = real
            out[:, high : high + nbins] = imag
            white[first : first + rows, low : low + nbins] = real
            white[first : first + rows, high : high + nbins] = imag


def whiten_call(got_r, got_l, own_r, own_l, quality):
    vmem = pl.BlockSpec(memory_space=pltpu.VMEM)
    split, lanes = got_r.shape
    rest = got_l.shape[0]
    return pl.pallas_call(
        whiten_kernel,
        out_shape=[
            jax.ShapeDtypeStruct((split + rest, lanes), BF16),
            jax.ShapeDtypeStruct((split, lanes), BF16),
            jax.ShapeDtypeStruct((rest, lanes), BF16),
        ],
        in_specs=[vmem] * 5,
        out_specs=[vmem] * 3,
        compiler_params=pltpu.CompilerParams(vmem_limit_bytes=VMEM_LIMIT),
        cost_estimate=pl.CostEstimate(
            flops=12 * (split + rest) * lanes,
            bytes_accessed=12 * (split + rest) * lanes,
            transcendentals=(split + rest) * lanes // 2,
        ),
        name="whiten",
    )(got_r, got_l, own_r, own_l, quality)


def rotate_kernel(cos_ref, sin_ref, near_o, near_t, far_o, far_t, out):
    nbins = cos_ref.shape[2]
    cosine = cos_ref[0]
    sine = sin_ref[0]
    half = near_o.shape[1]
    for side, (o_ref, t_ref) in enumerate(((near_o, near_t), (far_o, far_t))):

        @pl.when(pl.program_id(0) == side)
        def _():
            for ref, base in ((o_ref, 0), (t_ref, half)):
                for w in range(2):
                    low = w * 2 * nbins
                    high = low + nbins
                    real = ref[:, low : low + nbins].astype(F32)
                    imag = ref[:, high : high + nbins].astype(F32)
                    out[0, :, base + low : base + low + nbins] = (
                        real * cosine + imag * sine
                    ).astype(BF16)
                    out[0, :, base + high : base + high + nbins] = (
                        imag * cosine - real * sine
                    ).astype(BF16)


def rotate_call(cosine, sine, near_o, near_t, far_o, far_t):
    block, half = near_o.shape
    nbins = cosine.shape[2]
    whole = pl.BlockSpec((block, half), lambda x, l: (0, 0))
    lag = pl.BlockSpec((1, 1, nbins), lambda x, l: (l, 0, 0))
    return pl.pallas_call(
        rotate_kernel,
        grid=(2, LAGS),
        out_shape=jax.ShapeDtypeStruct((2 * LAGS, block, 2 * half), BF16),
        in_specs=[lag, lag] + [whole] * 4,
        out_specs=pl.BlockSpec((1, block, 2 * half), lambda x, l: (x * LAGS + l, 0, 0)),
        compiler_params=pltpu.CompilerParams(vmem_limit_bytes=VMEM_LIMIT),
        cost_estimate=pl.CostEstimate(
            flops=6 * 2 * LAGS * block * 2 * half,
            bytes_accessed=2 * 2 * LAGS * block * 2 * half,
            transcendentals=0,
        ),
        name="rotate",
    )(cosine, sine, near_o, near_t, far_o, far_t)


def product_kernel(gather, scale, has_base, *refs):
    info, rows = refs[:2]
    out = refs[-4]
    columns, tiles, sems = refs[-3:]
    parts = refs[2 : -5 if has_base else -4]
    step = pl.program_id(0)
    steps = pl.num_programs(0)
    block = rows.shape[1]
    width = columns.shape[0]
    start = pl.multiple_of(info[0], 128)

    def place(index):
        side = lax.div(index, LAGS)
        first = pl.multiple_of(info[1 + side] * block, 128)
        return pltpu.make_async_copy(
            tiles.at[lax.rem(index, 2)],
            out.at[lax.rem(index, LAGS), pl.ds(first, block), pl.ds(start, width)],
            sems.at[lax.rem(index, 2)],
        )

    @pl.when(step == 0)
    def _():
        gather(info, parts, columns)

    @pl.when(step >= 2)
    def _():
        place(step - 2).wait()

    tiles[lax.rem(step, 2)] = scale * lax.dot_general(
        rows[0], columns[...], (((1,), (1,)), ((), ())), preferred_element_type=F32
    )
    place(step).start()

    @pl.when(step == steps - 1)
    def _():
        place(step - 1).wait()
        place(step).wait()


def product_call(info, rows, parts, gather, width, scale, base, out_shape):
    steps, block, depth = rows.shape
    vmem = pl.BlockSpec(memory_space=pltpu.VMEM)
    anywhere = pl.BlockSpec(memory_space=pl.ANY)
    operands = [info, rows] + list(parts)
    in_specs = [
        pl.BlockSpec(memory_space=pltpu.SMEM),
        pl.BlockSpec((1, block, depth), lambda s: (s, 0, 0)),
    ] + [vmem] * len(parts)
    aliases = {}
    if base is not None:
        aliases = {len(operands): 0}
        operands.append(base)
        in_specs.append(anywhere)
    return pl.pallas_call(
        functools.partial(product_kernel, gather, scale, base is not None),
        grid=(steps,),
        out_shape=out_shape,
        in_specs=in_specs,
        out_specs=anywhere,
        scratch_shapes=[
            pltpu.VMEM((width, depth), BF16),
            pltpu.VMEM((2, block, width), F32),
            pltpu.SemaphoreType.DMA((2,)),
        ],
        input_output_aliases=aliases,
        compiler_params=pltpu.CompilerParams(vmem_limit_bytes=VMEM_LIMIT),
        cost_estimate=pl.CostEstimate(
            flops=2 * steps * block * depth * width,
            bytes_accessed=steps * block * (2 * depth + 4 * width),
            transcendentals=0,
        ),
        name="products",
    )(*operands)


def gather_full(split, info, parts, columns):
    own_o, own_t, right_o, right_t, left_o, left_t = parts
    half = own_o.shape[1]

    @pl.when(info[3] == 1)
    def _():
        columns[:, :half] = own_o[...]
        columns[:, half:] = own_t[...]

    @pl.when(info[3] == 0)
    def _():
        columns[:split, :half] = right_o[...]
        columns[:split, half:] = right_t[...]
        columns[split:, :half] = left_o[...]
        columns[split:, half:] = left_t[...]


def gather_first(info, parts, columns):
    right_o, right_t, left_o, left_t = parts
    half = right_o.shape[1]
    width = columns.shape[0]

    @pl.when(info[3] == 1)
    def _():
        columns[:, :half] = right_o[:width, :]
        columns[:, half:] = right_t[:width, :]

    @pl.when(info[3] == 0)
    def _():
        columns[:, :half] = left_o[...]
        columns[:, half:] = left_t[...]


def gather_last(overlap, info, parts, columns):
    early_o, early_t, right_o, right_t, left_o, left_t = parts
    half = right_o.shape[1]
    split = right_o.shape[0]

    @pl.when(info[3] == 1)
    def _():
        columns[:overlap, :half] = early_o[split - overlap :, :]
        columns[:overlap, half:] = early_t[split - overlap :, :]
        columns[overlap:, :half] = left_o[...]
        columns[overlap:, half:] = left_t[...]

    @pl.when(info[3] == 0)
    def _():
        columns[:, :half] = right_o[...]
        columns[:, half:] = right_t[...]


def local_rings(traces, quality_mask, band_bins):
    n = lax.axis_size("row")
    windows, channels, samples = traces.shape
    nbins = band_bins.shape[0]
    block = channels // n
    split = (block // 128 + 1) // 2 * 128
    rest = block - split
    z = lax.axis_index("row")
    x = lax.axis_index("col")
    c = lax.axis_index("sub")
    to_right = [(i, (i + 1) % n) for i in range(n)]
    to_left = [(i, (i - 1) % n) for i in range(n)]
    i32 = jnp.int32

    def where(k):
        return jnp.stack([z * samples, (z - 1 - k) % n, (z + 1 + k) % n]).astype(i32)

    own = []
    right, left, table = spectra_call(
        where(0), band_bins[None, :], traces, split, block, True, BF16
    )
    for k in range(1, n):
        own.append(spectra_call(where(k), table, traces, split, block, False, F32))
    for k in range(n - 1):
        right = lax.ppermute(right, "row", to_right)
        left = lax.ppermute(left, "row", to_left)
        if k < n - 2:
            right = (right.astype(F32) + own[k][0]).astype(BF16)
            left = (left.astype(F32) + own[k][1]).astype(BF16)
    quality = lax.dynamic_slice_in_dim(quality_mask, z * block, block).astype(F32)[:, None]
    white, white_r, white_l = whiten_call(right, left, *own[-1], quality)

    def core_of(b):
        return (b % n) * 2 // n

    def pairs(step, move, cross):
        found = []
        for i in range(n):
            core = core_of(i - step * move)
            source = 1 - core if cross else core
            found.append((i * 2 + source, (i + move) % n * 2 + core))
        return found

    axes = ("row", "sub")
    r0 = [lax.ppermute(white_r, axes, pairs(0, 1, cross)) for cross in (False, True)]
    l0 = [lax.ppermute(white_l, axes, pairs(0, -1, cross)) for cross in (False, True)]
    r1 = [lax.ppermute(part, axes, pairs(1, 1, False)) for part in r0]
    l1 = [lax.ppermute(part, axes, pairs(1, -1, False)) for part in l0]
    r2 = [lax.ppermute(part, axes, pairs(2, 1, False)) for part in r1]
    l2 = [lax.ppermute(part, axes, pairs(2, -1, False)) for part in l1]

    swap = [(0, 1), (1, 0)]
    white_t = lax.ppermute(white, "sub", swap)
    far = lax.ppermute(white, "col", swap)
    far_t = lax.ppermute(far, "sub", swap)
    shifts = jnp.array([(lag - LAGS // 2) * LAG_STEP for lag in range(LAGS)], i32)
    angles = TWO_PI / W * (band_bins[None, :] * shifts[:, None] % W).astype(F32)
    rows = rotate_call(
        jnp.cos(angles)[:, None, :], jnp.sin(angles)[:, None, :], white, white_t, far, far_t
    )

    per_core = n // 2
    owner = z // per_core == c
    from_right = (z - 1) % n // per_core == c
    full = jnp.where(owner, z, (z + 2) % n) - per_core * c
    other = 1 - full
    scale = 1.0 / math.sqrt(2 * windows * nbins)
    out_shape = jax.ShapeDtypeStruct((LAGS, 2 * block, per_core * block), F32)

    def info(start, flag):
        return jnp.stack([start, x, 1 - x, flag]).astype(i32)

    overlap = split - rest
    result = product_call(
        info(full * block, owner), rows, [white, white_t] + r1 + l1,
        functools.partial(gather_full, split), block, scale, None, out_shape,
    )
    result = product_call(
        info(other * block + jnp.where(from_right, 0, split), from_right), rows, r0 + l0,
        gather_first, rest, scale, result, out_shape,
    )
    return product_call(
        info(other * block + jnp.where(from_right, rest, 0), from_right), rows, r0 + r2 + l2,
        functools.partial(gather_last, overlap), split, scale, result, out_shape,
    )


def solution(mesh):
    in_specs = (P(("group", "sub"), "col", "row"), P("col"), P())
    out_specs = P("group", "row", ("col", "sub"))
    rings = (mesh.shape["row"], mesh.shape["col"], mesh.shape["sub"]) == (4, 2, 2)
    return jax.shard_map(
        local_rings if rings else local_plain,
        mesh=mesh, in_specs=in_specs, out_specs=out_specs, check_vma=False,
    )
```

time: 413 us -> 173 us (0.42)
  the two profiles are of different devices: /device:TPU:0 before, /device:TPU:1 now
where the time goes in v1:
time: 173 us; the launch traced here: 172 us
  Pallas kernels  91.7 us (53%)
  starting transfers between devices  55.6 us (32%)
  waiting for transfers between devices  12.4 us (7%)
  other arithmetic  7.65 us (4%)
  local copies, waits for them, and re-layouts  3.62 us (2%)
    pallas_call x4, Pallas kernels, spectra_call(): pl.pallas_call(functools.partial(spectra_kernel, with_table, split, block...  41.1 us
    pallas_call x3, Pallas kernels, product_call(): pl.pallas_call(functools.partial(product_kernel, gather, scale, base is n...  38.8 us
    ppermute x2, starting transfers between devices, local_rings(): lax.ppermute(white_l, axes, pairs(0, -1, cross))  13.7 us
    ppermute x2, waiting for transfers between devices, local_rings(): l1 = [lax.ppermute(part, axes, pairs(1, -1, False)) for part in l0]  10.3 us
    ppermute x1, starting transfers between devices, local_rings(): far_t = lax.ppermute(far, 'sub', swap)  9.77 us
    ppermute x3, starting transfers between devices, local_rings(): left = lax.ppermute(left, 'row', to_left)  9.44 us
    pallas_call x1, Pallas kernels, rotate_call(): pl.pallas_call(rotate_kernel, grid=(2, LAGS), out_shape=jax.ShapeDtypeStr...  8.79 us
    ppermute x2, starting transfers between devices, local_rings(): r2 = [lax.ppermute(part, axes, pairs(2, 1, False)) for part in r1]  5.31 us
  transfers between devices with their start and end apart: 21, of which 2 were waited for; matrix products, arithmetic and copies ran while one was open for 5% of the time, Pallas kernels for 38%

profile of v1, /device:TPU:1, one launch (start us, length us, event | category | flops | bytes accessed | tf_op | source)
XLA Modules:
  0.0 171.8 jit_solution(5222220839467827789)
XLA Ops:
  0.6 10.2 %spectra.4 = (bf16[384,512]{1,0:T(8,128)(2,1)}, bf16[256,512]{1,0:T(8,128)(2,1)}, bf16[4096,256]{1,0:T(8,128)(2,1)}) custom-call(s32[3]{0:T(128)} %get-tuple-element.31.where_ref, s32[1,128]{1,0:T(1,128)} %bitcast.19, bf16[2,2560,4096]{2,1,0:T(8,128)(2,1)} %traces_ref.7), custom_call_target="tpu_custom_call" | custom-call | flops 2684354560 | bytes 11796480 | tf_op jit(solution)/shard_map/spectra/pallas_call | solution.py:164
  10.8 2.2 %collective-permute-start = (bf16[384,512]{1,0:T(8,128)(2,1)}, bf16[384,512]{1,0:T(8,128)(2,1)S(1)}, u32[]{:S(2)}, u32[]{:S(2)}) collective-permute-start(bf16[384,512]{1,0:T(8,128)(2,1)} %get-tuple-element.17), channel_id=1, source_target_pairs={{0,4},{4,8},{8,12},{12,0},{1,5},{5,9},{9,13},{13,1},{2,6},{6,10},{... | collective-permute-start | bytes 1179656 | tf_op jit(solution)/shard_map/ppermute | solution.py:424
  13.0 2.1 %collective-permute-start.3 = (bf16[256,512]{1,0:T(8,128)(2,1)}, bf16[256,512]{1,0:T(8,128)(2,1)S(1)}, u32[]{:S(2)}, u32[]{:S(2)}) collective-permute-start(bf16[256,512]{1,0:T(8,128)(2,1)} %get-tuple-element.21), channel_id=1, source_target_pairs={{0,12},{4,0},{8,4},{12,8},{1,13},{5,1},{9,5},{13,9},{2,14},{6,2},{... | collective-permute-start | bytes 786440 | tf_op jit(solution)/shard_map/ppermute | solution.py:425
  15.7 10.3 %spectra.5 = (f32[384,512]{1,0:T(8,128)}, f32[256,512]{1,0:T(8,128)}) custom-call(s32[3]{0:T(128)} %get-tuple-element.32.where_ref, bf16[4096,256]{1,0:T(8,128)(2,1)} %get-tuple-element.18.bins_or_table, bf16[2,2560,4096]{2,1,0:T(8,128)(2,1)} %traces_ref.7), custom_call_target="tpu_custom_call" | custom-call | flops 2684354560 | bytes 11796480 | tf_op jit(solution)/shard_map/spectra/pallas_call | solution.py:164
  26.0 1.3 add_convert_fusion.1
  27.4 10.3 %spectra.6 = (f32[384,512]{1,0:T(8,128)}, f32[256,512]{1,0:T(8,128)}) custom-call(s32[3]{0:T(128)} %get-tuple-element.33.where_ref, bf16[4096,256]{1,0:T(8,128)(2,1)} %get-tuple-element.18.bins_or_table, bf16[2,2560,4096]{2,1,0:T(8,128)(2,1)} %traces_ref.7), custom_call_target="tpu_custom_call" | custom-call | flops 2684354560 | bytes 11796480 | tf_op jit(solution)/shard_map/spectra/pallas_call | solution.py:164
  37.8 3.3 %collective-permute-start.4 = (bf16[256,512]{1,0:T(8,128)(2,1)S(1)}, bf16[256,512]{1,0:T(8,128)(2,1)S(1)}, u32[]{:S(2)}, u32[]{:S(2)}) collective-permute-start(bf16[256,512]{1,0:T(8,128)(2,1)S(1)} %add_convert_fusion.3), channel_id=1, source_target_pairs={{0,12},{4,0},{8,4},{12,8},{1,13},{5,1},{9,5},{13,9},{2,14},{6,2},{... | collective-permute-start | bytes 786440 | tf_op jit(solution)/shard_map/ppermute | solution.py:425
  41.1 1.3 add_convert_fusion
  42.5 2.0 %collective-permute-done.4 = bf16[256,512]{1,0:T(8,128)(2,1)S(1)} collective-permute-done((bf16[256,512]{1,0:T(8,128)(2,1)S(1)}, bf16[256,512]{1,0:T(8,128)(2,1)S(1)}, u32[]{:S(2)}, u32[]{:S(2)}) %collective-permute-start.4) | collective-permute-done | bytes 262176 | tf_op jit(solution)/shard_map/ppermute | solution.py:425
  44.5 1.1 add_convert_fusion.2
  45.6 4.1 %collective-permute-start.5 = (bf16[256,512]{1,0:T(8,128)(2,1)S(1)}, bf16[256,512]{1,0:T(8,128)(2,1)S(1)}, u32[]{:S(2)}, u32[]{:S(2)}) collective-permute-start(bf16[256,512]{1,0:T(8,128)(2,1)S(1)} %add_convert_fusion.2), channel_id=1, source_target_pairs={{0,12},{4,0},{8,4},{12,8},{1,13},{5,1},{9,5},{13,9},{2,14},{6,2},{... | collective-permute-start | bytes 786440 | tf_op jit(solution)/shard_map/ppermute | solution.py:425
  50.4 0.9 broadcast_in_dim.12.quality
  51.3 10.3 %spectra.7 = (f32[384,512]{1,0:T(8,128)}, f32[256,512]{1,0:T(8,128)}) custom-call(s32[3]{0:T(128)} %get-tuple-element.34.where_ref, bf16[4096,256]{1,0:T(8,128)(2,1)} %get-tuple-element.18.bins_or_table, bf16[2,2560,4096]{2,1,0:T(8,128)(2,1)} %traces_ref.7), custom_call_target="tpu_custom_call" | custom-call | flops 2684354560 | bytes 11796480 | tf_op jit(solution)/shard_map/spectra/pallas_call | solution.py:164
  62.5 3.1 %whiten.1 = (bf16[640,512]{1,0:T(8,128)(2,1)}, bf16[384,512]{1,0:T(8,128)(2,1)}, bf16[256,512]{1,0:T(8,128)(2,1)}) custom-call(bf16[384,512]{1,0:T(8,128)(2,1)} %copy-done.8, bf16[256,512]{1,0:T(8,128)(2,1)} %copy-done.17, f32[384,512]{1,0:T(8,128)} %get-tuple-element.24.own_r, f32[256,512]{1,0:T(8,128)} %get-tuple-element.25.own_l, ...), custom_call_target="tpu_custom_call" | custom-call | flops 3932160 | bytes 3932160 | tf_op jit(solution)/shard_map/whiten/pallas_call | solution.py:211
  65.6 1.2 collective-permute-start.7
  66.8 13.0 %collective-permute-start.18 = (bf16[256,512]{1,0:T(8,128)(2,1)}, bf16[256,512]{1,0:T(8,128)(2,1)S(1)}, u32[]{:S(2)}, u32[]{:S(2)}) collective-permute-start(bf16[256,512]{1,0:T(8,128)(2,1)} %get-tuple-element.28), channel_id=1, source_target_pairs={{1,12},{5,0},{8,5},{12,9},{3,14},{7,2},{10,7},{14,11},{17,28},{21,... | collective-permute-start | bytes 786440 | tf_op jit(solution)/shard_map/ppermute | solution.py:445
  80.5 1.9 %collective-permute-start.10 = (bf16[384,512]{1,0:T(8,128)(2,1)}, bf16[384,512]{1,0:T(8,128)(2,1)S(1)}, u32[]{:S(2)}, u32[]{:S(2)}) collective-permute-start(bf16[384,512]{1,0:T(8,128)(2,1)} %get-tuple-element.27), channel_id=1, source_target_pairs={{1,4},{5,8},{8,13},{12,1},{3,6},{7,10},{10,15},{14,3},{17,20},{21,... | collective-permute-start | bytes 1179656 | tf_op jit(solution)/shard_map/ppermute | solution.py:444
  82.4 1.3 collective-permute-start.9
  84.3 1.3 collective-permute-start.19
  85.6 9.8 %collective-permute-start.8 = (bf16[640,512]{1,0:T(8,128)(2,1)S(1)}, bf16[640,512]{1,0:T(8,128)(2,1)S(1)}, u32[]{:S(2)}, u32[]{:S(2)}) collective-permute-start(bf16[640,512]{1,0:T(8,128)(2,1)S(1)} %collective-permute-done.7.far_o), channel_id=1, source_target_pairs={{0,1},{1,0},{2,3},{3,2},{4,5},{5,4},{6,7},{7,6},{8,9},{9,8},{10,11... | collective-permute-start | bytes 1966088 | tf_op jit(solution)/shard_map/ppermute | solution.py:454
  95.4 1.9 %collective-permute-start.13 = (bf16[384,512]{1,0:T(8,128)(2,1)S(1)}, bf16[384,512]{1,0:T(8,128)(2,1)S(1)}, u32[]{:S(2)}, u32[]{:S(2)}) collective-permute-start(bf16[384,512]{1,0:T(8,128)(2,1)S(1)} %collective-permute-done.10.refs_3_), channel_id=1, source_target_pairs={{1,5},{4,8},{8,12},{13,1},{3,7},{6,10},{10,14},{15,3},{17,21},{20,... | collective-permute-start | bytes 1179656 | tf_op jit(solution)/shard_map/ppermute | solution.py:446
  97.4 1.9 %collective-permute-start.11 = (bf16[384,512]{1,0:T(8,128)(2,1)S(1)}, bf16[384,512]{1,0:T(8,128)(2,1)S(1)}, u32[]{:S(2)}, u32[]{:S(2)}) collective-permute-start(bf16[384,512]{1,0:T(8,128)(2,1)S(1)} %collective-permute-done.9.refs_2_), channel_id=1, source_target_pairs={{1,5},{4,8},{8,12},{13,1},{3,7},{6,10},{10,14},{15,3},{17,21},{20,... | collective-permute-start | bytes 1179656 | tf_op jit(solution)/shard_map/ppermute | solution.py:446
  99.9 1.3 collective-permute-start.16
  102.5 10.3 %collective-permute-done.16.refs_6_ = bf16[256,512]{1,0:T(8,128)(2,1)S(1)} collective-permute-done((bf16[256,512]{1,0:T(8,128)(2,1)S(1)}, bf16[256,512]{1,0:T(8,128)(2,1)S(1)}, u32[]{:S(2)}, u32[]{:S(2)}) %collective-permute-start.16) | collective-permute-done | bytes 262176 | tf_op jit(solution)/shard_map/ppermute | solution.py:447
  112.8 1.9 %collective-permute-start.20 = (bf16[256,512]{1,0:T(8,128)(2,1)S(1)}, bf16[256,512]{1,0:T(8,128)(2,1)S(1)}, u32[]{:S(2)}, u32[]{:S(2)}) collective-permute-start(bf16[256,512]{1,0:T(8,128)(2,1)S(1)} %collective-permute-done.19.refs_7_), channel_id=1, source_target_pairs={{1,13},{5,1},{8,4},{12,8},{3,15},{7,3},{10,6},{14,10},{17,29},{21,... | collective-permute-start | bytes 786440 | tf_op jit(solution)/shard_map/ppermute | solution.py:449
  114.7 1.9 %collective-permute-start.17 = (bf16[256,512]{1,0:T(8,128)(2,1)S(1)}, bf16[256,512]{1,0:T(8,128)(2,1)S(1)}, u32[]{:S(2)}, u32[]{:S(2)}) collective-permute-start(bf16[256,512]{1,0:T(8,128)(2,1)S(1)} %collective-permute-done.16.refs_6_), channel_id=1, source_target_pairs={{1,13},{5,1},{8,4},{12,8},{3,15},{7,3},{10,6},{14,10},{17,29},{21,... | collective-permute-start | bytes 786440 | tf_op jit(solution)/shard_map/ppermute | solution.py:449
  116.6 3.4 %collective-permute-start.14 = (bf16[384,512]{1,0:T(8,128)(2,1)S(1)}, bf16[384,512]{1,0:T(8,128)(2,1)S(1)}, u32[]{:S(2)}, u32[]{:S(2)}) collective-permute-start(bf16[384,512]{1,0:T(8,128)(2,1)S(1)} %collective-permute-done.13.refs_5_), channel_id=1, source_target_pairs={{1,5},{5,9},{8,12},{12,0},{3,7},{7,11},{10,14},{14,2},{17,21},{21,... | collective-permute-start | bytes 1179656 | tf_op jit(solution)/shard_map/ppermute | solution.py:448
  120.1 1.9 %collective-permute-start.12 = (bf16[384,512]{1,0:T(8,128)(2,1)S(1)}, bf16[384,512]{1,0:T(8,128)(2,1)S(1)}, u32[]{:S(2)}, u32[]{:S(2)}) collective-permute-start(bf16[384,512]{1,0:T(8,128)(2,1)S(1)} %collective-permute-done.11.refs_4_), channel_id=1, source_target_pairs={{1,5},{5,9},{8,12},{12,0},{3,7},{7,11},{10,14},{14,2},{17,21},{21,... | collective-permute-start | bytes 1179656 | tf_op jit(solution)/shard_map/ppermute | solution.py:448
  122.9 8.8 %rotate.1.refs_1_ = bf16[8,640,1024]{2,1,0:T(8,128)(2,1)} custom-call(f32[4,1,128]{2,1,0:T(1,128)} %get-tuple-element.30.cos_ref, f32[4,1,128]{2,1,0:T(1,128)} %get-tuple-element.29.sin_ref, bf16[640,512]{1,0:T(8,128)(2,1)} %get-tuple-element.26.near_o.refs_2_, bf16[640,512]{1,0:T(8,128)(2,1)} %copy-done, bf16[640,512]{1,0:T(8,128)(2,1)} %copy-done.3, ...), custom_call_target="tpu_custom_call" | custom-call | flops 31457280 | bytes 10485760 | tf_op jit(solution)/shard_map/rotate/pallas_call | solution.py:258
  131.7 15.6 %products.3.refs_6_ = f32[4,1280,1280]{2,1,0:T(8,128)} custom-call(s32[4]{0:T(128)} %pad_add_fusion.4.refs_0_, bf16[8,640,1024]{2,1,0:T(8,128)(2,1)} %rotate.1.refs_1_, bf16[640,512]{1,0:T(8,128)(2,1)} %get-tuple-element.26.near_o.refs_2_, bf16[640,512]{1,0:T(8,128)(2,1)} %copy-done, bf16[384,512]{1,0:T(8,128)(2,1)} %copy-done.10, ...), custom_call_target="tpu_custom_call" | custom-call | flops 6710886400 | bytes 23592960 | tf_op jit(solution)/shard_map/products/pallas_call | solution.py:327
  147.4 10.4 %products.4.refs_8_ = f32[4,1280,1280]{2,1,0:T(8,128)} custom-call(s32[4]{0:T(128)} %get-tuple-element.36.refs_0_, bf16[8,640,1024]{2,1,0:T(8,128)(2,1)} %rotate.1.refs_1_, bf16[384,512]{1,0:T(8,128)(2,1)} %copy-done.2, bf16[384,512]{1,0:T(8,128)(2,1)} %copy-done.1, bf16[256,512]{1,0:T(8,128)(2,1)} %copy-done.12, ...), custom_call_target="tpu_custom_call", output_to_operand_aliasing={{}: (6, {})} | custom-call | flops 2684354560 | bytes 15728640 | tf_op jit(solution)/shard_map/products/pallas_call | solution.py:327
  158.9 12.7 %products.5 = f32[4,1280,1280]{2,1,0:T(8,128)} custom-call(s32[4]{0:T(128)} %get-tuple-element.35.refs_0_, bf16[8,640,1024]{2,1,0:T(8,128)(2,1)} %rotate.1.refs_1_, bf16[384,512]{1,0:T(8,128)(2,1)} %copy-done.2, bf16[384,512]{1,0:T(8,128)(2,1)} %copy-done.1, bf16[384,512]{1,0:T(8,128)(2,1)} %copy-done.7, ...), custom_call_target="tpu_custom_call", output_to_operand_aliasing={{}: (8, {})} | custom-call | flops 4026531840 | bytes 18350080 | tf_op jit(solution)/shard_map/products/pallas_call | solution.py:327
  (71 shorter events, 8.0 us)
Async XLA Ops:
  10.8 15.2 %collective-permute-start = (bf16[384,512]{1,0:T(8,128)(2,1)}, bf16[384,512]{1,0:T(8,128)(2,1)S(1)}, u32[]{:S(2)}, u32[]{:S(2)}) collective-permute-start(bf16[384,512]{1,0:T(8,128)(2,1)} %get-tuple-element.17), channel_id=1, source_target_pairs={{0,4},{4,8},{8,12},{12,0},{1,5},{5,9},{9,13},{13,1},{2,6},{6,10},{... | collective-permute-start | bytes 1179656 | tf_op jit(solution)/shard_map/ppermute | solution.py:424
  13.0 24.8 %collective-permute-start.3 = (bf16[256,512]{1,0:T(8,128)(2,1)}, bf16[256,512]{1,0:T(8,128)(2,1)S(1)}, u32[]{:S(2)}, u32[]{:S(2)}) collective-permute-start(bf16[256,512]{1,0:T(8,128)(2,1)} %get-tuple-element.21), channel_id=1, source_target_pairs={{0,12},{4,0},{8,4},{12,8},{1,13},{5,1},{9,5},{13,9},{2,14},{6,2},{... | collective-permute-start | bytes 786440 | tf_op jit(solution)/shard_map/ppermute | solution.py:425
  26.0 11.8 %copy-start.5 = (f32[256,512]{1,0:T(8,128)S(1)}, f32[256,512]{1,0:T(8,128)}, u32[]{:S(2)}) copy-start(f32[256,512]{1,0:T(8,128)} %get-tuple-element.22) | copy-start | bytes 1572868
  27.3 13.8 %collective-permute-start.1 = (bf16[384,512]{1,0:T(8,128)(2,1)S(1)}, bf16[384,512]{1,0:T(8,128)(2,1)S(1)}, u32[]{:S(2)}, u32[]{:S(2)}) collective-permute-start(bf16[384,512]{1,0:T(8,128)(2,1)S(1)} %add_convert_fusion.1), channel_id=1, source_target_pairs={{0,4},{4,8},{8,12},{12,0},{1,5},{5,9},{9,13},{13,1},{2,6},{6,10},{... | collective-permute-start | bytes 1179656 | tf_op jit(solution)/shard_map/ppermute | solution.py:424
  37.7 57.7 %copy-start.18 = (s32[128]{0:T(128)S(1)}, s32[128]{0:T(128)}, u32[]{:S(2)}) copy-start(s32[128]{0:T(128)} %param.6) | copy-start | bytes 1540
  37.7 57.6 %copy-start.19 = (s32[4]{0:T(128)S(1)}, s32[4]{0:T(128)}, u32[]{:S(2)}) copy-start(s32[4]{0:T(128)} %constant.121.clone) | copy-start | bytes 52
  37.8 6.7 %collective-permute-start.4 = (bf16[256,512]{1,0:T(8,128)(2,1)S(1)}, bf16[256,512]{1,0:T(8,128)(2,1)S(1)}, u32[]{:S(2)}, u32[]{:S(2)}) collective-permute-start(bf16[256,512]{1,0:T(8,128)(2,1)S(1)} %add_convert_fusion.3), channel_id=1, source_target_pairs={{0,12},{4,0},{8,4},{12,8},{1,13},{5,1},{9,5},{13,9},{2,14},{6,2},{... | collective-permute-start | bytes 786440 | tf_op jit(solution)/shard_map/ppermute | solution.py:425
  42.4 19.3 %collective-permute-start.2 = (bf16[384,512]{1,0:T(8,128)(2,1)S(1)}, bf16[384,512]{1,0:T(8,128)(2,1)S(1)}, u32[]{:S(2)}, u32[]{:S(2)}) collective-permute-start(bf16[384,512]{1,0:T(8,128)(2,1)S(1)} %add_convert_fusion), channel_id=1, source_target_pairs={{0,4},{4,8},{8,12},{12,0},{1,5},{5,9},{9,13},{13,1},{2,6},{6,10},{... | collective-permute-start | bytes 1179656 | tf_op jit(solution)/shard_map/ppermute | solution.py:424
  45.6 16.1 %collective-permute-start.5 = (bf16[256,512]{1,0:T(8,128)(2,1)S(1)}, bf16[256,512]{1,0:T(8,128)(2,1)S(1)}, u32[]{:S(2)}, u32[]{:S(2)}) collective-permute-start(bf16[256,512]{1,0:T(8,128)(2,1)S(1)} %add_convert_fusion.2), channel_id=1, source_target_pairs={{0,12},{4,0},{8,4},{12,8},{1,13},{5,1},{9,5},{13,9},{2,14},{6,2},{... | collective-permute-start | bytes 786440 | tf_op jit(solution)/shard_map/ppermute | solution.py:425
  65.6 20.0 %collective-permute-start.7 = (bf16[640,512]{1,0:T(8,128)(2,1)}, bf16[640,512]{1,0:T(8,128)(2,1)S(1)}, u32[]{:S(2)}, u32[]{:S(2)}) collective-permute-start(bf16[640,512]{1,0:T(8,128)(2,1)} %get-tuple-element.26.near_o.refs_2_), channel_id=1, source_target_pairs={{0,2},{2,0},{1,3},{3,1},{4,6},{6,4},{5,7},{7,5},{8,10},{10,8},{9,1... | collective-permute-start | bytes 1966088 | tf_op jit(solution)/shard_map/ppermute | solution.py:453
  66.8 17.0 %collective-permute-start.18 = (bf16[256,512]{1,0:T(8,128)(2,1)}, bf16[256,512]{1,0:T(8,128)(2,1)S(1)}, u32[]{:S(2)}, u32[]{:S(2)}) collective-permute-start(bf16[256,512]{1,0:T(8,128)(2,1)} %get-tuple-element.28), channel_id=1, source_target_pairs={{1,12},{5,0},{8,5},{12,9},{3,14},{7,2},{10,7},{14,11},{17,28},{21,... | collective-permute-start | bytes 786440 | tf_op jit(solution)/shard_map/ppermute | solution.py:445
  79.8 4.5 %collective-permute-start.15 = (bf16[256,512]{1,0:T(8,128)(2,1)}, bf16[256,512]{1,0:T(8,128)(2,1)S(1)}, u32[]{:S(2)}, u32[]{:S(2)}) collective-permute-start(bf16[256,512]{1,0:T(8,128)(2,1)} %get-tuple-element.28), channel_id=1, source_target_pairs={{0,12},{4,0},{9,5},{13,9},{2,14},{6,2},{11,7},{15,11},{16,28},{20,... | collective-permute-start | bytes 786440 | tf_op jit(solution)/shard_map/ppermute | solution.py:445
  80.5 15.0 %collective-permute-start.10 = (bf16[384,512]{1,0:T(8,128)(2,1)}, bf16[384,512]{1,0:T(8,128)(2,1)S(1)}, u32[]{:S(2)}, u32[]{:S(2)}) collective-permute-start(bf16[384,512]{1,0:T(8,128)(2,1)} %get-tuple-element.27), channel_id=1, source_target_pairs={{1,4},{5,8},{8,13},{12,1},{3,6},{7,10},{10,15},{14,3},{17,20},{21,... | collective-permute-start | bytes 1179656 | tf_op jit(solution)/shard_map/ppermute | solution.py:444
  82.4 15.0 %collective-permute-start.9 = (bf16[384,512]{1,0:T(8,128)(2,1)}, bf16[384,512]{1,0:T(8,128)(2,1)S(1)}, u32[]{:S(2)}, u32[]{:S(2)}) collective-permute-start(bf16[384,512]{1,0:T(8,128)(2,1)} %get-tuple-element.27), channel_id=1, source_target_pairs={{0,4},{4,8},{9,13},{13,1},{2,6},{6,10},{11,15},{15,3},{16,20},{20,... | collective-permute-start | bytes 1179656 | tf_op jit(solution)/shard_map/ppermute | solution.py:444
  83.8 63.6 %copy-start.11 = (bf16[256,512]{1,0:T(8,128)(2,1)}, bf16[256,512]{1,0:T(8,128)(2,1)S(1)}, u32[]{:S(2)}) copy-start(bf16[256,512]{1,0:T(8,128)(2,1)S(1)} %collective-permute-done.18.refs_5_) | copy-start | bytes 786436
  83.8 30.9 %collective-permute-start.6 = (bf16[640,512]{1,0:T(8,128)(2,1)}, bf16[640,512]{1,0:T(8,128)(2,1)S(1)}, u32[]{:S(2)}, u32[]{:S(2)}) collective-permute-start(bf16[640,512]{1,0:T(8,128)(2,1)} %get-tuple-element.26.near_o.refs_2_), channel_id=1, source_target_pairs={{0,1},{1,0},{2,3},{3,2},{4,5},{5,4},{6,7},{7,6},{8,9},{9,8},{10,11... | collective-permute-start | bytes 1966088 | tf_op jit(solution)/shard_map/ppermute | solution.py:452
  84.3 63.1 %copy-start.12 = (bf16[256,512]{1,0:T(8,128)(2,1)}, bf16[256,512]{1,0:T(8,128)(2,1)S(1)}, u32[]{:S(2)}) copy-start(bf16[256,512]{1,0:T(8,128)(2,1)S(1)} %collective-permute-done.15.refs_4_) | copy-start | bytes 786436
  84.3 15.7 %collective-permute-start.19 = (bf16[256,512]{1,0:T(8,128)(2,1)S(1)}, bf16[256,512]{1,0:T(8,128)(2,1)S(1)}, u32[]{:S(2)}, u32[]{:S(2)}) collective-permute-start(bf16[256,512]{1,0:T(8,128)(2,1)S(1)} %collective-permute-done.18.refs_5_), channel_id=1, source_target_pairs={{0,12},{5,1},{9,5},{12,8},{2,14},{7,3},{11,7},{14,10},{16,28},{21,... | collective-permute-start | bytes 786440 | tf_op jit(solution)/shard_map/ppermute | solution.py:447
  85.6 36.4 %copy-start.3 = (bf16[640,512]{1,0:T(8,128)(2,1)}, bf16[640,512]{1,0:T(8,128)(2,1)S(1)}, u32[]{:S(2)}) copy-start(bf16[640,512]{1,0:T(8,128)(2,1)S(1)} %collective-permute-done.7.far_o) | copy-start | bytes 1966084
  85.6 36.4 %collective-permute-start.8 = (bf16[640,512]{1,0:T(8,128)(2,1)S(1)}, bf16[640,512]{1,0:T(8,128)(2,1)S(1)}, u32[]{:S(2)}, u32[]{:S(2)}) collective-permute-start(bf16[640,512]{1,0:T(8,128)(2,1)S(1)} %collective-permute-done.7.far_o), channel_id=1, source_target_pairs={{0,1},{1,0},{2,3},{3,2},{4,5},{5,4},{6,7},{7,6},{8,9},{9,8},{10,11... | collective-permute-start | bytes 1966088 | tf_op jit(solution)/shard_map/ppermute | solution.py:454
  95.4 51.9 %copy-start.1 = (bf16[384,512]{1,0:T(8,128)(2,1)}, bf16[384,512]{1,0:T(8,128)(2,1)S(1)}, u32[]{:S(2)}) copy-start(bf16[384,512]{1,0:T(8,128)(2,1)S(1)} %collective-permute-done.10.refs_3_) | copy-start | bytes 1179652
  95.4 21.2 %collective-permute-start.13 = (bf16[384,512]{1,0:T(8,128)(2,1)S(1)}, bf16[384,512]{1,0:T(8,128)(2,1)S(1)}, u32[]{:S(2)}, u32[]{:S(2)}) collective-permute-start(bf16[384,512]{1,0:T(8,128)(2,1)S(1)} %collective-permute-done.10.refs_3_), channel_id=1, source_target_pairs={{1,5},{4,8},{8,12},{13,1},{3,7},{6,10},{10,14},{15,3},{17,21},{20,... | collective-permute-start | bytes 1179656 | tf_op jit(solution)/shard_map/ppermute | solution.py:446
  97.4 50.0 %copy-start.2 = (bf16[384,512]{1,0:T(8,128)(2,1)}, bf16[384,512]{1,0:T(8,128)(2,1)S(1)}, u32[]{:S(2)}) copy-start(bf16[384,512]{1,0:T(8,128)(2,1)S(1)} %collective-permute-done.9.refs_2_) | copy-start | bytes 1179652
  97.4 22.7 %collective-permute-start.11 = (bf16[384,512]{1,0:T(8,128)(2,1)S(1)}, bf16[384,512]{1,0:T(8,128)(2,1)S(1)}, u32[]{:S(2)}, u32[]{:S(2)}) collective-permute-start(bf16[384,512]{1,0:T(8,128)(2,1)S(1)} %collective-permute-done.9.refs_2_), channel_id=1, source_target_pairs={{1,5},{4,8},{8,12},{13,1},{3,7},{6,10},{10,14},{15,3},{17,21},{20,... | collective-permute-start | bytes 1179656 | tf_op jit(solution)/shard_map/ppermute | solution.py:446
  99.9 31.7 %copy-start.13 = (bf16[256,512]{1,0:T(8,128)(2,1)}, bf16[256,512]{1,0:T(8,128)(2,1)S(1)}, u32[]{:S(2)}) copy-start(bf16[256,512]{1,0:T(8,128)(2,1)S(1)} %collective-permute-done.19.refs_7_) | copy-start | bytes 786436
  99.9 12.8 %collective-permute-start.16 = (bf16[256,512]{1,0:T(8,128)(2,1)S(1)}, bf16[256,512]{1,0:T(8,128)(2,1)S(1)}, u32[]{:S(2)}, u32[]{:S(2)}) collective-permute-start(bf16[256,512]{1,0:T(8,128)(2,1)S(1)} %collective-permute-done.15.refs_4_), channel_id=1, source_target_pairs={{0,12},{5,1},{9,5},{12,8},{2,14},{7,3},{11,7},{14,10},{16,28},{21,... | collective-permute-start | bytes 786440 | tf_op jit(solution)/shard_map/ppermute | solution.py:447
  112.8 18.9 %copy-start.15 = (bf16[256,512]{1,0:T(8,128)(2,1)}, bf16[256,512]{1,0:T(8,128)(2,1)S(1)}, u32[]{:S(2)}) copy-start(bf16[256,512]{1,0:T(8,128)(2,1)S(1)} %collective-permute-done.16.refs_6_) | copy-start | bytes 786436
  112.8 45.0 %collective-permute-start.20 = (bf16[256,512]{1,0:T(8,128)(2,1)S(1)}, bf16[256,512]{1,0:T(8,128)(2,1)S(1)}, u32[]{:S(2)}, u32[]{:S(2)}) collective-permute-start(bf16[256,512]{1,0:T(8,128)(2,1)S(1)} %collective-permute-done.19.refs_7_), channel_id=1, source_target_pairs={{1,13},{5,1},{8,4},{12,8},{3,15},{7,3},{10,6},{14,10},{17,29},{21,... | collective-permute-start | bytes 786440 | tf_op jit(solution)/shard_map/ppermute | solution.py:449
  114.7 43.1 %collective-permute-start.17 = (bf16[256,512]{1,0:T(8,128)(2,1)S(1)}, bf16[256,512]{1,0:T(8,128)(2,1)S(1)}, u32[]{:S(2)}, u32[]{:S(2)}) collective-permute-start(bf16[256,512]{1,0:T(8,128)(2,1)S(1)} %collective-permute-done.16.refs_6_), channel_id=1, source_target_pairs={{1,13},{5,1},{8,4},{12,8},{3,15},{7,3},{10,6},{14,10},{17,29},{21,... | collective-permute-start | bytes 786440 | tf_op jit(solution)/shard_map/ppermute | solution.py:449
  116.6 15.0 %copy-start.9 = (bf16[384,512]{1,0:T(8,128)(2,1)}, bf16[384,512]{1,0:T(8,128)(2,1)S(1)}, u32[]{:S(2)}) copy-start(bf16[384,512]{1,0:T(8,128)(2,1)S(1)} %collective-permute-done.13.refs_5_) | copy-start | bytes 1179652
  116.6 41.2 %collective-permute-start.14 = (bf16[384,512]{1,0:T(8,128)(2,1)S(1)}, bf16[384,512]{1,0:T(8,128)(2,1)S(1)}, u32[]{:S(2)}, u32[]{:S(2)}) collective-permute-start(bf16[384,512]{1,0:T(8,128)(2,1)S(1)} %collective-permute-done.13.refs_5_), channel_id=1, source_target_pairs={{1,5},{5,9},{8,12},{12,0},{3,7},{7,11},{10,14},{14,2},{17,21},{21,... | collective-permute-start | bytes 1179656 | tf_op jit(solution)/shard_map/ppermute | solution.py:448
  120.1 37.8 %collective-permute-start.12 = (bf16[384,512]{1,0:T(8,128)(2,1)S(1)}, bf16[384,512]{1,0:T(8,128)(2,1)S(1)}, u32[]{:S(2)}, u32[]{:S(2)}) collective-permute-start(bf16[384,512]{1,0:T(8,128)(2,1)S(1)} %collective-permute-done.11.refs_4_), channel_id=1, source_target_pairs={{1,5},{5,9},{8,12},{12,0},{3,7},{7,11},{10,14},{14,2},{17,21},{21,... | collective-permute-start | bytes 1179656 | tf_op jit(solution)/shard_map/ppermute | solution.py:448
  (9 other events, 24.7 us)

commit v2 on v1

--- a/solution.py
+++ b/solution.py
@@ -15,7 +15,11 @@
 
 F32 = jnp.float32
 BF16 = jnp.bfloat16
-VMEM_LIMIT = 56 * 1024 * 1024
+MIB = 1024 * 1024
+SPECTRA_VMEM = 18 * MIB
+SMALL_VMEM = 8 * MIB
+PRODUCT_VMEM = 12 * MIB
+SMALL = pl.CostEstimate(flops=1000, bytes_accessed=1000, transcendentals=0)
 FINE = 64
 
 
@@ -85,14 +89,28 @@
     return summed * scale
 
 
-def fill_table(first_sample, bins_ref, table_ref, coarse_ref):
+def fill_table(first_sample, bins_ref, table_ref, coarse_ref, halfway):
     nbins = bins_ref.shape[1]
     runs = table_ref.shape[0] // FINE
     bins = bins_ref[...]
 
     def turn(ids, times):
-        angles = TWO_PI / W * ((ids * times) & (W - 1)).astype(F32)
-        return jnp.cos(angles), jnp.sin(angles)
+        phase = (ids * times) & (W - 1)
+        quarter = (phase + W // 8) // (W // 4)
+        angle = (TWO_PI / W) * (phase - quarter * (W // 4)).astype(F32)
+        square = angle * angle
+        sine = jnp.full_like(square, 1.0 / 362880)
+        for term in (-1.0 / 5040, 1.0 / 120, -1.0 / 6, 1.0):
+            sine = sine * square + term
+        sine = sine * angle
+        cosine = jnp.full_like(square, -1.0 / 3628800)
+        for term in (1.0 / 40320, -1.0 / 720, 1.0 / 24, -0.5, 1.0):
+            cosine = cosine * square + term
+        odd = (quarter & 1) == 1
+        cosine, sine = jnp.where(odd, sine, cosine), jnp.where(odd, cosine, sine)
+        cosine = jnp.where(((quarter + 1) & 2) == 2, -cosine, cosine)
+        sine = jnp.where((quarter & 2) == 2, -sine, sine)
+        return cosine, sine
 
     fine_times = lax.broadcasted_iota(jnp.int32, (FINE, nbins), 0)
     coarse_times = first_sample + FINE * lax.broadcasted_iota(jnp.int32, (runs, nbins), 0)
@@ -101,68 +119,63 @@
     for place, value in enumerate(turn(bins, coarse_times) + turn(1, coarse_times)):
         coarse_ref[place] = value
 
-    @pl.loop(0, runs)
-    def _(a):
+    def fill(a):
         cos_c, sin_c, cos_g, sin_g = (coarse_ref[i, pl.ds(a, 1), :] for i in range(4))
         taper = 0.5 - 0.5 * (cos_g * cos_h - sin_g * sin_h)
         rows = pl.ds(pl.multiple_of(a * FINE, FINE), FINE)
         table_ref[rows, :nbins] = (taper * (cos_c * cos_f - sin_c * sin_f)).astype(BF16)
         table_ref[rows, nbins:] = (-taper * (sin_c * cos_f + cos_c * sin_f)).astype(BF16)
 
-
-def spectra_kernel(with_table, split, block, where_ref, bins_or_table, traces_ref, *rest):
-    if with_table:
-        right_ref, left_ref, table_ref, right_buf, left_buf, sems, coarse_ref = rest
-    else:
-        right_ref, left_ref, right_buf, left_buf, sems = rest
-        table_ref = bins_or_table
+    pl.loop(0, runs // 2)(fill)
+    halfway()
+    pl.loop(runs // 2, runs)(fill)
+
+
+def spectra_kernel(with_table, firsts, sizes, block, where_ref, bins_or_table, traces_ref, *rest):
+    sides = len(sizes)
+    outs, bufs, sems = rest[:sides], rest[-sides - 1 : -1], rest[-1]
     windows = traces_ref.shape[0]
-    right_start = pl.multiple_of(where_ref[1] * block, 128)
-    left_start = pl.multiple_of(where_ref[2] * block + split, 128)
     copies = []
     for w in range(windows):
-        copies.append(
-            pltpu.make_async_copy(
-                traces_ref.at[w, pl.ds(right_start, split), :], right_buf.at[w], sems.at[0, w]
+        for i, size in enumerate(sizes):
+            start = pl.multiple_of(where_ref[1 + i] * block + firsts[i], 128)
+            copies.append(
+                pltpu.make_async_copy(
+                    traces_ref.at[w, pl.ds(start, size), :], bufs[i].at[w], sems.at[i, w]
+                )
             )
-        )
-        copies.append(
-            pltpu.make_async_copy(
-                traces_ref.at[w, pl.ds(left_start, block - split), :], left_buf.at[w], sems.at[1, w]
-            )
-        )
-    for copy in copies:
-        copy.start()
+    copies[0].start()
     if with_table:
-        fill_table(where_ref[0], bins_or_table, table_ref, coarse_ref)
+        table_ref, coarse_ref = rest[sides : sides + 2]
+        fill_table(where_ref[0], bins_or_table, table_ref, coarse_ref, copies[1].start)
+    else:
+        table_ref = bins_or_table
+        copies[1].start()
     width = table_ref.shape[1]
-    for w in range(windows):
-        for side, (buf, out) in enumerate(((right_buf, right_ref), (left_buf, left_ref))):
-            copies[2 * w + side].wait()
-            out[:, w * width : (w + 1) * width] = jnp.dot(
-                buf[w], table_ref[...], preferred_element_type=F32
-            ).astype(out.dtype)
-
-
-def spectra_call(where, bins_or_table, traces, split, block, with_table, dtype):
+    for index, copy in enumerate(copies):
+        w, i = divmod(index, sides)
+        copy.wait()
+        if index + 2 < len(copies):
+            copies[index + 2].start()
+        outs[i][:, w * width : (w + 1) * width] = jnp.dot(
+            bufs[i][w], table_ref[...], preferred_element_type=F32
+        ).astype(outs[i].dtype)
+
+
+def spectra_call(where, bins_or_table, traces, firsts, sizes, block, with_table, dtype):
     windows, _, samples = traces.shape
     nbins = bins_or_table.shape[1] if with_table else bins_or_table.shape[1] // 2
     lanes = windows * 2 * nbins
     vmem = pl.BlockSpec(memory_space=pltpu.VMEM)
-    out_shape = [
-        jax.ShapeDtypeStruct((split, lanes), dtype),
-        jax.ShapeDtypeStruct((block - split, lanes), dtype),
-    ]
-    scratch = [
-        pltpu.VMEM((windows, split, samples), BF16),
-        pltpu.VMEM((windows, block - split, samples), BF16),
-        pltpu.SemaphoreType.DMA((2, windows)),
-    ]
+    out_shape = [jax.ShapeDtypeStruct((size, lanes), dtype) for size in sizes]
+    scratch = []
     if with_table:
         out_shape.append(jax.ShapeDtypeStruct((samples, 2 * nbins), BF16))
         scratch.append(pltpu.VMEM((4, samples // FINE, nbins), F32))
+    scratch += [pltpu.VMEM((windows, size, samples), BF16) for size in sizes]
+    scratch.append(pltpu.SemaphoreType.DMA((len(sizes), windows)))
     return pl.pallas_call(
-        functools.partial(spectra_kernel, with_table, split, block),
+        functools.partial(spectra_kernel, with_table, firsts, sizes, block),
         out_shape=out_shape,
         in_specs=[
             pl.BlockSpec(memory_space=pltpu.SMEM),
@@ -171,12 +184,8 @@
         ],
         out_specs=[vmem] * len(out_shape),
         scratch_shapes=scratch,
-        compiler_params=pltpu.CompilerParams(vmem_limit_bytes=VMEM_LIMIT),
-        cost_estimate=pl.CostEstimate(
-            flops=2 * block * lanes * samples,
-            bytes_accessed=2 * windows * block * samples + 4 * block * lanes,
-            transcendentals=0,
-        ),
+        compiler_params=pltpu.CompilerParams(vmem_limit_bytes=SPECTRA_VMEM),
+        cost_estimate=SMALL,
         name="spectra",
     )(where, bins_or_table, traces)
 
@@ -217,12 +226,8 @@
         ],
         in_specs=[vmem] * 5,
         out_specs=[vmem] * 3,
-        compiler_params=pltpu.CompilerParams(vmem_limit_bytes=VMEM_LIMIT),
-        cost_estimate=pl.CostEstimate(
-            flops=12 * (split + rest) * lanes,
-            bytes_accessed=12 * (split + rest) * lanes,
-            transcendentals=(split + rest) * lanes // 2,
-        ),
+        compiler_params=pltpu.CompilerParams(vmem_limit_bytes=SMALL_VMEM),
+        cost_estimate=SMALL,
         name="whiten",
     )(got_r, got_l, own_r, own_l, quality)
 
@@ -261,53 +266,44 @@
         out_shape=jax.ShapeDtypeStruct((2 * LAGS, block, 2 * half), BF16),
         in_specs=[lag, lag] + [whole] * 4,
         out_specs=pl.BlockSpec((1, block, 2 * half), lambda x, l: (x * LAGS + l, 0, 0)),
-        compiler_params=pltpu.CompilerParams(vmem_limit_bytes=VMEM_LIMIT),
-        cost_estimate=pl.CostEstimate(
-            flops=6 * 2 * LAGS * block * 2 * half,
-            bytes_accessed=2 * 2 * LAGS * block * 2 * half,
-            transcendentals=0,
-        ),
+        compiler_params=pltpu.CompilerParams(vmem_limit_bytes=SMALL_VMEM),
+        cost_estimate=SMALL,
         name="rotate",
     )(cosine, sine, near_o, near_t, far_o, far_t)
 
 
 def product_kernel(gather, scale, has_base, *refs):
     info, rows = refs[:2]
-    out = refs[-4]
-    columns, tiles, sems = refs[-3:]
+    out, columns, tiles, sems = refs[-4:]
     parts = refs[2 : -5 if has_base else -4]
-    step = pl.program_id(0)
-    steps = pl.num_programs(0)
-    block = rows.shape[1]
+    steps, block, _ = rows.shape
     width = columns.shape[0]
-    start = pl.multiple_of(info[0], 128)
+    start = pl.multiple_of(info[2], 128)
+    gather(info, parts, columns)
 
     def place(index):
         side = lax.div(index, LAGS)
-        first = pl.multiple_of(info[1 + side] * block, 128)
+        slot = lax.rem(index, 2)
+        first = pl.multiple_of(info[side] * block, 128)
         return pltpu.make_async_copy(
-            tiles.at[lax.rem(index, 2)],
+            tiles.at[slot],
             out.at[lax.rem(index, LAGS), pl.ds(first, block), pl.ds(start, width)],
-            sems.at[lax.rem(index, 2)],
+            sems.at[slot],
         )
 
-    @pl.when(step == 0)
-    def _():
-        gather(info, parts, columns)
-
-    @pl.when(step >= 2)
-    def _():
-        place(step - 2).wait()
-
-    tiles[lax.rem(step, 2)] = scale * lax.dot_general(
-        rows[0], columns[...], (((1,), (1,)), ((), ())), preferred_element_type=F32
-    )
-    place(step).start()
-
-    @pl.when(step == steps - 1)
-    def _():
-        place(step - 1).wait()
-        place(step).wait()
+    @pl.loop(0, steps)
+    def _(step):
+        @pl.when(step >= 2)
+        def _():
+            place(step - 2).wait()
+
+        tiles[lax.rem(step, 2)] = scale * lax.dot_general(
+            rows[step], columns[...], (((1,), (1,)), ((), ())), preferred_element_type=F32
+        )
+        place(step).start()
+
+    place(steps - 2).wait()
+    place(steps - 1).wait()
 
 
 def product_call(info, rows, parts, gather, width, scale, base, out_shape):
@@ -315,10 +311,7 @@
     vmem = pl.BlockSpec(memory_space=pltpu.VMEM)
     anywhere = pl.BlockSpec(memory_space=pl.ANY)
     operands = [info, rows] + list(parts)
-    in_specs = [
-        pl.BlockSpec(memory_space=pltpu.SMEM),
-        pl.BlockSpec((1, block, depth), lambda s: (s, 0, 0)),
-    ] + [vmem] * len(parts)
+    in_specs = [pl.BlockSpec(memory_space=pltpu.SMEM)] + [vmem] * (1 + len(parts))
     aliases = {}
     if base is not None:
         aliases = {len(operands): 0}
@@ -326,7 +319,6 @@
         in_specs.append(anywhere)
     return pl.pallas_call(
         functools.partial(product_kernel, gather, scale, base is not None),
-        grid=(steps,),
         out_shape=out_shape,
         in_specs=in_specs,
         out_specs=anywhere,
@@ -336,18 +328,14 @@
             pltpu.SemaphoreType.DMA((2,)),
         ],
         input_output_aliases=aliases,
-        compiler_params=pltpu.CompilerParams(vmem_limit_bytes=VMEM_LIMIT),
-        cost_estimate=pl.CostEstimate(
-            flops=2 * steps * block * depth * width,
-            bytes_accessed=steps * block * (2 * depth + 4 * width),
-            transcendentals=0,
-        ),
+        compiler_params=pltpu.CompilerParams(vmem_limit_bytes=PRODUCT_VMEM),
+        cost_estimate=SMALL,
         name="products",
     )(*operands)
 
 
 def gather_full(split, info, parts, columns):
-    own_o, own_t, right_o, right_t, left_o, left_t = parts
+    own_o, own_t, right, left = parts
     half = own_o.shape[1]
 
     @pl.when(info[3] == 1)
@@ -357,44 +345,33 @@
 
     @pl.when(info[3] == 0)
     def _():
-        columns[:split, :half] = right_o[...]
-        columns[:split, half:] = right_t[...]
-        columns[split:, :half] = left_o[...]
-        columns[split:, half:] = left_t[...]
+        columns[:split, :] = right[...]
+        columns[split:, :] = left[...]
 
 
 def gather_first(info, parts, columns):
-    right_o, right_t, left_o, left_t = parts
-    half = right_o.shape[1]
-    width = columns.shape[0]
+    right, left = parts
 
     @pl.when(info[3] == 1)
     def _():
-        columns[:, :half] = right_o[:width, :]
-        columns[:, half:] = right_t[:width, :]
+        columns[...] = right[: columns.shape[0], :]
 
     @pl.when(info[3] == 0)
     def _():
-        columns[:, :half] = left_o[...]
-        columns[:, half:] = left_t[...]
+        columns[...] = left[...]
 
 
 def gather_last(overlap, info, parts, columns):
-    early_o, early_t, right_o, right_t, left_o, left_t = parts
-    half = right_o.shape[1]
-    split = right_o.shape[0]
+    early, right, left = parts
 
     @pl.when(info[3] == 1)
     def _():
-        columns[:overlap, :half] = early_o[split - overlap :, :]
-        columns[:overlap, half:] = early_t[split - overlap :, :]
-        columns[overlap:, :half] = left_o[...]
-        columns[overlap:, half:] = left_t[...]
+        columns[:overlap, :] = early[early.shape[0] - overlap :, :]
+        columns[overlap:, :] = left[...]
 
     @pl.when(info[3] == 0)
     def _():
-        columns[:, :half] = right_o[...]
-        columns[:, half:] = right_t[...]
+        columns[...] = right[...]
 
 
 def local_rings(traces, quality_mask, band_bins):
@@ -411,23 +388,26 @@
     to_left = [(i, (i - 1) % n) for i in range(n)]
     i32 = jnp.int32
 
-    def where(k):
-        return jnp.stack([z * samples, (z - 1 - k) % n, (z + 1 + k) % n]).astype(i32)
-
-    own = []
+    def where(*blocks):
+        return jnp.stack([z * samples, *(b % n for b in blocks)]).astype(i32)
+
     right, left, table = spectra_call(
-        where(0), band_bins[None, :], traces, split, block, True, BF16
+        where(z - 1, z + 1), band_bins[None, :], traces, (0, split), (split, rest), block, True, BF16
     )
     for k in range(1, n):
-        own.append(spectra_call(where(k), table, traces, split, block, False, F32))
-    for k in range(n - 1):
+        places = where(z - 1 - k, z + 1 + k)
+        if k > 1:
+            places, right, left = lax.optimization_barrier((places, right, left))
+        own_r, own_l = spectra_call(
+            places, table, traces, (0, split), (split, rest), block, False, F32
+        )
         right = lax.ppermute(right, "row", to_right)
         left = lax.ppermute(left, "row", to_left)
-        if k < n - 2:
-            right = (right.astype(F32) + own[k][0]).astype(BF16)
-            left = (left.astype(F32) + own[k][1]).astype(BF16)
+        if k < n - 1:
+            right = (right.astype(F32) + own_r).astype(BF16)
+            left = (left.astype(F32) + own_l).astype(BF16)
     quality = lax.dynamic_slice_in_dim(quality_mask, z * block, block).astype(F32)[:, None]
-    white, white_r, white_l = whiten_call(right, left, *own[-1], quality)
+    white, white_r, white_l = whiten_call(right, left, own_r, own_l, quality)
 
     def core_of(b):
         return (b % n) * 2 // n
@@ -441,16 +421,16 @@
         return found
 
     axes = ("row", "sub")
+    swap = [(0, 1), (1, 0)]
+    white_t = lax.ppermute(white, "sub", swap)
     r0 = [lax.ppermute(white_r, axes, pairs(0, 1, cross)) for cross in (False, True)]
     l0 = [lax.ppermute(white_l, axes, pairs(0, -1, cross)) for cross in (False, True)]
-    r1 = [lax.ppermute(part, axes, pairs(1, 1, False)) for part in r0]
-    l1 = [lax.ppermute(part, axes, pairs(1, -1, False)) for part in l0]
-    r2 = [lax.ppermute(part, axes, pairs(2, 1, False)) for part in r1]
-    l2 = [lax.ppermute(part, axes, pairs(2, -1, False)) for part in l1]
-
-    swap = [(0, 1), (1, 0)]
-    white_t = lax.ppermute(white, "sub", swap)
-    far = lax.ppermute(white, "col", swap)
+    r0, l0 = jnp.concatenate(r0, axis=1), jnp.concatenate(l0, axis=1)
+    r1 = lax.ppermute(r0, axes, pairs(1, 1, False))
+    l1 = lax.ppermute(l0, axes, pairs(1, -1, False))
+
+    near, white_t = lax.optimization_barrier((white, white_t))
+    far = lax.ppermute(near, "col", swap)
     far_t = lax.ppermute(far, "sub", swap)
     shifts = jnp.array([(lag - LAGS // 2) * LAG_STEP for lag in range(LAGS)], i32)
     angles = TWO_PI / W * (band_bins[None, :] * shifts[:, None] % W).astype(F32)
@@ -466,21 +446,25 @@
     scale = 1.0 / math.sqrt(2 * windows * nbins)
     out_shape = jax.ShapeDtypeStruct((LAGS, 2 * block, per_core * block), F32)
 
+    first_start = other * block + jnp.where(from_right, 0, split)
+    last_start = other * block + jnp.where(from_right, rest, 0)
+
     def info(start, flag):
-        return jnp.stack([start, x, 1 - x, flag]).astype(i32)
-
-    overlap = split - rest
+        return jnp.stack([x, 1 - x, start, flag]).astype(i32)
+
     result = product_call(
-        info(full * block, owner), rows, [white, white_t] + r1 + l1,
-        functools.partial(gather_full, split), block, scale, None, out_shape,
-    )
+        info(first_start, from_right), rows, [r0, l0], gather_first, rest, scale, None, out_shape
+    )
+    r1, l1, result = lax.optimization_barrier((r1, l1, result))
+    r2 = lax.ppermute(r1, axes, pairs(2, 1, False))
+    l2 = lax.ppermute(l1, axes, pairs(2, -1, False))
     result = product_call(
-        info(other * block + jnp.where(from_right, 0, split), from_right), rows, r0 + l0,
-        gather_first, rest, scale, result, out_shape,
+        info(full * block, owner), rows, [white, white_t, r1, l1],
+        functools.partial(gather_full, split), block, scale, result, out_shape,
     )
     return product_call(
-        info(other * block + jnp.where(from_right, rest, 0), from_right), rows, r0 + r2 + l2,
-        functools.partial(gather_last, overlap), split, scale, result, out_shape,
+        info(last_start, from_right), rows, [r0, r2, l2],
+        functools.partial(gather_last, split - rest), split, scale, result, out_shape,
     )
 
 

time: 173 us -> 138 us (0.80)
  the two profiles are of different devices: /device:TPU:1 before, /device:TPU:0 now
where the time goes in v2:
time: 138 us; the launch traced here: 136 us
  Pallas kernels  68.4 us (50%)
  starting transfers between devices  33.2 us (24%)
  waiting for transfers between devices  18.6 us (13%)
  local copies, waits for them, and re-layouts  9.88 us (7%)
  other arithmetic  5.06 us (4%)
    pallas_call x4, Pallas kernels, spectra_call(): pl.pallas_call(functools.partial(spectra_kernel, with_table, firsts, size...  34.5 us
    pallas_call x3, Pallas kernels, product_call(): pl.pallas_call(functools.partial(product_kernel, gather, scale, base is n...  28.3 us
    unnamed x14, local copies, waits for them, and re-layouts  9.67 us
    ppermute x3, waiting for transfers between devices, local_rings(): right = lax.ppermute(right, 'row', to_right)  9.34 us
    ppermute x3, starting transfers between devices, local_rings(): left = lax.ppermute(left, 'row', to_left)  8.29 us
    ppermute x2, starting transfers between devices, local_rings(): lax.ppermute(white_l, axes, pairs(0, -1, cross))  7.08 us
    ppermute x1, starting transfers between devices, local_rings(): l1 = lax.ppermute(l0, axes, pairs(1, -1, False))  6.29 us
    ppermute x2, waiting for transfers between devices, local_rings(): lax.ppermute(white_l, axes, pairs(0, -1, cross))  6.16 us
  transfers between devices with their start and end apart: 17, of which 4 were waited for; matrix products, arithmetic and copies ran while one was open for 4% of the time, Pallas kernels for 36%

profile of v2, /device:TPU:0, one launch (start us, length us, event | category | flops | bytes accessed | tf_op | source)
XLA Modules:
  0.0 135.8 jit_solution(11374902807928607390)
XLA Ops:
  0.7 9.2 %spectra.4 = (bf16[384,512]{1,0:T(8,128)(2,1)}, bf16[256,512]{1,0:T(8,128)(2,1)}, bf16[4096,256]{1,0:T(8,128)(2,1)S(1)}) custom-call(s32[3]{0:T(128)S(1)} %get-tuple-element.53.where_ref, s32[1,128]{1,0:T(1,128)S(1)} %bitcast.18, bf16[2,2560,4096]{2,1,0:T(8,128)(2,1)} %traces_ref.7), custom_call_target="tpu_custom_call" | custom-call | flops 1000 | bytes 1000 | tf_op jit(solution)/shard_map/spectra/pallas_call | solution.py:177
  9.9 5.1 %collective-permute-start.1 = (bf16[256,512]{1,0:T(8,128)(2,1)}, bf16[256,512]{1,0:T(8,128)(2,1)}, u32[]{:S(2)}, u32[]{:S(2)}) collective-permute-start(bf16[256,512]{1,0:T(8,128)(2,1)} %get-tuple-element.31), channel_id=1, source_target_pairs={{0,12},{4,0},{8,4},{12,8},{1,13},{5,1},{9,5},{13,9},{2,14},{6,2},{... | collective-permute-start | bytes 786440 | tf_op jit(solution)/shard_map/ppermute | solution.py:405
  15.0 8.5 %spectra.5 = (f32[384,512]{1,0:T(8,128)S(1)}, f32[256,512]{1,0:T(8,128)S(1)}) custom-call(s32[3]{0:T(128)S(1)} %get-tuple-element.54.where_ref, bf16[4096,256]{1,0:T(8,128)(2,1)S(1)} %get-tuple-element.29.bins_or_table, bf16[2,2560,4096]{2,1,0:T(8,128)(2,1)} %traces_ref.7), custom_call_target="tpu_custom_call" | custom-call | flops 1000 | bytes 1000 | tf_op jit(solution)/shard_map/spectra/pallas_call | solution.py:177
  23.6 1.7 %add_convert_fusion.3 = bf16[256,512]{1,0:T(8,128)(2,1)} fusion(f32[256,512]{1,0:T(8,128)S(1)} %get-tuple-element.32, bf16[256,512]{1,0:T(8,128)(2,1)} %collective-permute-done.1), kind=kLoop, calls=%fused_computation.3 | loop fusion | flops 393216 | bytes 1048576 | tf_op jit(solution)/shard_map/convert_element_type | solution.py:408
  25.3 4.9 %collective-permute-done = bf16[384,512]{1,0:T(8,128)(2,1)} collective-permute-done((bf16[384,512]{1,0:T(8,128)(2,1)}, bf16[384,512]{1,0:T(8,128)(2,1)}, u32[]{:S(2)}, u32[]{:S(2)}) %collective-permute-start) | collective-permute-done | bytes 393248 | tf_op jit(solution)/shard_map/ppermute | solution.py:404
  30.2 1.1 add_convert_fusion.1
  31.3 1.8 %collective-permute-start.3 = (bf16[256,512]{1,0:T(8,128)(2,1)}, bf16[256,512]{1,0:T(8,128)(2,1)S(1)}, u32[]{:S(2)}, u32[]{:S(2)}) collective-permute-start(bf16[256,512]{1,0:T(8,128)(2,1)} %add_convert_fusion.3), channel_id=1, source_target_pairs={{0,12},{4,0},{8,4},{12,8},{1,13},{5,1},{9,5},{13,9},{2,14},{6,2},{... | collective-permute-start | bytes 786440 | tf_op jit(solution)/shard_map/ppermute | solution.py:405
  33.5 8.5 %spectra.6 = (f32[384,512]{1,0:T(8,128)S(1)}, f32[256,512]{1,0:T(8,128)S(1)}) custom-call(s32[3]{0:T(128)S(1)} %pad_add_fusion.2.where_ref, bf16[4096,256]{1,0:T(8,128)(2,1)S(1)} %get-tuple-element.29.bins_or_table, bf16[2,2560,4096]{2,1,0:T(8,128)(2,1)} %traces_ref.7), custom_call_target="tpu_custom_call" | custom-call | flops 1000 | bytes 1000 | tf_op jit(solution)/shard_map/spectra/pallas_call | solution.py:177
  42.0 0.8 add_convert_fusion.2
  42.8 4.4 %collective-permute-done.2 = bf16[384,512]{1,0:T(8,128)(2,1)S(1)} collective-permute-done((bf16[384,512]{1,0:T(8,128)(2,1)S(1)}, bf16[384,512]{1,0:T(8,128)(2,1)S(1)}, u32[]{:S(2)}, u32[]{:S(2)}) %collective-permute-start.2) | collective-permute-done | bytes 393248 | tf_op jit(solution)/shard_map/ppermute | solution.py:404
  47.4 2.5 %collective-permute-start.4 = (bf16[384,512]{1,0:T(8,128)(2,1)S(1)}, bf16[384,512]{1,0:T(8,128)(2,1)S(1)}, u32[]{:S(2)}, u32[]{:S(2)}) collective-permute-start(bf16[384,512]{1,0:T(8,128)(2,1)S(1)} %add_convert_fusion), channel_id=1, source_target_pairs={{0,4},{4,8},{8,12},{12,0},{1,5},{5,9},{9,13},{13,1},{2,6},{6,10},{... | collective-permute-start | bytes 1179656 | tf_op jit(solution)/shard_map/ppermute | solution.py:404
  49.8 1.4 %collective-permute-start.5 = (bf16[256,512]{1,0:T(8,128)(2,1)}, bf16[256,512]{1,0:T(8,128)(2,1)S(1)}, u32[]{:S(2)}, u32[]{:S(2)}) collective-permute-start(bf16[256,512]{1,0:T(8,128)(2,1)} %add_convert_fusion.2), channel_id=1, source_target_pairs={{0,12},{4,0},{8,4},{12,8},{1,13},{5,1},{9,5},{13,9},{2,14},{6,2},{... | collective-permute-start | bytes 786440 | tf_op jit(solution)/shard_map/ppermute | solution.py:405
  51.2 0.8 dynamic-slice_convert_fusion
  52.1 8.5 %spectra.7 = (f32[384,512]{1,0:T(8,128)S(1)}, f32[256,512]{1,0:T(8,128)S(1)}) custom-call(s32[3]{0:T(128)S(1)} %pad_add_fusion.1.where_ref, bf16[4096,256]{1,0:T(8,128)(2,1)S(1)} %get-tuple-element.29.bins_or_table, bf16[2,2560,4096]{2,1,0:T(8,128)(2,1)} %traces_ref.7), custom_call_target="tpu_custom_call" | custom-call | flops 1000 | bytes 1000 | tf_op jit(solution)/shard_map/spectra/pallas_call | solution.py:177
  60.6 3.1 %collective-permute-done.5.got_l = bf16[256,512]{1,0:T(8,128)(2,1)S(1)} collective-permute-done((bf16[256,512]{1,0:T(8,128)(2,1)}, bf16[256,512]{1,0:T(8,128)(2,1)S(1)}, u32[]{:S(2)}, u32[]{:S(2)}) %collective-permute-start.5) | collective-permute-done | bytes 262176 | tf_op jit(solution)/shard_map/ppermute | solution.py:405
  63.7 1.3 whiten.1
  65.0 2.7 %collective-permute-start.9 = (bf16[384,512]{1,0:T(8,128)(2,1)}, bf16[384,512]{1,0:T(8,128)(2,1)S(1)}, u32[]{:S(2)}, u32[]{:S(2)}) collective-permute-start(bf16[384,512]{1,0:T(8,128)(2,1)} %get-tuple-element.46), channel_id=1, source_target_pairs={{0,4},{4,8},{9,13},{13,1},{2,6},{6,10},{11,15},{15,3},{16,20},{20,... | collective-permute-start | bytes 1179656 | tf_op jit(solution)/shard_map/ppermute | solution.py:426
  67.7 1.6 %collective-permute-start.7 = (bf16[640,512]{1,0:T(8,128)(2,1)S(1)}, bf16[640,512]{1,0:T(8,128)(2,1)S(1)}, u32[]{:S(2)}, u32[]{:S(2)}) collective-permute-start(bf16[640,512]{1,0:T(8,128)(2,1)S(1)} %get-tuple-element.45.near_o.refs_2_), channel_id=1, source_target_pairs={{0,2},{2,0},{1,3},{3,1},{4,6},{6,4},{5,7},{7,5},{8,10},{10,8},{9,1... | collective-permute-start | bytes 1966088 | tf_op jit(solution)/shard_map/ppermute | solution.py:433
  69.9 5.8 %collective-permute-start.12 = (bf16[256,512]{1,0:T(8,128)(2,1)}, bf16[256,512]{1,0:T(8,128)(2,1)}, u32[]{:S(2)}, u32[]{:S(2)}) collective-permute-start(bf16[256,512]{1,0:T(8,128)(2,1)} %get-tuple-element.47), channel_id=1, source_target_pairs={{0,12},{4,0},{9,5},{13,9},{2,14},{6,2},{11,7},{15,11},{16,28},{20,... | collective-permute-start | bytes 786440 | tf_op jit(solution)/shard_map/ppermute | solution.py:427
  75.8 1.3 collective-permute-start.13
  77.2 0.7 collective-permute-start.11
  77.9 6.2 %collective-permute-done.12 = bf16[256,512]{1,0:T(8,128)(2,1)} collective-permute-done((bf16[256,512]{1,0:T(8,128)(2,1)}, bf16[256,512]{1,0:T(8,128)(2,1)}, u32[]{:S(2)}, u32[]{:S(2)}) %collective-permute-start.12) | collective-permute-done | bytes 262176 | tf_op jit(solution)/shard_map/ppermute | solution.py:427
  84.1 1.0 constant_dynamic-update-slice_fusion.3
  85.1 1.2 collective-permute-start.8
  86.3 6.3 %collective-permute-start.14 = (bf16[256,1024]{1,0:T(8,128)(2,1)S(1)}, bf16[256,1024]{1,0:T(8,128)(2,1)}, u32[]{:S(2)}, u32[]{:S(2)}) collective-permute-start(bf16[256,1024]{1,0:T(8,128)(2,1)S(1)} %constant_dynamic-update-slice_fusion.2.refs_3_), channel_id=1, source_target_pairs={{0,12},{5,1},{9,5},{12,8},{2,14},{7,3},{11,7},{14,10},{16,28},{21,... | collective-permute-start | bytes 1572872 | tf_op jit(solution)/shard_map/ppermute | solution.py:430
  92.8 4.3 %rotate.1.refs_1_ = bf16[8,640,1024]{2,1,0:T(8,128)(2,1)S(1)} custom-call(f32[4,1,128]{2,1,0:T(1,128)S(1)} %get-tuple-element.52.cos_ref, f32[4,1,128]{2,1,0:T(1,128)S(1)} %get-tuple-element.51.sin_ref, bf16[640,512]{1,0:T(8,128)(2,1)S(1)} %get-tuple-element.45.near_o.refs_2_, bf16[640,512]{1,0:T(8,128)(2,1)S(1)} %collective-permute-done.6.near_t.refs_3_, ...), custom_call_target="tpu_custom_call" | custom-call | flops 1000 | bytes 1000 | tf_op jit(solution)/shard_map/rotate/pallas_call | solution.py:263
  97.1 6.7 %products.3.refs_6_ = f32[4,1280,1280]{2,1,0:T(8,128)} custom-call(s32[4]{0:T(128)S(1)} %add_add_fusion.1.refs_0_, bf16[8,640,1024]{2,1,0:T(8,128)(2,1)S(1)} %rotate.1.refs_1_, bf16[384,1024]{1,0:T(8,128)(2,1)S(1)} %constant_dynamic-update-slice_fusion.refs_2_, bf16[256,1024]{1,0:T(8,128)(2,1)S(1)} %constant_dynamic-update-slice_fusion.2.refs_3_), custom_call_target="tpu_custom_call" | custom-call | flops 1000 | bytes 1000 | tf_op jit(solution)/shard_map/products/pallas_call | solution.py:320
  103.8 4.0 %copy-done = bf16[8,640,1024]{2,1,0:T(8,128)(2,1)} copy-done((bf16[8,640,1024]{2,1,0:T(8,128)(2,1)}, bf16[8,640,1024]{2,1,0:T(8,128)(2,1)S(1)}, u32[]{:S(2)}) %copy-start) | copy-done | bytes 10485784
  107.8 1.3 collective-permute-start.15
  109.9 4.0 %copy-done.1 = bf16[8,640,1024]{2,1,0:T(8,128)(2,1)S(1)} copy-done((bf16[8,640,1024]{2,1,0:T(8,128)(2,1)S(1)}, bf16[8,640,1024]{2,1,0:T(8,128)(2,1)}, u32[]{:S(2)}) %copy-start.1) | copy-done | bytes 10485784
  113.9 12.3 %products.4.refs_5_ = f32[4,1280,1280]{2,1,0:T(8,128)} custom-call(s32[4]{0:T(128)S(1)} %get-tuple-element.56.refs_0_, bf16[8,640,1024]{2,1,0:T(8,128)(2,1)S(1)} %copy-done.1, bf16[640,512]{1,0:T(8,128)(2,1)S(1)} %get-tuple-element.45.near_o.refs_2_, bf16[640,512]{1,0:T(8,128)(2,1)S(1)} %collective-permute-done.6.near_t.refs_3_, ...), custom_call_target="tpu_custom_call", output_to_operand_aliasing={{}: (6, {})} | custom-call | flops 1000 | bytes 1000 | tf_op jit(solution)/shard_map/products/pallas_call | solution.py:320
  126.2 9.4 %products.5 = f32[4,1280,1280]{2,1,0:T(8,128)} custom-call(s32[4]{0:T(128)S(1)} %get-tuple-element.55.refs_0_, bf16[8,640,1024]{2,1,0:T(8,128)(2,1)S(1)} %copy-done.2, bf16[384,1024]{1,0:T(8,128)(2,1)S(1)} %constant_dynamic-update-slice_fusion.refs_2_, bf16[384,1024]{1,0:T(8,128)(2,1)} %collective-permute-done.15.refs_3_, ...), custom_call_target="tpu_custom_call", output_to_operand_aliasing={{}: (5, {})} | custom-call | flops 1000 | bytes 1000 | tf_op jit(solution)/shard_map/products/pallas_call | solution.py:320
  (40 shorter events, 3.3 us)
Async XLA Ops:
  0.1 0.7 copy-start.3
  9.9 13.7 %collective-permute-start.1 = (bf16[256,512]{1,0:T(8,128)(2,1)}, bf16[256,512]{1,0:T(8,128)(2,1)}, u32[]{:S(2)}, u32[]{:S(2)}) collective-permute-start(bf16[256,512]{1,0:T(8,128)(2,1)} %get-tuple-element.31), channel_id=1, source_target_pairs={{0,12},{4,0},{8,4},{12,8},{1,13},{5,1},{9,5},{13,9},{2,14},{6,2},{... | collective-permute-start | bytes 786440 | tf_op jit(solution)/shard_map/ppermute | solution.py:405
  15.0 15.2 %collective-permute-start = (bf16[384,512]{1,0:T(8,128)(2,1)}, bf16[384,512]{1,0:T(8,128)(2,1)}, u32[]{:S(2)}, u32[]{:S(2)}) collective-permute-start(bf16[384,512]{1,0:T(8,128)(2,1)} %get-tuple-element.28), channel_id=1, source_target_pairs={{0,4},{4,8},{8,12},{12,0},{1,5},{5,9},{9,13},{13,1},{2,6},{6,10},{... | collective-permute-start | bytes 1179656 | tf_op jit(solution)/shard_map/ppermute | solution.py:404
  31.3 10.6 %collective-permute-start.3 = (bf16[256,512]{1,0:T(8,128)(2,1)}, bf16[256,512]{1,0:T(8,128)(2,1)S(1)}, u32[]{:S(2)}, u32[]{:S(2)}) collective-permute-start(bf16[256,512]{1,0:T(8,128)(2,1)} %add_convert_fusion.3), channel_id=1, source_target_pairs={{0,12},{4,0},{8,4},{12,8},{1,13},{5,1},{9,5},{13,9},{2,14},{6,2},{... | collective-permute-start | bytes 786440 | tf_op jit(solution)/shard_map/ppermute | solution.py:405
  33.1 14.1 %collective-permute-start.2 = (bf16[384,512]{1,0:T(8,128)(2,1)S(1)}, bf16[384,512]{1,0:T(8,128)(2,1)S(1)}, u32[]{:S(2)}, u32[]{:S(2)}) collective-permute-start(bf16[384,512]{1,0:T(8,128)(2,1)S(1)} %add_convert_fusion.1), channel_id=1, source_target_pairs={{0,4},{4,8},{8,12},{12,0},{1,5},{5,9},{9,13},{13,1},{2,6},{6,10},{... | collective-permute-start | bytes 1179656 | tf_op jit(solution)/shard_map/ppermute | solution.py:404
  42.0 50.7 %copy-start.4 = (s32[128]{0:T(128)S(1)}, s32[128]{0:T(128)}, u32[]{:S(2)}) copy-start(s32[128]{0:T(128)} %param.6) | copy-start | bytes 1540
  42.0 50.7 %copy-start.5 = (s32[4]{0:T(128)S(1)}, s32[4]{0:T(128)}, u32[]{:S(2)}) copy-start(s32[4]{0:T(128)} %constant.121.clone) | copy-start | bytes 52
  47.4 16.4 %collective-permute-start.4 = (bf16[384,512]{1,0:T(8,128)(2,1)S(1)}, bf16[384,512]{1,0:T(8,128)(2,1)S(1)}, u32[]{:S(2)}, u32[]{:S(2)}) collective-permute-start(bf16[384,512]{1,0:T(8,128)(2,1)S(1)} %add_convert_fusion), channel_id=1, source_target_pairs={{0,4},{4,8},{8,12},{12,0},{1,5},{5,9},{9,13},{13,1},{2,6},{6,10},{... | collective-permute-start | bytes 1179656 | tf_op jit(solution)/shard_map/ppermute | solution.py:404
  49.8 13.9 %collective-permute-start.5 = (bf16[256,512]{1,0:T(8,128)(2,1)}, bf16[256,512]{1,0:T(8,128)(2,1)S(1)}, u32[]{:S(2)}, u32[]{:S(2)}) collective-permute-start(bf16[256,512]{1,0:T(8,128)(2,1)} %add_convert_fusion.2), channel_id=1, source_target_pairs={{0,12},{4,0},{8,4},{12,8},{1,13},{5,1},{9,5},{13,9},{2,14},{6,2},{... | collective-permute-start | bytes 786440 | tf_op jit(solution)/shard_map/ppermute | solution.py:405
  65.0 2.7 %collective-permute-start.6 = (bf16[640,512]{1,0:T(8,128)(2,1)S(1)}, bf16[640,512]{1,0:T(8,128)(2,1)S(1)}, u32[]{:S(2)}, u32[]{:S(2)}) collective-permute-start(bf16[640,512]{1,0:T(8,128)(2,1)S(1)} %get-tuple-element.45.near_o.refs_2_), channel_id=1, source_target_pairs={{0,1},{1,0},{2,3},{3,2},{4,5},{5,4},{6,7},{7,6},{8,9},{9,8},{10,11... | collective-permute-start | bytes 1966088 | tf_op jit(solution)/shard_map/ppermute | solution.py:425
  65.0 12.1 %collective-permute-start.9 = (bf16[384,512]{1,0:T(8,128)(2,1)}, bf16[384,512]{1,0:T(8,128)(2,1)S(1)}, u32[]{:S(2)}, u32[]{:S(2)}) collective-permute-start(bf16[384,512]{1,0:T(8,128)(2,1)} %get-tuple-element.46), channel_id=1, source_target_pairs={{0,4},{4,8},{9,13},{13,1},{2,6},{6,10},{11,15},{15,3},{16,20},{20,... | collective-permute-start | bytes 1179656 | tf_op jit(solution)/shard_map/ppermute | solution.py:426
  67.7 17.4 %collective-permute-start.7 = (bf16[640,512]{1,0:T(8,128)(2,1)S(1)}, bf16[640,512]{1,0:T(8,128)(2,1)S(1)}, u32[]{:S(2)}, u32[]{:S(2)}) collective-permute-start(bf16[640,512]{1,0:T(8,128)(2,1)S(1)} %get-tuple-element.45.near_o.refs_2_), channel_id=1, source_target_pairs={{0,2},{2,0},{1,3},{3,1},{4,6},{6,4},{5,7},{7,5},{8,10},{10,8},{9,1... | collective-permute-start | bytes 1966088 | tf_op jit(solution)/shard_map/ppermute | solution.py:433
  69.3 7.9 %collective-permute-start.10 = (bf16[384,512]{1,0:T(8,128)(2,1)}, bf16[384,512]{1,0:T(8,128)(2,1)S(1)}, u32[]{:S(2)}, u32[]{:S(2)}) collective-permute-start(bf16[384,512]{1,0:T(8,128)(2,1)} %get-tuple-element.46), channel_id=1, source_target_pairs={{1,4},{5,8},{8,13},{12,1},{3,6},{7,10},{10,15},{14,3},{17,20},{21,... | collective-permute-start | bytes 1179656 | tf_op jit(solution)/shard_map/ppermute | solution.py:426
  69.9 14.1 %collective-permute-start.12 = (bf16[256,512]{1,0:T(8,128)(2,1)}, bf16[256,512]{1,0:T(8,128)(2,1)}, u32[]{:S(2)}, u32[]{:S(2)}) collective-permute-start(bf16[256,512]{1,0:T(8,128)(2,1)} %get-tuple-element.47), channel_id=1, source_target_pairs={{0,12},{4,0},{9,5},{13,9},{2,14},{6,2},{11,7},{15,11},{16,28},{20,... | collective-permute-start | bytes 786440 | tf_op jit(solution)/shard_map/ppermute | solution.py:427
  75.8 10.5 %collective-permute-start.13 = (bf16[256,512]{1,0:T(8,128)(2,1)}, bf16[256,512]{1,0:T(8,128)(2,1)S(1)}, u32[]{:S(2)}, u32[]{:S(2)}) collective-permute-start(bf16[256,512]{1,0:T(8,128)(2,1)} %get-tuple-element.47), channel_id=1, source_target_pairs={{1,12},{5,0},{8,5},{12,9},{3,14},{7,2},{10,7},{14,11},{17,28},{21,... | collective-permute-start | bytes 786440 | tf_op jit(solution)/shard_map/ppermute | solution.py:427
  77.2 30.6 %collective-permute-start.11 = (bf16[384,1024]{1,0:T(8,128)(2,1)S(1)}, bf16[384,1024]{1,0:T(8,128)(2,1)S(1)}, u32[]{:S(2)}, u32[]{:S(2)}) collective-permute-start(bf16[384,1024]{1,0:T(8,128)(2,1)S(1)} %constant_dynamic-update-slice_fusion.refs_2_), channel_id=1, source_target_pairs={{1,5},{4,8},{8,12},{13,1},{3,7},{6,10},{10,14},{15,3},{17,21},{20,... | collective-permute-start | bytes 2359304 | tf_op jit(solution)/shard_map/ppermute | solution.py:429
  85.1 7.8 %collective-permute-start.8 = (bf16[640,512]{1,0:T(8,128)(2,1)S(1)}, bf16[640,512]{1,0:T(8,128)(2,1)S(1)}, u32[]{:S(2)}, u32[]{:S(2)}) collective-permute-start(bf16[640,512]{1,0:T(8,128)(2,1)S(1)} %collective-permute-done.7.far_o), channel_id=1, source_target_pairs={{0,1},{1,0},{2,3},{3,2},{4,5},{5,4},{6,7},{7,6},{8,9},{9,8},{10,11... | collective-permute-start | bytes 1966088 | tf_op jit(solution)/shard_map/ppermute | solution.py:434
  86.3 21.5 %collective-permute-start.14 = (bf16[256,1024]{1,0:T(8,128)(2,1)S(1)}, bf16[256,1024]{1,0:T(8,128)(2,1)}, u32[]{:S(2)}, u32[]{:S(2)}) collective-permute-start(bf16[256,1024]{1,0:T(8,128)(2,1)S(1)} %constant_dynamic-update-slice_fusion.2.refs_3_), channel_id=1, source_target_pairs={{0,12},{5,1},{9,5},{12,8},{2,14},{7,3},{11,7},{14,10},{16,28},{21,... | collective-permute-start | bytes 1572872 | tf_op jit(solution)/shard_map/ppermute | solution.py:430
  103.8 4.0 %copy-start = (bf16[8,640,1024]{2,1,0:T(8,128)(2,1)}, bf16[8,640,1024]{2,1,0:T(8,128)(2,1)S(1)}, u32[]{:S(2)}) copy-start(bf16[8,640,1024]{2,1,0:T(8,128)(2,1)S(1)} %rotate.1.refs_1_) | copy-start | bytes 31457284
  107.8 18.4 %collective-permute-start.15 = (bf16[384,1024]{1,0:T(8,128)(2,1)S(1)}, bf16[384,1024]{1,0:T(8,128)(2,1)}, u32[]{:S(2)}, u32[]{:S(2)}) collective-permute-start(bf16[384,1024]{1,0:T(8,128)(2,1)S(1)} %collective-permute-done.11.refs_4_), channel_id=1, source_target_pairs={{1,5},{5,9},{8,12},{12,0},{3,7},{7,11},{10,14},{14,2},{17,21},{21,... | collective-permute-start | bytes 2359304 | tf_op jit(solution)/shard_map/ppermute | solution.py:459
  109.1 17.1 %collective-permute-start.16 = (bf16[256,1024]{1,0:T(8,128)(2,1)}, bf16[256,1024]{1,0:T(8,128)(2,1)S(1)}, u32[]{:S(2)}, u32[]{:S(2)}) collective-permute-start(bf16[256,1024]{1,0:T(8,128)(2,1)} %collective-permute-done.14.refs_5_), channel_id=1, source_target_pairs={{1,13},{5,1},{8,4},{12,8},{3,15},{7,3},{10,6},{14,10},{17,29},{21,... | collective-permute-start | bytes 1572872 | tf_op jit(solution)/shard_map/ppermute | solution.py:460
  109.9 4.0 %copy-start.1 = (bf16[8,640,1024]{2,1,0:T(8,128)(2,1)S(1)}, bf16[8,640,1024]{2,1,0:T(8,128)(2,1)}, u32[]{:S(2)}) copy-start(bf16[8,640,1024]{2,1,0:T(8,128)(2,1)} %copy-done) | copy-start | bytes 31457284
  113.9 12.3 %copy-start.2 = (bf16[8,640,1024]{2,1,0:T(8,128)(2,1)S(1)}, bf16[8,640,1024]{2,1,0:T(8,128)(2,1)}, u32[]{:S(2)}) copy-start(bf16[8,640,1024]{2,1,0:T(8,128)(2,1)} %copy-done) | copy-start | bytes 31457284

commit v3 on v2

--- a/solution.py
+++ b/solution.py
@@ -18,8 +18,10 @@
 MIB = 1024 * 1024
 SPECTRA_VMEM = 18 * MIB
 SMALL_VMEM = 8 * MIB
-PRODUCT_VMEM = 12 * MIB
+PRODUCT_VMEM = 16 * MIB
 SMALL = pl.CostEstimate(flops=1000, bytes_accessed=1000, transcendentals=0)
+AHEAD = 3
+ROWS_KEPT = 48
 FINE = 64
 
 
@@ -190,188 +192,254 @@
     )(where, bins_or_table, traces)
 
 
-def whiten_kernel(got_r, got_l, own_r, own_l, quality, white, white_r, white_l):
-    split = got_r.shape[0]
-    lanes = got_r.shape[1]
-    nbins = lanes // 4
-    for got, own, out, first in ((got_r, own_r, white_r, 0), (got_l, own_l, white_l, split)):
-        rows = got.shape[0]
-        mask = quality[first : first + rows, :]
-        for w in range(2):
-            low = w * 2 * nbins
-            real = got[:, low : low + nbins].astype(F32) + own[:, low : low + nbins]
-            high = low + nbins
-            imag = got[:, high : high + nbins].astype(F32) + own[:, high : high + nbins]
-            power = real * real + imag * imag
-            mean = jnp.sum(power, axis=1, keepdims=True) * (0.5 / nbins)
-            factor = mask * jnp.minimum(lax.rsqrt(power), 4.0 * lax.rsqrt(mean + 1e-05))
-            real = (real * factor).astype(BF16)
-            imag = (imag * factor).astype(BF16)
-            out[:, low : low + nbins] = real
-            out[:, high : high + nbins] = imag
-            white[first : first + rows, low : low + nbins] = real
-            white[first : first + rows, high : high + nbins] = imag
-
-
-def whiten_call(got_r, got_l, own_r, own_l, quality):
+def whiten_kernel(got, own, quality, white):
+    nbins = got.shape[1] // 4
+    mask = quality[...]
+    for w in range(2):
+        low = w * 2 * nbins
+        high = low + nbins
+        real = got[:, low : low + nbins].astype(F32) + own[:, low : low + nbins]
+        imag = got[:, high : high + nbins].astype(F32) + own[:, high : high + nbins]
+        power = real * real + imag * imag
+        mean = jnp.sum(power, axis=1, keepdims=True) * (0.5 / nbins)
+        factor = mask * jnp.minimum(lax.rsqrt(power), 4.0 * lax.rsqrt(mean + 1e-05))
+        white[:, low : low + nbins] = (real * factor).astype(BF16)
+        white[:, high : high + nbins] = (imag * factor).astype(BF16)
+
+
+def whiten_call(got, own, quality):
     vmem = pl.BlockSpec(memory_space=pltpu.VMEM)
-    split, lanes = got_r.shape
-    rest = got_l.shape[0]
     return pl.pallas_call(
         whiten_kernel,
-        out_shape=[
-            jax.ShapeDtypeStruct((split + rest, lanes), BF16),
-            jax.ShapeDtypeStruct((split, lanes), BF16),
-            jax.ShapeDtypeStruct((rest, lanes), BF16),
-        ],
-        in_specs=[vmem] * 5,
-        out_specs=[vmem] * 3,
+        out_shape=jax.ShapeDtypeStruct(got.shape, BF16),
+        in_specs=[vmem] * 3,
+        out_specs=vmem,
         compiler_params=pltpu.CompilerParams(vmem_limit_bytes=SMALL_VMEM),
         cost_estimate=SMALL,
         name="whiten",
-    )(got_r, got_l, own_r, own_l, quality)
-
-
-def rotate_kernel(cos_ref, sin_ref, near_o, near_t, far_o, far_t, out):
-    nbins = cos_ref.shape[2]
-    cosine = cos_ref[0]
-    sine = sin_ref[0]
-    half = near_o.shape[1]
-    for side, (o_ref, t_ref) in enumerate(((near_o, near_t), (far_o, far_t))):
-
-        @pl.when(pl.program_id(0) == side)
-        def _():
-            for ref, base in ((o_ref, 0), (t_ref, half)):
+    )(got, own, quality)
+
+
+def place_tile(tiles, sems, out, index, sides, start):
+    block, width = tiles.shape[1:]
+    slot = index % 2
+    first = pl.multiple_of(sides[index // LAGS] * block, 128)
+    return pltpu.make_async_copy(
+        tiles.at[slot],
+        out.at[index % LAGS, pl.ds(first, block), pl.ds(start, width)],
+        sems.at[slot],
+    )
+
+
+def times_columns(scale, rows, columns):
+    return scale * lax.dot_general(
+        rows, columns, (((1,), (1,)), ((), ())), preferred_element_type=F32
+    )
+
+
+def first_kernel(gather, scale, count, info, cos_ref, sin_ref, *refs):
+    whites = refs[:4]
+    parts = refs[4 : 4 + count]
+    out, rows_out, columns, turned, tiles, sems, row_sems = refs[4 + count :]
+    nbins = cos_ref.shape[1]
+    half = whites[0].shape[1]
+    start = pl.multiple_of(info[2], 128)
+    gather(info, parts, columns)
+    steps = 2 * LAGS
+
+    def place(index):
+        return place_tile(tiles, sems, out, index, info, start)
+
+    def keep(index):
+        slot = lax.rem(index, 2)
+        return pltpu.make_async_copy(turned.at[slot], rows_out.at[index], row_sems.at[slot])
+
+    for side in range(2):
+
+        @pl.loop(side * LAGS, (side + 1) * LAGS)
+        def _(step):
+            slot = lax.rem(step, 2)
+
+            @pl.when(step >= 2)
+            def _():
+                place(step - 2).wait()
+                keep(step - 2).wait()
+
+            lag = lax.rem(step, LAGS)
+            cosine = cos_ref[pl.ds(lag, 1), :]
+            sine = sin_ref[pl.ds(lag, 1), :]
+            for part in range(2):
+                ref = whites[2 * side + part]
                 for w in range(2):
                     low = w * 2 * nbins
                     high = low + nbins
                     real = ref[:, low : low + nbins].astype(F32)
                     imag = ref[:, high : high + nbins].astype(F32)
-                    out[0, :, base + low : base + low + nbins] = (
+                    base = part * half
+                    turned[slot, :, base + low : base + low + nbins] = (
                         real * cosine + imag * sine
                     ).astype(BF16)
-                    out[0, :, base + high : base + high + nbins] = (
+                    turned[slot, :, base + high : base + high + nbins] = (
                         imag * cosine - real * sine
                     ).astype(BF16)
-
-
-def rotate_call(cosine, sine, near_o, near_t, far_o, far_t):
-    block, half = near_o.shape
-    nbins = cosine.shape[2]
-    whole = pl.BlockSpec((block, half), lambda x, l: (0, 0))
-    lag = pl.BlockSpec((1, 1, nbins), lambda x, l: (l, 0, 0))
+            keep(step).start()
+            tiles[slot] = times_columns(scale, turned[slot], columns[...])
+            place(step).start()
+
+    for step in (steps - 2, steps - 1):
+        place(step).wait()
+        keep(step).wait()
+
+
+def first_call(info, cosine, sine, whites, parts, gather, width, scale, out_shape):
+    block, half = whites[0].shape
+    vmem = pl.BlockSpec(memory_space=pltpu.VMEM)
+    hbm = pl.BlockSpec(memory_space=pltpu.HBM)
     return pl.pallas_call(
-        rotate_kernel,
-        grid=(2, LAGS),
-        out_shape=jax.ShapeDtypeStruct((2 * LAGS, block, 2 * half), BF16),
-        in_specs=[lag, lag] + [whole] * 4,
-        out_specs=pl.BlockSpec((1, block, 2 * half), lambda x, l: (x * LAGS + l, 0, 0)),
-        compiler_params=pltpu.CompilerParams(vmem_limit_bytes=SMALL_VMEM),
+        functools.partial(first_kernel, gather, scale, len(parts)),
+        out_shape=[out_shape, jax.ShapeDtypeStruct((ROWS_KEPT, block, 2 * half), BF16)],
+        in_specs=[pl.BlockSpec(memory_space=pltpu.SMEM)] + [vmem] * (6 + len(parts)),
+        out_specs=[hbm, hbm],
+        scratch_shapes=[
+            pltpu.VMEM((width, 2 * half), BF16),
+            pltpu.VMEM((2, block, 2 * half), BF16),
+            pltpu.VMEM((2, block, width), F32),
+            pltpu.SemaphoreType.DMA((2,)),
+            pltpu.SemaphoreType.DMA((2,)),
+        ],
+        compiler_params=pltpu.CompilerParams(vmem_limit_bytes=PRODUCT_VMEM),
         cost_estimate=SMALL,
-        name="rotate",
-    )(cosine, sine, near_o, near_t, far_o, far_t)
-
-
-def product_kernel(gather, scale, has_base, *refs):
+        name="turn_products",
+    )(info, cosine, sine, *whites, *parts)
+
+
+def product_kernel(gather, scale, fetch, count, *refs):
     info, rows = refs[:2]
-    out, columns, tiles, sems = refs[-4:]
-    parts = refs[2 : -5 if has_base else -4]
-    steps, block, _ = rows.shape
-    width = columns.shape[0]
+    parts = refs[2 : 2 + count]
+    out = refs[3 + count]
+    steps = 2 * LAGS
     start = pl.multiple_of(info[2], 128)
+    if fetch:
+        held, columns, tiles, sems, fetch_sems = refs[4 + count :]
+    else:
+        columns, tiles, sems = refs[4 + count :]
+        held = rows
+
+    def place(index):
+        return place_tile(tiles, sems, out, index, info, start)
+
+    def bring(index):
+        return pltpu.make_async_copy(rows.at[index], held.at[index], fetch_sems.at[index])
+
+    if fetch:
+        for step in range(AHEAD):
+            bring(step).start()
     gather(info, parts, columns)
 
-    def place(index):
-        side = lax.div(index, LAGS)
-        slot = lax.rem(index, 2)
-        first = pl.multiple_of(info[side] * block, 128)
-        return pltpu.make_async_copy(
-            tiles.at[slot],
-            out.at[lax.rem(index, LAGS), pl.ds(first, block), pl.ds(start, width)],
-            sems.at[slot],
-        )
-
-    @pl.loop(0, steps)
-    def _(step):
+    def run(step):
+        if fetch:
+
+            @pl.when(step + AHEAD < steps)
+            def _():
+                bring(step + AHEAD).start()
+
+            bring(step).wait()
+
         @pl.when(step >= 2)
         def _():
             place(step - 2).wait()
 
-        tiles[lax.rem(step, 2)] = scale * lax.dot_general(
-            rows[step], columns[...], (((1,), (1,)), ((), ())), preferred_element_type=F32
-        )
+        tiles[lax.rem(step, 2)] = times_columns(scale, held[step], columns[...])
         place(step).start()
 
+    if fetch:
+        pl.loop(0, steps)(run)
+    else:
+        for step in range(steps):
+            if step >= 2:
+                place(step - 2).wait()
+            tiles[step % 2] = times_columns(scale, held[step], columns[...])
+            place(step).start()
     place(steps - 2).wait()
     place(steps - 1).wait()
 
 
-def product_call(info, rows, parts, gather, width, scale, base, out_shape):
-    steps, block, depth = rows.shape
+def product_call(info, rows, parts, gather, width, scale, base, fetch):
+    _, block, depth = rows.shape
     vmem = pl.BlockSpec(memory_space=pltpu.VMEM)
-    anywhere = pl.BlockSpec(memory_space=pl.ANY)
-    operands = [info, rows] + list(parts)
-    in_specs = [pl.BlockSpec(memory_space=pltpu.SMEM)] + [vmem] * (1 + len(parts))
-    aliases = {}
-    if base is not None:
-        aliases = {len(operands): 0}
-        operands.append(base)
-        in_specs.append(anywhere)
+    hbm = pl.BlockSpec(memory_space=pltpu.HBM)
+    out_shape = [jax.ShapeDtypeStruct(base.shape, base.dtype)]
+    out_specs = [hbm]
+    scratch = [
+        pltpu.VMEM((width, depth), BF16),
+        pltpu.VMEM((2, block, width), F32),
+        pltpu.SemaphoreType.DMA((2,)),
+    ]
+    if fetch:
+        out_shape.append(jax.ShapeDtypeStruct((2 * LAGS, block, depth), rows.dtype))
+        out_specs.append(vmem)
+        scratch.append(pltpu.SemaphoreType.DMA((2 * LAGS,)))
     return pl.pallas_call(
-        functools.partial(product_kernel, gather, scale, base is not None),
+        functools.partial(product_kernel, gather, scale, fetch, len(parts)),
         out_shape=out_shape,
-        in_specs=in_specs,
-        out_specs=anywhere,
-        scratch_shapes=[
-            pltpu.VMEM((width, depth), BF16),
-            pltpu.VMEM((2, block, width), F32),
-            pltpu.SemaphoreType.DMA((2,)),
-        ],
-        input_output_aliases=aliases,
+        in_specs=[pl.BlockSpec(memory_space=pltpu.SMEM), hbm if fetch else vmem]
+        + [vmem] * len(parts)
+        + [hbm],
+        out_specs=out_specs,
+        scratch_shapes=scratch,
+        input_output_aliases={2 + len(parts): 0},
         compiler_params=pltpu.CompilerParams(vmem_limit_bytes=PRODUCT_VMEM),
         cost_estimate=SMALL,
         name="products",
-    )(*operands)
-
-
-def gather_full(split, info, parts, columns):
-    own_o, own_t, right, left = parts
-    half = own_o.shape[1]
+    )(info, rows, *parts, base)
+
+
+def put(columns, first, rows, own, other):
+    half = own.shape[1]
+    count = rows.stop - rows.start
+    columns[first : first + count, :half] = own[rows, :]
+    columns[first : first + count, half:] = other[rows, :]
+
+
+def gather_full(info, parts, columns):
+    own_o, own_t, right_o, right_t, left_o, left_t = parts
+    split = right_o.shape[0]
 
     @pl.when(info[3] == 1)
     def _():
-        columns[:, :half] = own_o[...]
-        columns[:, half:] = own_t[...]
+        put(columns, 0, slice(0, own_o.shape[0]), own_o, own_t)
 
     @pl.when(info[3] == 0)
     def _():
-        columns[:split, :] = right[...]
-        columns[split:, :] = left[...]
+        put(columns, 0, slice(0, split), right_o, right_t)
+        put(columns, split, slice(0, left_o.shape[0]), left_o, left_t)
 
 
 def gather_first(info, parts, columns):
-    right, left = parts
+    right_o, right_t, left_o, left_t = parts
+    rows = slice(0, columns.shape[0])
 
     @pl.when(info[3] == 1)
     def _():
-        columns[...] = right[: columns.shape[0], :]
+        put(columns, 0, rows, right_o, right_t)
 
     @pl.when(info[3] == 0)
     def _():
-        columns[...] = left[...]
-
-
-def gather_last(overlap, info, parts, columns):
-    early, right, left = parts
+        put(columns, 0, rows, left_o, left_t)
+
+
+def gather_last(info, parts, columns):
+    early_o, early_t, right_o, right_t, left_o, left_t = parts
+    split, rest = right_o.shape[0], left_o.shape[0]
 
     @pl.when(info[3] == 1)
     def _():
-        columns[:overlap, :] = early[early.shape[0] - overlap :, :]
-        columns[overlap:, :] = left[...]
+        put(columns, 0, slice(rest, split), early_o, early_t)
+        put(columns, split - rest, slice(0, rest), left_o, left_t)
 
     @pl.when(info[3] == 0)
     def _():
-        columns[...] = right[...]
+        put(columns, 0, slice(0, split), right_o, right_t)
 
 
 def local_rings(traces, quality_mask, band_bins):
@@ -397,7 +465,7 @@
     for k in range(1, n):
         places = where(z - 1 - k, z + 1 + k)
         if k > 1:
-            places, right, left = lax.optimization_barrier((places, right, left))
+            places = lax.optimization_barrier((places, right, left))[0]
         own_r, own_l = spectra_call(
             places, table, traces, (0, split), (split, rest), block, False, F32
         )
@@ -407,37 +475,36 @@
             right = (right.astype(F32) + own_r).astype(BF16)
             left = (left.astype(F32) + own_l).astype(BF16)
     quality = lax.dynamic_slice_in_dim(quality_mask, z * block, block).astype(F32)[:, None]
-    white, white_r, white_l = whiten_call(right, left, own_r, own_l, quality)
-
-    def core_of(b):
-        return (b % n) * 2 // n
+    right = whiten_call(right, own_r, quality[:split])
+    left = whiten_call(left, own_l, quality[split:])
+    white = jnp.concatenate([right, left], axis=0)
 
     def pairs(step, move, cross):
         found = []
         for i in range(n):
-            core = core_of(i - step * move)
+            core = (i - step * move) % n * 2 // n
             source = 1 - core if cross else core
             found.append((i * 2 + source, (i + move) % n * 2 + core))
         return found
 
+    def last_step(part, move):
+        return [lax.ppermute(part, axes, pairs(n - 2, move, cross)) for cross in (False, True)]
+
     axes = ("row", "sub")
     swap = [(0, 1), (1, 0)]
+    right0 = lax.ppermute(right, "row", to_right)
+    left0 = lax.ppermute(left, "row", to_left)
     white_t = lax.ppermute(white, "sub", swap)
-    r0 = [lax.ppermute(white_r, axes, pairs(0, 1, cross)) for cross in (False, True)]
-    l0 = [lax.ppermute(white_l, axes, pairs(0, -1, cross)) for cross in (False, True)]
-    r0, l0 = jnp.concatenate(r0, axis=1), jnp.concatenate(l0, axis=1)
-    r1 = lax.ppermute(r0, axes, pairs(1, 1, False))
-    l1 = lax.ppermute(l0, axes, pairs(1, -1, False))
-
-    near, white_t = lax.optimization_barrier((white, white_t))
-    far = lax.ppermute(near, "col", swap)
+    far = lax.ppermute(white, "col", swap)
+    right1 = lax.ppermute(right0, "row", to_right)
+    left1 = lax.ppermute(left0, "row", to_left)
+    r0 = [right0, lax.ppermute(right0, "sub", swap)]
+    l0 = [left0, lax.ppermute(left0, "sub", swap)]
     far_t = lax.ppermute(far, "sub", swap)
+
     shifts = jnp.array([(lag - LAGS // 2) * LAG_STEP for lag in range(LAGS)], i32)
     angles = TWO_PI / W * (band_bins[None, :] * shifts[:, None] % W).astype(F32)
-    rows = rotate_call(
-        jnp.cos(angles)[:, None, :], jnp.sin(angles)[:, None, :], white, white_t, far, far_t
-    )
-
+    cosine, sine = jnp.cos(angles), jnp.sin(angles)
     per_core = n // 2
     owner = z // per_core == c
     from_right = (z - 1) % n // per_core == c
@@ -445,27 +512,30 @@
     other = 1 - full
     scale = 1.0 / math.sqrt(2 * windows * nbins)
     out_shape = jax.ShapeDtypeStruct((LAGS, 2 * block, per_core * block), F32)
-
     first_start = other * block + jnp.where(from_right, 0, split)
     last_start = other * block + jnp.where(from_right, rest, 0)
 
     def info(start, flag):
         return jnp.stack([x, 1 - x, start, flag]).astype(i32)
 
-    result = product_call(
-        info(first_start, from_right), rows, [r0, l0], gather_first, rest, scale, None, out_shape
-    )
-    r1, l1, result = lax.optimization_barrier((r1, l1, result))
-    r2 = lax.ppermute(r1, axes, pairs(2, 1, False))
-    l2 = lax.ppermute(l1, axes, pairs(2, -1, False))
-    result = product_call(
-        info(full * block, owner), rows, [white, white_t, r1, l1],
-        functools.partial(gather_full, split), block, scale, result, out_shape,
+    result, rows = first_call(
+        info(first_start, from_right), cosine, sine, [white, white_t, far, far_t], r0 + l0,
+        gather_first, rest, scale, out_shape,
+    )
+    right1 = lax.optimization_barrier((right1, result))[0]
+    left1 = lax.optimization_barrier((left1, result))[0]
+    r2 = last_step(right1, 1)
+    l2 = last_step(left1, -1)
+    r1 = [right1, lax.ppermute(right1, "sub", swap)]
+    l1 = [left1, lax.ppermute(left1, "sub", swap)]
+    result, rows = product_call(
+        info(full * block, owner), rows, [white, white_t] + r1 + l1,
+        gather_full, block, scale, result, True,
     )
     return product_call(
-        info(last_start, from_right), rows, [r0, r2, l2],
-        functools.partial(gather_last, split - rest), split, scale, result, out_shape,
-    )
+        info(last_start, from_right), rows, r0 + r2 + l2,
+        gather_last, split, scale, result, False,
+    )[0]
 
 
 def solution(mesh):

time: 138 us -> 131 us (0.949); the launches traced: 136 us -> 131 us
  waiting for transfers between devices: 18.6 us -> 29 us
  local copies, waits for them, and re-layouts: 9.88 us -> 2.57 us
  starting transfers between devices: 33.2 us -> 28.1 us
  other arithmetic: 5.06 us -> 3.54 us
  Pallas kernels: 68.4 us -> 67 us
    ppermute x9 -> x13, waiting for transfers between devices: 6.17 us -> 20.9 us  [the longest x1 13.1 us: local_rings(): far = lax.ppermute(white, 'col', swap)]
    ppermute x3, waiting for transfers between devices: 9.34 us -> 1.47 us  [local_rings(): right = lax.ppermute(right, 'row', to_right)]
    unnamed x14 -> x10, local copies, waits for them, and re-layouts: 9.67 us -> 2.32 us
    ppermute x9 -> x13, starting transfers between devices: 20.9 us -> 15.8 us  [the longest x4 10.7 us: last_step(): lax.ppermute(part, axes, pairs(n - 2, move, cross))]
    ppermute x3, waiting for transfers between devices: 3.1 us -> 6.67 us  [local_rings(): left = lax.ppermute(left, 'row', to_left)]
    convert_element_type x2, other arithmetic: 2.5 us -> 0.14 us  [local_rings(): left = (left.astype(F32) + own_l).astype(BF16)]
  transfers between devices with their start and end apart: 17 -> 21, of which waited for: 4 -> 8; matrix products, arithmetic and copies ran while one was open for 4% -> 3% of each run, Pallas kernels for 36% -> 37%
where the time goes in v3:
time: 131 us
  Pallas kernels  67 us (51%)
  waiting for transfers between devices  29 us (22%)
  starting transfers between devices  28.1 us (21%)
  other arithmetic  3.54 us (3%)
  local copies, waits for them, and re-layouts  2.57 us (2%)
    pallas_call x4, Pallas kernels, spectra_call(): pl.pallas_call(functools.partial(spectra_kernel, with_table, firsts, size...  33.8 us
    pallas_call x2, Pallas kernels, product_call(): pl.pallas_call(functools.partial(product_kernel, gather, scale, fetch, le...  22.9 us
    ppermute x1, waiting for transfers between devices, local_rings(): far = lax.ppermute(white, 'col', swap)  13.1 us
    ppermute x4, starting transfers between devices, last_step(): lax.ppermute(part, axes, pairs(n - 2, move, cross))  10.7 us
    pallas_call x1, Pallas kernels, first_call(): pl.pallas_call(functools.partial(first_kernel, gather, scale, len(parts))...  9.72 us
    ppermute x3, starting transfers between devices, local_rings(): left = lax.ppermute(left, 'row', to_left)  9.11 us
    ppermute x3, waiting for transfers between devices, local_rings(): left = lax.ppermute(left, 'row', to_left)  6.67 us
    ppermute x1, waiting for transfers between devices, local_rings(): right1 = lax.ppermute(right0, 'row', to_right)  5.38 us
  transfers between devices with their start and end apart: 21, of which 8 were waited for; matrix products, arithmetic and copies ran while one was open for 3% of the time, Pallas kernels for 37%

profile of v3, /device:TPU:0, one launch (start us, length us, event | category | flops | bytes accessed | tf_op | source)
XLA Modules:
  0.0 130.7 jit_solution(1554423690019913554)
XLA Ops:
  0.1 0.7 copy-done.2
  0.7 8.5 %spectra.4 = (bf16[384,512]{1,0:T(8,128)(2,1)S(1)}, bf16[256,512]{1,0:T(8,128)(2,1)S(1)}, bf16[4096,256]{1,0:T(8,128)(2,1)S(1)}) custom-call(s32[3]{0:T(128)S(1)} %get-tuple-element.41.where_ref, s32[1,128]{1,0:T(1,128)S(1)} %bitcast.18, bf16[2,2560,4096]{2,1,0:T(8,128)(2,1)} %traces_ref.7), custom_call_target="tpu_custom_call" | custom-call | flops 1000 | bytes 1000 | tf_op jit(solution)/shard_map/spectra/pallas_call | solution.py:179
  9.2 3.1 %collective-permute-start = (bf16[384,512]{1,0:T(8,128)(2,1)S(1)}, bf16[384,512]{1,0:T(8,128)(2,1)S(1)}, u32[]{:S(2)}, u32[]{:S(2)}) collective-permute-start(bf16[384,512]{1,0:T(8,128)(2,1)S(1)} %get-tuple-element.22), channel_id=1, source_target_pairs={{0,4},{4,8},{8,12},{12,0},{1,5},{5,9},{9,13},{13,1},{2,6},{6,10},{... | collective-permute-start | bytes 1179656 | tf_op jit(solution)/shard_map/ppermute | solution.py:472
  12.3 2.1 %collective-permute-start.2 = (bf16[256,512]{1,0:T(8,128)(2,1)S(1)}, bf16[256,512]{1,0:T(8,128)(2,1)S(1)}, u32[]{:S(2)}, u32[]{:S(2)}) collective-permute-start(bf16[256,512]{1,0:T(8,128)(2,1)S(1)} %get-tuple-element.25), channel_id=1, source_target_pairs={{0,12},{4,0},{8,4},{12,8},{1,13},{5,1},{9,5},{13,9},{2,14},{6,2},{... | collective-permute-start | bytes 786440 | tf_op jit(solution)/shard_map/ppermute | solution.py:473
  14.4 8.5 %spectra.5 = (f32[384,512]{1,0:T(8,128)S(1)}, f32[256,512]{1,0:T(8,128)S(1)}) custom-call(s32[3]{0:T(128)S(1)} %get-tuple-element.42.where_ref, bf16[4096,256]{1,0:T(8,128)(2,1)S(1)} %get-tuple-element.23.bins_or_table, bf16[2,2560,4096]{2,1,0:T(8,128)(2,1)} %traces_ref.7), custom_call_target="tpu_custom_call" | custom-call | flops 1000 | bytes 1000 | tf_op jit(solution)/shard_map/spectra/pallas_call | solution.py:179
  22.8 1.5 %collective-permute-done = bf16[384,512]{1,0:T(8,128)(2,1)S(1)} collective-permute-done((bf16[384,512]{1,0:T(8,128)(2,1)S(1)}, bf16[384,512]{1,0:T(8,128)(2,1)S(1)}, u32[]{:S(2)}, u32[]{:S(2)}) %collective-permute-start) | collective-permute-done | bytes 393248 | tf_op jit(solution)/shard_map/ppermute | solution.py:472
  24.6 4.1 %collective-permute-done.2 = bf16[256,512]{1,0:T(8,128)(2,1)S(1)} collective-permute-done((bf16[256,512]{1,0:T(8,128)(2,1)S(1)}, bf16[256,512]{1,0:T(8,128)(2,1)S(1)}, u32[]{:S(2)}, u32[]{:S(2)}) %collective-permute-start.2) | collective-permute-done | bytes 262176 | tf_op jit(solution)/shard_map/ppermute | solution.py:473
  28.8 3.1 %collective-permute-start.4 = (bf16[256,512]{1,0:T(8,128)(2,1)S(1)}, bf16[256,512]{1,0:T(8,128)(2,1)S(1)}, u32[]{:S(2)}, u32[]{:S(2)}) collective-permute-start(bf16[256,512]{1,0:T(8,128)(2,1)S(1)} %add_convert_fusion.3), channel_id=1, source_target_pairs={{0,12},{4,0},{8,4},{12,8},{1,13},{5,1},{9,5},{13,9},{2,14},{6,2},{... | collective-permute-start | bytes 786440 | tf_op jit(solution)/shard_map/ppermute | solution.py:473
  31.9 8.5 %spectra.6 = (f32[384,512]{1,0:T(8,128)S(1)}, f32[256,512]{1,0:T(8,128)S(1)}) custom-call(s32[3]{0:T(128)S(1)} %pad_add_fusion.4.where_ref, bf16[4096,256]{1,0:T(8,128)(2,1)S(1)} %get-tuple-element.23.bins_or_table, bf16[2,2560,4096]{2,1,0:T(8,128)(2,1)} %traces_ref.7), custom_call_target="tpu_custom_call" | custom-call | flops 1000 | bytes 1000 | tf_op jit(solution)/shard_map/spectra/pallas_call | solution.py:179
  40.4 1.9 %add_convert_fusion = bf16[384,512]{1,0:T(8,128)(2,1)} fusion(f32[384,512]{1,0:T(8,128)S(1)} %get-tuple-element.28, bf16[384,512]{1,0:T(8,128)(2,1)} %collective-permute-done.1), kind=kLoop, calls=%fused_computation | loop fusion | flops 589824 | bytes 1572864 | tf_op jit(solution)/shard_map/convert_element_type | solution.py:475
  42.3 0.9 collective-permute-done.4
  43.2 3.9 %collective-permute-start.5 = (bf16[256,512]{1,0:T(8,128)(2,1)S(1)}, bf16[256,512]{1,0:T(8,128)(2,1)S(1)}, u32[]{:S(2)}, u32[]{:S(2)}) collective-permute-start(bf16[256,512]{1,0:T(8,128)(2,1)S(1)} %add_convert_fusion.2), channel_id=1, source_target_pairs={{0,12},{4,0},{8,4},{12,8},{1,13},{5,1},{9,5},{13,9},{2,14},{6,2},{... | collective-permute-start | bytes 786440 | tf_op jit(solution)/shard_map/ppermute | solution.py:473
  47.1 0.8 dynamic-slice_convert_fusion
  48.3 8.5 %spectra.7 = (f32[384,512]{1,0:T(8,128)S(1)}, f32[256,512]{1,0:T(8,128)S(1)}) custom-call(s32[3]{0:T(128)S(1)} %pad_add_fusion.5.where_ref, bf16[4096,256]{1,0:T(8,128)(2,1)S(1)} %get-tuple-element.23.bins_or_table, bf16[2,2560,4096]{2,1,0:T(8,128)(2,1)} %traces_ref.7), custom_call_target="tpu_custom_call" | custom-call | flops 1000 | bytes 1000 | tf_op jit(solution)/shard_map/spectra/pallas_call | solution.py:179
  56.7 1.7 %collective-permute-done.5.got = bf16[256,512]{1,0:T(8,128)(2,1)S(1)} collective-permute-done((bf16[256,512]{1,0:T(8,128)(2,1)S(1)}, bf16[256,512]{1,0:T(8,128)(2,1)S(1)}, u32[]{:S(2)}, u32[]{:S(2)}) %collective-permute-start.5) | collective-permute-done | bytes 262176 | tf_op jit(solution)/shard_map/ppermute | solution.py:473
  59.1 1.6 %collective-permute-start.7 = (bf16[640,512]{1,0:T(8,128)(2,1)S(1)}, bf16[640,512]{1,0:T(8,128)(2,1)S(1)}, u32[]{:S(2)}, u32[]{:S(2)}) collective-permute-start(bf16[640,512]{1,0:T(8,128)(2,1)S(1)} %pad_maximum_fusion.refs_0_.refs_2_), channel_id=1, source_target_pairs={{0,2},{2,0},{1,3},{3,1},{4,6},{6,4},{5,7},{7,5},{8,10},{10,8},{9,1... | collective-permute-start | bytes 1966088 | tf_op jit(solution)/shard_map/ppermute | solution.py:498
  60.6 1.7 %collective-permute-start.11 = (bf16[256,512]{1,0:T(8,128)(2,1)S(1)}, bf16[256,512]{1,0:T(8,128)(2,1)}, u32[]{:S(2)}, u32[]{:S(2)}) collective-permute-start(bf16[256,512]{1,0:T(8,128)(2,1)S(1)} %whiten.3), channel_id=1, source_target_pairs={{0,12},{4,0},{8,4},{12,8},{1,13},{5,1},{9,5},{13,9},{2,14},{6,2},{... | collective-permute-start | bytes 786440 | tf_op jit(solution)/shard_map/ppermute | solution.py:496
  62.6 13.1 %collective-permute-done.7.refs_2_ = bf16[640,512]{1,0:T(8,128)(2,1)S(1)} collective-permute-done((bf16[640,512]{1,0:T(8,128)(2,1)S(1)}, bf16[640,512]{1,0:T(8,128)(2,1)S(1)}, u32[]{:S(2)}, u32[]{:S(2)}) %collective-permute-start.7) | collective-permute-done | bytes 655392 | tf_op jit(solution)/shard_map/ppermute | solution.py:498
  75.8 1.3 %collective-permute-done.11.refs_6_ = bf16[256,512]{1,0:T(8,128)(2,1)} collective-permute-done((bf16[256,512]{1,0:T(8,128)(2,1)S(1)}, bf16[256,512]{1,0:T(8,128)(2,1)}, u32[]{:S(2)}, u32[]{:S(2)}) %collective-permute-start.11) | collective-permute-done | bytes 262176 | tf_op jit(solution)/shard_map/ppermute | solution.py:496
  77.1 0.5 collective-permute-start.10
  77.6 0.6 collective-permute-start.15
  78.2 1.0 collective-permute-done.12.refs_7_
  79.9 9.7 %turn_products.1 = (f32[4,1280,1280]{2,1,0:T(8,128)}, bf16[48,640,1024]{2,1,0:T(8,128)(2,1)}) custom-call(s32[4]{0:T(128)S(1)} %add_add_fusion.1.info, f32[4,128]{1,0:T(4,128)S(1)} %get-tuple-element.40.cos_ref, f32[4,128]{1,0:T(4,128)S(1)} %get-tuple-element.39.sin_ref, bf16[640,512]{1,0:T(8,128)(2,1)S(1)} %pad_maximum_fusion.refs_0_.refs_2_, ...), custom_call_target="tpu_custom_call" | custom-call | flops 1000 | bytes 1000 | tf_op jit(solution)/shard_map/turn_products/pallas_call | solution.py:298
  89.7 5.4 %collective-permute-done.13.refs_4_ = bf16[384,512]{1,0:T(8,128)(2,1)} collective-permute-done((bf16[384,512]{1,0:T(8,128)(2,1)S(1)}, bf16[384,512]{1,0:T(8,128)(2,1)}, u32[]{:S(2)}, u32[]{:S(2)}) %collective-permute-start.13) | collective-permute-done | bytes 393248 | tf_op jit(solution)/shard_map/ppermute | solution.py:499
  95.1 1.3 collective-permute-start.17
  96.4 4.0 %collective-permute-start.18 = (bf16[384,512]{1,0:T(8,128)(2,1)}, bf16[384,512]{1,0:T(8,128)(2,1)S(1)}, u32[]{:S(2)}, u32[]{:S(2)}) collective-permute-start(bf16[384,512]{1,0:T(8,128)(2,1)} %collective-permute-done.13.refs_4_), channel_id=1, source_target_pairs={{0,5},{4,9},{9,12},{13,0},{2,7},{6,11},{11,14},{15,2},{16,21},{20,... | collective-permute-start | bytes 1179656 | tf_op jit(solution)/shard_map/ppermute | solution.py:491
  100.4 0.7 collective-permute-start.19
  101.1 0.7 copy-done
  101.8 4.6 %collective-permute-start.20 = (bf16[256,512]{1,0:T(8,128)(2,1)}, bf16[256,512]{1,0:T(8,128)(2,1)}, u32[]{:S(2)}, u32[]{:S(2)}) collective-permute-start(bf16[256,512]{1,0:T(8,128)(2,1)} %collective-permute-done.15.refs_6_), channel_id=1, source_target_pairs={{0,13},{4,1},{9,4},{13,8},{2,15},{6,3},{11,6},{15,10},{16,29},{20,... | collective-permute-start | bytes 786440 | tf_op jit(solution)/shard_map/ppermute | solution.py:491
  106.6 1.0 copy-done.1
  107.6 13.5 %products.2 = (f32[4,1280,1280]{2,1,0:T(8,128)}, bf16[8,640,1024]{2,1,0:T(8,128)(2,1)S(1)}) custom-call(s32[4]{0:T(128)S(1)} %pad_add_fusion.1.refs_0_, bf16[48,640,1024]{2,1,0:T(8,128)(2,1)} %get-tuple-element.33.refs_1_, bf16[640,512]{1,0:T(8,128)(2,1)S(1)} %pad_maximum_fusion.refs_0_.refs_2_, ...), custom_call_target="tpu_custom_call", output_to_operand_aliasing={{0}: (8, {})} | custom-call | flops 1000 | bytes 1000 | tf_op jit(solution)/shard_map/products/pallas_call | solution.py:382
  121.1 9.4 %products.3 = f32[4,1280,1280]{2,1,0:T(8,128)} custom-call(s32[4]{0:T(128)S(1)} %add_add_fusion.refs_0_, bf16[8,640,1024]{2,1,0:T(8,128)(2,1)S(1)} %get-tuple-element.37.refs_1_, bf16[384,512]{1,0:T(8,128)(2,1)S(1)} %collective-permute-done.9.refs_4_.refs_2_, ...), custom_call_target="tpu_custom_call", output_to_operand_aliasing={{}: (8, {})} | custom-call | flops 1000 | bytes 1000 | tf_op jit(solution)/shard_map/products/pallas_call | solution.py:382
  (46 shorter events, 2.6 us)
Async XLA Ops:
  0.1 0.7 copy-start.2
  9.2 15.1 %collective-permute-start = (bf16[384,512]{1,0:T(8,128)(2,1)S(1)}, bf16[384,512]{1,0:T(8,128)(2,1)S(1)}, u32[]{:S(2)}, u32[]{:S(2)}) collective-permute-start(bf16[384,512]{1,0:T(8,128)(2,1)S(1)} %get-tuple-element.22), channel_id=1, source_target_pairs={{0,4},{4,8},{8,12},{12,0},{1,5},{5,9},{9,13},{13,1},{2,6},{6,10},{... | collective-permute-start | bytes 1179656 | tf_op jit(solution)/shard_map/ppermute | solution.py:472
  12.3 16.4 %collective-permute-start.2 = (bf16[256,512]{1,0:T(8,128)(2,1)S(1)}, bf16[256,512]{1,0:T(8,128)(2,1)S(1)}, u32[]{:S(2)}, u32[]{:S(2)}) collective-permute-start(bf16[256,512]{1,0:T(8,128)(2,1)S(1)} %get-tuple-element.25), channel_id=1, source_target_pairs={{0,12},{4,0},{8,4},{12,8},{1,13},{5,1},{9,5},{13,9},{2,14},{6,2},{... | collective-permute-start | bytes 786440 | tf_op jit(solution)/shard_map/ppermute | solution.py:473
  24.4 15.9 %collective-permute-start.1 = (bf16[384,512]{1,0:T(8,128)(2,1)S(1)}, bf16[384,512]{1,0:T(8,128)(2,1)}, u32[]{:S(2)}, u32[]{:S(2)}) collective-permute-start(bf16[384,512]{1,0:T(8,128)(2,1)S(1)} %add_convert_fusion.1), channel_id=1, source_target_pairs={{0,4},{4,8},{8,12},{12,0},{1,5},{5,9},{9,13},{13,1},{2,6},{6,10},{... | collective-permute-start | bytes 1179656 | tf_op jit(solution)/shard_map/ppermute | solution.py:472
  28.8 14.4 %collective-permute-start.4 = (bf16[256,512]{1,0:T(8,128)(2,1)S(1)}, bf16[256,512]{1,0:T(8,128)(2,1)S(1)}, u32[]{:S(2)}, u32[]{:S(2)}) collective-permute-start(bf16[256,512]{1,0:T(8,128)(2,1)S(1)} %add_convert_fusion.3), channel_id=1, source_target_pairs={{0,12},{4,0},{8,4},{12,8},{1,13},{5,1},{9,5},{13,9},{2,14},{6,2},{... | collective-permute-start | bytes 786440 | tf_op jit(solution)/shard_map/ppermute | solution.py:473
  40.3 39.4 %copy-start.3 = (s32[128]{0:T(128)S(1)}, s32[128]{0:T(128)}, u32[]{:S(2)}) copy-start(s32[128]{0:T(128)} %param.6) | copy-start | bytes 1540
  40.4 39.4 %copy-start.4 = (s32[4]{0:T(128)S(1)}, s32[4]{0:T(128)}, u32[]{:S(2)}) copy-start(s32[4]{0:T(128)} %constant.121.clone) | copy-start | bytes 52
  42.3 16.4 %collective-permute-start.3 = (bf16[384,512]{1,0:T(8,128)(2,1)}, bf16[384,512]{1,0:T(8,128)(2,1)S(1)}, u32[]{:S(2)}, u32[]{:S(2)}) collective-permute-start(bf16[384,512]{1,0:T(8,128)(2,1)} %add_convert_fusion), channel_id=1, source_target_pairs={{0,4},{4,8},{8,12},{12,0},{1,5},{5,9},{9,13},{13,1},{2,6},{6,10},{... | collective-permute-start | bytes 1179656 | tf_op jit(solution)/shard_map/ppermute | solution.py:472
  43.2 15.2 %collective-permute-start.5 = (bf16[256,512]{1,0:T(8,128)(2,1)S(1)}, bf16[256,512]{1,0:T(8,128)(2,1)S(1)}, u32[]{:S(2)}, u32[]{:S(2)}) collective-permute-start(bf16[256,512]{1,0:T(8,128)(2,1)S(1)} %add_convert_fusion.2), channel_id=1, source_target_pairs={{0,12},{4,0},{8,4},{12,8},{1,13},{5,1},{9,5},{13,9},{2,14},{6,2},{... | collective-permute-start | bytes 786440 | tf_op jit(solution)/shard_map/ppermute | solution.py:473
  59.1 16.7 %collective-permute-start.7 = (bf16[640,512]{1,0:T(8,128)(2,1)S(1)}, bf16[640,512]{1,0:T(8,128)(2,1)S(1)}, u32[]{:S(2)}, u32[]{:S(2)}) collective-permute-start(bf16[640,512]{1,0:T(8,128)(2,1)S(1)} %pad_maximum_fusion.refs_0_.refs_2_), channel_id=1, source_target_pairs={{0,2},{2,0},{1,3},{3,1},{4,6},{6,4},{5,7},{7,5},{8,10},{10,8},{9,1... | collective-permute-start | bytes 1966088 | tf_op jit(solution)/shard_map/ppermute | solution.py:498
  60.6 16.5 %collective-permute-start.11 = (bf16[256,512]{1,0:T(8,128)(2,1)S(1)}, bf16[256,512]{1,0:T(8,128)(2,1)}, u32[]{:S(2)}, u32[]{:S(2)}) collective-permute-start(bf16[256,512]{1,0:T(8,128)(2,1)S(1)} %whiten.3), channel_id=1, source_target_pairs={{0,12},{4,0},{8,4},{12,8},{1,13},{5,1},{9,5},{13,9},{2,14},{6,2},{... | collective-permute-start | bytes 786440 | tf_op jit(solution)/shard_map/ppermute | solution.py:496
  62.3 14.8 %collective-permute-start.9 = (bf16[384,512]{1,0:T(8,128)(2,1)S(1)}, bf16[384,512]{1,0:T(8,128)(2,1)S(1)}, u32[]{:S(2)}, u32[]{:S(2)}) collective-permute-start(bf16[384,512]{1,0:T(8,128)(2,1)S(1)} %whiten.2), channel_id=1, source_target_pairs={{0,4},{4,8},{8,12},{12,0},{1,5},{5,9},{9,13},{13,1},{2,6},{6,10},{... | collective-permute-start | bytes 1179656 | tf_op jit(solution)/shard_map/ppermute | solution.py:495
  62.6 17.2 %collective-permute-start.6 = (bf16[640,512]{1,0:T(8,128)(2,1)S(1)}, bf16[640,512]{1,0:T(8,128)(2,1)S(1)}, u32[]{:S(2)}, u32[]{:S(2)}) collective-permute-start(bf16[640,512]{1,0:T(8,128)(2,1)S(1)} %pad_maximum_fusion.refs_0_.refs_2_), channel_id=1, source_target_pairs={{0,1},{1,0},{2,3},{3,2},{4,5},{5,4},{6,7},{7,6},{8,9},{9,8},{10,11... | collective-permute-start | bytes 1966088 | tf_op jit(solution)/shard_map/ppermute | solution.py:497
  75.8 4.1 %collective-permute-start.8 = (bf16[640,512]{1,0:T(8,128)(2,1)S(1)}, bf16[640,512]{1,0:T(8,128)(2,1)S(1)}, u32[]{:S(2)}, u32[]{:S(2)}) collective-permute-start(bf16[640,512]{1,0:T(8,128)(2,1)S(1)} %collective-permute-done.7.refs_2_), channel_id=1, source_target_pairs={{0,1},{1,0},{2,3},{3,2},{4,5},{5,4},{6,7},{7,6},{8,9},{9,8},{10,11... | collective-permute-start | bytes 1966088 | tf_op jit(solution)/shard_map/ppermute | solution.py:503
  77.1 2.2 %collective-permute-start.12 = (bf16[256,512]{1,0:T(8,128)(2,1)}, bf16[256,512]{1,0:T(8,128)(2,1)}, u32[]{:S(2)}, u32[]{:S(2)}) collective-permute-start(bf16[256,512]{1,0:T(8,128)(2,1)} %collective-permute-done.11.refs_6_), channel_id=1, source_target_pairs={{0,1},{1,0},{2,3},{3,2},{4,5},{5,4},{6,7},{7,6},{8,9},{9,8},{10,11... | collective-permute-start | bytes 786440 | tf_op jit(solution)/shard_map/ppermute | solution.py:502
  77.1 2.8 %collective-permute-start.10 = (bf16[384,512]{1,0:T(8,128)(2,1)S(1)}, bf16[384,512]{1,0:T(8,128)(2,1)S(1)}, u32[]{:S(2)}, u32[]{:S(2)}) collective-permute-start(bf16[384,512]{1,0:T(8,128)(2,1)S(1)} %collective-permute-done.9.refs_4_.refs_2_), channel_id=1, source_target_pairs={{0,1},{1,0},{2,3},{3,2},{4,5},{5,4},{6,7},{7,6},{8,9},{9,8},{10,11... | collective-permute-start | bytes 1179656 | tf_op jit(solution)/shard_map/ppermute | solution.py:501
  77.6 12.0 %collective-permute-start.15 = (bf16[256,512]{1,0:T(8,128)(2,1)}, bf16[256,512]{1,0:T(8,128)(2,1)}, u32[]{:S(2)}, u32[]{:S(2)}) collective-permute-start(bf16[256,512]{1,0:T(8,128)(2,1)} %collective-permute-done.11.refs_6_), channel_id=1, source_target_pairs={{0,12},{4,0},{8,4},{12,8},{1,13},{5,1},{9,5},{13,9},{2,14},{6,2},{... | collective-permute-start | bytes 786440 | tf_op jit(solution)/shard_map/ppermute | solution.py:500
  79.3 15.8 %collective-permute-start.13 = (bf16[384,512]{1,0:T(8,128)(2,1)S(1)}, bf16[384,512]{1,0:T(8,128)(2,1)}, u32[]{:S(2)}, u32[]{:S(2)}) collective-permute-start(bf16[384,512]{1,0:T(8,128)(2,1)S(1)} %collective-permute-done.9.refs_4_.refs_2_), channel_id=1, source_target_pairs={{0,4},{4,8},{8,12},{12,0},{1,5},{5,9},{9,13},{13,1},{2,6},{6,10},{... | collective-permute-start | bytes 1179656 | tf_op jit(solution)/shard_map/ppermute | solution.py:499
  89.6 11.5 %collective-permute-start.16 = (bf16[256,512]{1,0:T(8,128)(2,1)}, bf16[256,512]{1,0:T(8,128)(2,1)S(1)}, u32[]{:S(2)}, u32[]{:S(2)}) collective-permute-start(bf16[256,512]{1,0:T(8,128)(2,1)} %collective-permute-done.15.refs_6_), channel_id=1, source_target_pairs={{0,1},{1,0},{2,3},{3,2},{4,5},{5,4},{6,7},{7,6},{8,9},{9,8},{10,11... | collective-permute-start | bytes 786440 | tf_op jit(solution)/shard_map/ppermute | solution.py:530
  95.1 11.6 %collective-permute-start.14 = (bf16[384,512]{1,0:T(8,128)(2,1)}, bf16[384,512]{1,0:T(8,128)(2,1)S(1)}, u32[]{:S(2)}, u32[]{:S(2)}) collective-permute-start(bf16[384,512]{1,0:T(8,128)(2,1)} %collective-permute-done.13.refs_4_), channel_id=1, source_target_pairs={{0,1},{1,0},{2,3},{3,2},{4,5},{5,4},{6,7},{7,6},{8,9},{9,8},{10,11... | collective-permute-start | bytes 1179656 | tf_op jit(solution)/shard_map/ppermute | solution.py:529
  95.1 26.0 %collective-permute-start.17 = (bf16[384,512]{1,0:T(8,128)(2,1)}, bf16[384,512]{1,0:T(8,128)(2,1)S(1)}, u32[]{:S(2)}, u32[]{:S(2)}) collective-permute-start(bf16[384,512]{1,0:T(8,128)(2,1)} %collective-permute-done.13.refs_4_), channel_id=1, source_target_pairs={{1,5},{5,9},{8,12},{12,0},{3,7},{7,11},{10,14},{14,2},{17,21},{21,... | collective-permute-start | bytes 1179656 | tf_op jit(solution)/shard_map/ppermute | solution.py:491
  96.4 24.8 %collective-permute-start.18 = (bf16[384,512]{1,0:T(8,128)(2,1)}, bf16[384,512]{1,0:T(8,128)(2,1)S(1)}, u32[]{:S(2)}, u32[]{:S(2)}) collective-permute-start(bf16[384,512]{1,0:T(8,128)(2,1)} %collective-permute-done.13.refs_4_), channel_id=1, source_target_pairs={{0,5},{4,9},{9,12},{13,0},{2,7},{6,11},{11,14},{15,2},{16,21},{20,... | collective-permute-start | bytes 1179656 | tf_op jit(solution)/shard_map/ppermute | solution.py:491
  100.4 20.7 %collective-permute-start.19 = (bf16[256,512]{1,0:T(8,128)(2,1)}, bf16[256,512]{1,0:T(8,128)(2,1)S(1)}, u32[]{:S(2)}, u32[]{:S(2)}) collective-permute-start(bf16[256,512]{1,0:T(8,128)(2,1)} %collective-permute-done.15.refs_6_), channel_id=1, source_target_pairs={{1,13},{5,1},{8,4},{12,8},{3,15},{7,3},{10,6},{14,10},{17,29},{21,... | collective-permute-start | bytes 786440 | tf_op jit(solution)/shard_map/ppermute | solution.py:491
  101.1 0.7 copy-start
  101.8 19.3 %collective-permute-start.20 = (bf16[256,512]{1,0:T(8,128)(2,1)}, bf16[256,512]{1,0:T(8,128)(2,1)}, u32[]{:S(2)}, u32[]{:S(2)}) collective-permute-start(bf16[256,512]{1,0:T(8,128)(2,1)} %collective-permute-done.15.refs_6_), channel_id=1, source_target_pairs={{0,13},{4,1},{9,4},{13,8},{2,15},{6,3},{11,6},{15,10},{16,29},{20,... | collective-permute-start | bytes 786440 | tf_op jit(solution)/shard_map/ppermute | solution.py:491
  106.6 1.0 copy-start.1

commit v4 on v3

--- a/solution.py
+++ b/solution.py
@@ -220,15 +220,18 @@
     )(got, own, quality)
 
 
-def place_tile(tiles, sems, out, index, sides, start):
-    block, width = tiles.shape[1:]
+def place_tile(tiles, sems, out, index, sides, starts):
+    block = tiles.shape[1]
     slot = index % 2
     first = pl.multiple_of(sides[index // LAGS] * block, 128)
-    return pltpu.make_async_copy(
-        tiles.at[slot],
-        out.at[index % LAGS, pl.ds(first, block), pl.ds(start, width)],
-        sems.at[slot],
-    )
+    return [
+        pltpu.make_async_copy(
+            tiles.at[slot, :, pl.ds(low, lanes)],
+            out.at[index % LAGS, pl.ds(first, block), pl.ds(pl.multiple_of(start, 128), lanes)],
+            sems.at[slot, i],
+        )
+        for i, (low, lanes, start) in enumerate(starts)
+    ]
 
 
 def times_columns(scale, rows, columns):
@@ -243,12 +246,11 @@
     out, rows_out, columns, turned, tiles, sems, row_sems = refs[4 + count :]
     nbins = cos_ref.shape[1]
     half = whites[0].shape[1]
-    start = pl.multiple_of(info[2], 128)
     gather(info, parts, columns)
     steps = 2 * LAGS
 
     def place(index):
-        return place_tile(tiles, sems, out, index, info, start)
+        return place_tile(tiles, sems, out, index, info, [(0, tiles.shape[2], info[2])])[0]
 
     def keep(index):
         slot = lax.rem(index, 2)
@@ -304,7 +306,7 @@
             pltpu.VMEM((width, 2 * half), BF16),
             pltpu.VMEM((2, block, 2 * half), BF16),
             pltpu.VMEM((2, block, width), F32),
-            pltpu.SemaphoreType.DMA((2,)),
+            pltpu.SemaphoreType.DMA((2, 1)),
             pltpu.SemaphoreType.DMA((2,)),
         ],
         compiler_params=pltpu.CompilerParams(vmem_limit_bytes=PRODUCT_VMEM),
@@ -313,20 +315,27 @@
     )(info, cosine, sine, *whites, *parts)
 
 
-def product_kernel(gather, scale, fetch, count, *refs):
+def product_kernel(gather, widths, scale, fetch, count, *refs):
     info, rows = refs[:2]
     parts = refs[2 : 2 + count]
     out = refs[3 + count]
     steps = 2 * LAGS
-    start = pl.multiple_of(info[2], 128)
     if fetch:
         held, columns, tiles, sems, fetch_sems = refs[4 + count :]
     else:
         columns, tiles, sems = refs[4 + count :]
         held = rows
 
-    def place(index):
-        return place_tile(tiles, sems, out, index, info, start)
+    lows = [sum(widths[:i]) for i in range(len(widths))]
+    starts = [(lows[i], widths[i], info[2 + 2 * i]) for i in range(len(widths))]
+
+    def start_placing(index):
+        for copy in place_tile(tiles, sems, out, index, info, starts):
+            copy.start()
+
+    def end_placing(index):
+        for copy in place_tile(tiles, sems, out, index, info, starts):
+            copy.wait()
 
     def bring(index):
         return pltpu.make_async_copy(rows.at[index], held.at[index], fetch_sems.at[index])
@@ -347,25 +356,26 @@
 
         @pl.when(step >= 2)
         def _():
-            place(step - 2).wait()
+            end_placing(step - 2)
 
         tiles[lax.rem(step, 2)] = times_columns(scale, held[step], columns[...])
-        place(step).start()
+        start_placing(step)
 
     if fetch:
         pl.loop(0, steps)(run)
     else:
         for step in range(steps):
             if step >= 2:
-                place(step - 2).wait()
+                end_placing(step - 2)
             tiles[step % 2] = times_columns(scale, held[step], columns[...])
-            place(step).start()
-    place(steps - 2).wait()
-    place(steps - 1).wait()
-
-
-def product_call(info, rows, parts, gather, width, scale, base, fetch):
+            start_placing(step)
+    end_placing(steps - 2)
+    end_placing(steps - 1)
+
+
+def product_call(info, rows, parts, gather, widths, scale, base, fetch):
     _, block, depth = rows.shape
+    width = sum(widths)
     vmem = pl.BlockSpec(memory_space=pltpu.VMEM)
     hbm = pl.BlockSpec(memory_space=pltpu.HBM)
     out_shape = [jax.ShapeDtypeStruct(base.shape, base.dtype)]
@@ -373,14 +383,14 @@
     scratch = [
         pltpu.VMEM((width, depth), BF16),
         pltpu.VMEM((2, block, width), F32),
-        pltpu.SemaphoreType.DMA((2,)),
+        pltpu.SemaphoreType.DMA((2, len(widths))),
     ]
     if fetch:
         out_shape.append(jax.ShapeDtypeStruct((2 * LAGS, block, depth), rows.dtype))
         out_specs.append(vmem)
         scratch.append(pltpu.SemaphoreType.DMA((2 * LAGS,)))
     return pl.pallas_call(
-        functools.partial(product_kernel, gather, scale, fetch, len(parts)),
+        functools.partial(product_kernel, gather, widths, scale, fetch, len(parts)),
         out_shape=out_shape,
         in_specs=[pl.BlockSpec(memory_space=pltpu.SMEM), hbm if fetch else vmem]
         + [vmem] * len(parts)
@@ -403,16 +413,16 @@
 
 def gather_full(info, parts, columns):
     own_o, own_t, right_o, right_t, left_o, left_t = parts
-    split = right_o.shape[0]
+    split, count = right_o.shape[0], columns.shape[0]
 
     @pl.when(info[3] == 1)
     def _():
-        put(columns, 0, slice(0, own_o.shape[0]), own_o, own_t)
+        put(columns, 0, slice(0, count), own_o, own_t)
 
     @pl.when(info[3] == 0)
     def _():
         put(columns, 0, slice(0, split), right_o, right_t)
-        put(columns, split, slice(0, left_o.shape[0]), left_o, left_t)
+        put(columns, split, slice(0, count - split), left_o, left_t)
 
 
 def gather_first(info, parts, columns):
@@ -429,8 +439,9 @@
 
 
 def gather_last(info, parts, columns):
-    early_o, early_t, right_o, right_t, left_o, left_t = parts
+    early_o, early_t, right_o, right_t, left_o, left_t, own_o, own_t, tail_o, tail_t = parts
     split, rest = right_o.shape[0], left_o.shape[0]
+    tail = columns.shape[0] - split
 
     @pl.when(info[3] == 1)
     def _():
@@ -440,6 +451,14 @@
     @pl.when(info[3] == 0)
     def _():
         put(columns, 0, slice(0, split), right_o, right_t)
+
+    @pl.when(info[5] == 1)
+    def _():
+        put(columns, split, slice(own_o.shape[0] - tail, own_o.shape[0]), own_o, own_t)
+
+    @pl.when(info[5] == 0)
+    def _():
+        put(columns, split, slice(tail_o.shape[0] - tail, tail_o.shape[0]), tail_o, tail_t)
 
 
 def local_rings(traces, quality_mask, band_bins):
@@ -505,6 +524,7 @@
     shifts = jnp.array([(lag - LAGS // 2) * LAG_STEP for lag in range(LAGS)], i32)
     angles = TWO_PI / W * (band_bins[None, :] * shifts[:, None] % W).astype(F32)
     cosine, sine = jnp.cos(angles), jnp.sin(angles)
+    tail = 128
     per_core = n // 2
     owner = z // per_core == c
     from_right = (z - 1) % n // per_core == c
@@ -515,8 +535,8 @@
     first_start = other * block + jnp.where(from_right, 0, split)
     last_start = other * block + jnp.where(from_right, rest, 0)
 
-    def info(start, flag):
-        return jnp.stack([x, 1 - x, start, flag]).astype(i32)
+    def info(*places):
+        return jnp.stack([x, 1 - x, *places]).astype(i32)
 
     result, rows = first_call(
         info(first_start, from_right), cosine, sine, [white, white_t, far, far_t], r0 + l0,
@@ -530,11 +550,11 @@
     l1 = [left1, lax.ppermute(left1, "sub", swap)]
     result, rows = product_call(
         info(full * block, owner), rows, [white, white_t] + r1 + l1,
-        gather_full, block, scale, result, True,
+        gather_full, (block - tail,), scale, result, True,
     )
     return product_call(
-        info(last_start, from_right), rows, r0 + r2 + l2,
-        gather_last, split, scale, result, False,
+        info(last_start, from_right, full * block + block - tail, owner), rows,
+        r0 + r2 + l2 + [white, white_t] + l1, gather_last, (split, tail), scale, result, False,
     )[0]
 
 

time: 131 us -> 128 us (0.977)
  waiting for transfers between devices: 29 us -> 27 us
  Pallas kernels: 67 us -> 65.4 us
    ppermute x1, waiting for transfers between devices: 5.38 us -> 3.5 us  [local_rings(): right1 = lax.ppermute(right0, 'row', to_right)]
    pallas_call x2, Pallas kernels: 22.9 us -> 21.2 us  [product_call(): pl.pallas_call(functools.partial(product_kernel, gather, widths, scale, f...]
  transfers between devices with their start and end apart: 21 -> 21, of which waited for: 8 -> 8; matrix products, arithmetic and copies ran while one was open for 3% -> 3% of each run, Pallas kernels for 37% -> 36%
where the time goes in v4:
time: 128 us
  Pallas kernels  65.4 us (51%)
  starting transfers between devices  28.9 us (23%)
  waiting for transfers between devices  27 us (21%)
  other arithmetic  3.47 us (3%)
  local copies, waits for them, and re-layouts  2.65 us (2%)
    pallas_call x4, Pallas kernels, spectra_call(): pl.pallas_call(functools.partial(spectra_kernel, with_table, firsts, size...  33.8 us
    pallas_call x2, Pallas kernels, product_call(): pl.pallas_call(functools.partial(product_kernel, gather, widths, scale, f...  21.2 us
    ppermute x1, waiting for transfers between devices, local_rings(): far = lax.ppermute(white, 'col', swap)  13.1 us
    ppermute x4, starting transfers between devices, last_step(): lax.ppermute(part, axes, pairs(n - 2, move, cross))  11.4 us
    pallas_call x1, Pallas kernels, first_call(): pl.pallas_call(functools.partial(first_kernel, gather, scale, len(parts))...  9.84 us
    ppermute x3, starting transfers between devices, local_rings(): left = lax.ppermute(left, 'row', to_left)  9.11 us
    ppermute x3, waiting for transfers between devices, local_rings(): left = lax.ppermute(left, 'row', to_left)  6.67 us
    ppermute x1, waiting for transfers between devices, local_rings(): right1 = lax.ppermute(right0, 'row', to_right)  3.5 us
  transfers between devices with their start and end apart: 21, of which 8 were waited for; matrix products, arithmetic and copies ran while one was open for 3% of the time, Pallas kernels for 36%

profile of v4, /device:TPU:0, one launch (start us, length us, event | category | flops | bytes accessed | tf_op | source)
XLA Modules:
  0.0 128.0 jit_solution(11651645524439939508)
XLA Ops:
  0.1 0.7 copy-done.2
  0.7 8.5 %spectra.4 = (bf16[384,512]{1,0:T(8,128)(2,1)S(1)}, bf16[256,512]{1,0:T(8,128)(2,1)S(1)}, bf16[4096,256]{1,0:T(8,128)(2,1)S(1)}) custom-call(s32[3]{0:T(128)S(1)} %get-tuple-element.41.where_ref, s32[1,128]{1,0:T(1,128)S(1)} %bitcast.19, bf16[2,2560,4096]{2,1,0:T(8,128)(2,1)} %traces_ref.7), custom_call_target="tpu_custom_call" | custom-call | flops 1000 | bytes 1000 | tf_op jit(solution)/shard_map/spectra/pallas_call | solution.py:179
  9.2 3.1 %collective-permute-start = (bf16[384,512]{1,0:T(8,128)(2,1)S(1)}, bf16[384,512]{1,0:T(8,128)(2,1)S(1)}, u32[]{:S(2)}, u32[]{:S(2)}) collective-permute-start(bf16[384,512]{1,0:T(8,128)(2,1)S(1)} %get-tuple-element.22), channel_id=1, source_target_pairs={{0,4},{4,8},{8,12},{12,0},{1,5},{5,9},{9,13},{13,1},{2,6},{6,10},{... | collective-permute-start | bytes 1179656 | tf_op jit(solution)/shard_map/ppermute | solution.py:491
  12.3 2.1 %collective-permute-start.2 = (bf16[256,512]{1,0:T(8,128)(2,1)S(1)}, bf16[256,512]{1,0:T(8,128)(2,1)S(1)}, u32[]{:S(2)}, u32[]{:S(2)}) collective-permute-start(bf16[256,512]{1,0:T(8,128)(2,1)S(1)} %get-tuple-element.25), channel_id=1, source_target_pairs={{0,12},{4,0},{8,4},{12,8},{1,13},{5,1},{9,5},{13,9},{2,14},{6,2},{... | collective-permute-start | bytes 786440 | tf_op jit(solution)/shard_map/ppermute | solution.py:492
  14.4 8.5 %spectra.5 = (f32[384,512]{1,0:T(8,128)S(1)}, f32[256,512]{1,0:T(8,128)S(1)}) custom-call(s32[3]{0:T(128)S(1)} %get-tuple-element.42.where_ref, bf16[4096,256]{1,0:T(8,128)(2,1)S(1)} %get-tuple-element.23.bins_or_table, bf16[2,2560,4096]{2,1,0:T(8,128)(2,1)} %traces_ref.7), custom_call_target="tpu_custom_call" | custom-call | flops 1000 | bytes 1000 | tf_op jit(solution)/shard_map/spectra/pallas_call | solution.py:179
  22.8 1.5 %collective-permute-done = bf16[384,512]{1,0:T(8,128)(2,1)S(1)} collective-permute-done((bf16[384,512]{1,0:T(8,128)(2,1)S(1)}, bf16[384,512]{1,0:T(8,128)(2,1)S(1)}, u32[]{:S(2)}, u32[]{:S(2)}) %collective-permute-start) | collective-permute-done | bytes 393248 | tf_op jit(solution)/shard_map/ppermute | solution.py:491
  24.6 4.1 %collective-permute-done.2 = bf16[256,512]{1,0:T(8,128)(2,1)S(1)} collective-permute-done((bf16[256,512]{1,0:T(8,128)(2,1)S(1)}, bf16[256,512]{1,0:T(8,128)(2,1)S(1)}, u32[]{:S(2)}, u32[]{:S(2)}) %collective-permute-start.2) | collective-permute-done | bytes 262176 | tf_op jit(solution)/shard_map/ppermute | solution.py:492
  28.8 3.1 %collective-permute-start.4 = (bf16[256,512]{1,0:T(8,128)(2,1)S(1)}, bf16[256,512]{1,0:T(8,128)(2,1)S(1)}, u32[]{:S(2)}, u32[]{:S(2)}) collective-permute-start(bf16[256,512]{1,0:T(8,128)(2,1)S(1)} %add_convert_fusion.3), channel_id=1, source_target_pairs={{0,12},{4,0},{8,4},{12,8},{1,13},{5,1},{9,5},{13,9},{2,14},{6,2},{... | collective-permute-start | bytes 786440 | tf_op jit(solution)/shard_map/ppermute | solution.py:492
  31.9 8.5 %spectra.6 = (f32[384,512]{1,0:T(8,128)S(1)}, f32[256,512]{1,0:T(8,128)S(1)}) custom-call(s32[3]{0:T(128)S(1)} %pad_add_fusion.5.where_ref, bf16[4096,256]{1,0:T(8,128)(2,1)S(1)} %get-tuple-element.23.bins_or_table, bf16[2,2560,4096]{2,1,0:T(8,128)(2,1)} %traces_ref.7), custom_call_target="tpu_custom_call" | custom-call | flops 1000 | bytes 1000 | tf_op jit(solution)/shard_map/spectra/pallas_call | solution.py:179
  40.4 1.9 %add_convert_fusion = bf16[384,512]{1,0:T(8,128)(2,1)} fusion(f32[384,512]{1,0:T(8,128)S(1)} %get-tuple-element.28, bf16[384,512]{1,0:T(8,128)(2,1)} %collective-permute-done.1), kind=kLoop, calls=%fused_computation | loop fusion | flops 589824 | bytes 1572864 | tf_op jit(solution)/shard_map/convert_element_type | solution.py:494
  42.3 0.9 collective-permute-done.4
  43.2 3.9 %collective-permute-start.5 = (bf16[256,512]{1,0:T(8,128)(2,1)S(1)}, bf16[256,512]{1,0:T(8,128)(2,1)S(1)}, u32[]{:S(2)}, u32[]{:S(2)}) collective-permute-start(bf16[256,512]{1,0:T(8,128)(2,1)S(1)} %add_convert_fusion.2), channel_id=1, source_target_pairs={{0,12},{4,0},{8,4},{12,8},{1,13},{5,1},{9,5},{13,9},{2,14},{6,2},{... | collective-permute-start | bytes 786440 | tf_op jit(solution)/shard_map/ppermute | solution.py:492
  47.1 0.8 dynamic-slice_convert_fusion
  48.3 8.5 %spectra.7 = (f32[384,512]{1,0:T(8,128)S(1)}, f32[256,512]{1,0:T(8,128)S(1)}) custom-call(s32[3]{0:T(128)S(1)} %pad_add_fusion.6.where_ref, bf16[4096,256]{1,0:T(8,128)(2,1)S(1)} %get-tuple-element.23.bins_or_table, bf16[2,2560,4096]{2,1,0:T(8,128)(2,1)} %traces_ref.7), custom_call_target="tpu_custom_call" | custom-call | flops 1000 | bytes 1000 | tf_op jit(solution)/shard_map/spectra/pallas_call | solution.py:179
  56.7 1.7 %collective-permute-done.5.got = bf16[256,512]{1,0:T(8,128)(2,1)S(1)} collective-permute-done((bf16[256,512]{1,0:T(8,128)(2,1)S(1)}, bf16[256,512]{1,0:T(8,128)(2,1)S(1)}, u32[]{:S(2)}, u32[]{:S(2)}) %collective-permute-start.5) | collective-permute-done | bytes 262176 | tf_op jit(solution)/shard_map/ppermute | solution.py:492
  59.1 1.6 %collective-permute-start.7 = (bf16[640,512]{1,0:T(8,128)(2,1)S(1)}, bf16[640,512]{1,0:T(8,128)(2,1)S(1)}, u32[]{:S(2)}, u32[]{:S(2)}) collective-permute-start(bf16[640,512]{1,0:T(8,128)(2,1)S(1)} %pad_maximum_fusion.refs_0_.refs_2_.refs_8_), channel_id=1, source_target_pairs={{0,2},{2,0},{1,3},{3,1},{4,6},{6,4},{5,7},{7,5},{8,10},{10,8},{9,1... | collective-permute-start | bytes 1966088 | tf_op jit(solution)/shard_map/ppermute | solution.py:517
  60.6 1.7 %collective-permute-start.11 = (bf16[256,512]{1,0:T(8,128)(2,1)S(1)}, bf16[256,512]{1,0:T(8,128)(2,1)}, u32[]{:S(2)}, u32[]{:S(2)}) collective-permute-start(bf16[256,512]{1,0:T(8,128)(2,1)S(1)} %whiten.3), channel_id=1, source_target_pairs={{0,12},{4,0},{8,4},{12,8},{1,13},{5,1},{9,5},{13,9},{2,14},{6,2},{... | collective-permute-start | bytes 786440 | tf_op jit(solution)/shard_map/ppermute | solution.py:515
  62.6 13.1 %collective-permute-done.7.refs_2_ = bf16[640,512]{1,0:T(8,128)(2,1)S(1)} collective-permute-done((bf16[640,512]{1,0:T(8,128)(2,1)S(1)}, bf16[640,512]{1,0:T(8,128)(2,1)S(1)}, u32[]{:S(2)}, u32[]{:S(2)}) %collective-permute-start.7) | collective-permute-done | bytes 655392 | tf_op jit(solution)/shard_map/ppermute | solution.py:517
  75.8 1.3 %collective-permute-done.11.refs_6_ = bf16[256,512]{1,0:T(8,128)(2,1)} collective-permute-done((bf16[256,512]{1,0:T(8,128)(2,1)S(1)}, bf16[256,512]{1,0:T(8,128)(2,1)}, u32[]{:S(2)}, u32[]{:S(2)}) %collective-permute-start.11) | collective-permute-done | bytes 262176 | tf_op jit(solution)/shard_map/ppermute | solution.py:515
  77.1 0.5 collective-permute-start.10
  77.6 0.6 collective-permute-start.15
  78.2 0.9 collective-permute-done.12.refs_7_
  79.1 0.7 copy-done
  80.6 0.9 copy-done.1
  81.5 9.8 %turn_products.1 = (f32[4,1280,1280]{2,1,0:T(8,128)}, bf16[48,640,1024]{2,1,0:T(8,128)(2,1)}) custom-call(s32[4]{0:T(128)S(1)} %pad_add_fusion.2.info, f32[4,128]{1,0:T(4,128)S(1)} %get-tuple-element.40.cos_ref, f32[4,128]{1,0:T(4,128)S(1)} %get-tuple-element.39.sin_ref, bf16[640,512]{1,0:T(8,128)(2,1)S(1)} %pad_maximum_fusion.refs_0_.refs_2_.refs_8_, ...), custom_call_target="tpu_custom_call" | custom-call | flops 1000 | bytes 1000 | tf_op jit(solution)/shard_map/turn_products/pallas_call | solution.py:300
  91.5 3.5 %collective-permute-done.13.refs_4_ = bf16[384,512]{1,0:T(8,128)(2,1)S(1)} collective-permute-done((bf16[384,512]{1,0:T(8,128)(2,1)S(1)}, bf16[384,512]{1,0:T(8,128)(2,1)S(1)}, u32[]{:S(2)}, u32[]{:S(2)}) %collective-permute-start.13) | collective-permute-done | bytes 393248 | tf_op jit(solution)/shard_map/ppermute | solution.py:518
  95.0 1.3 %collective-permute-start.17 = (bf16[384,512]{1,0:T(8,128)(2,1)S(1)}, bf16[384,512]{1,0:T(8,128)(2,1)S(1)}, u32[]{:S(2)}, u32[]{:S(2)}) collective-permute-start(bf16[384,512]{1,0:T(8,128)(2,1)S(1)} %collective-permute-done.13.refs_4_), channel_id=1, source_target_pairs={{1,5},{5,9},{8,12},{12,0},{3,7},{7,11},{10,14},{14,2},{17,21},{21,... | collective-permute-start | bytes 1179656 | tf_op jit(solution)/shard_map/ppermute | solution.py:510
  96.3 4.4 %collective-permute-start.18 = (bf16[384,512]{1,0:T(8,128)(2,1)S(1)}, bf16[384,512]{1,0:T(8,128)(2,1)}, u32[]{:S(2)}, u32[]{:S(2)}) collective-permute-start(bf16[384,512]{1,0:T(8,128)(2,1)S(1)} %collective-permute-done.13.refs_4_), channel_id=1, source_target_pairs={{0,5},{4,9},{9,12},{13,0},{2,7},{6,11},{11,14},{15,2},{16,21},{20,... | collective-permute-start | bytes 1179656 | tf_op jit(solution)/shard_map/ppermute | solution.py:510
  100.7 1.4 %collective-permute-start.19 = (bf16[256,512]{1,0:T(8,128)(2,1)S(1)}, bf16[256,512]{1,0:T(8,128)(2,1)}, u32[]{:S(2)}, u32[]{:S(2)}) collective-permute-start(bf16[256,512]{1,0:T(8,128)(2,1)S(1)} %collective-permute-done.15.refs_6_.refs_10_), channel_id=1, source_target_pairs={{1,13},{5,1},{8,4},{12,8},{3,15},{7,3},{10,6},{14,10},{17,29},{21,... | collective-permute-start | bytes 786440 | tf_op jit(solution)/shard_map/ppermute | solution.py:510
  102.1 4.3 %collective-permute-start.20 = (bf16[256,512]{1,0:T(8,128)(2,1)S(1)}, bf16[256,512]{1,0:T(8,128)(2,1)}, u32[]{:S(2)}, u32[]{:S(2)}) collective-permute-start(bf16[256,512]{1,0:T(8,128)(2,1)S(1)} %collective-permute-done.15.refs_6_.refs_10_), channel_id=1, source_target_pairs={{0,13},{4,1},{9,4},{13,8},{2,15},{6,3},{11,6},{15,10},{16,29},{20,... | collective-permute-start | bytes 786440 | tf_op jit(solution)/shard_map/ppermute | solution.py:510
  106.5 11.1 %products.2 = (f32[4,1280,1280]{2,1,0:T(8,128)}, bf16[8,640,1024]{2,1,0:T(8,128)(2,1)S(1)}) custom-call(s32[4]{0:T(128)S(1)} %pad_add_fusion.refs_0_, bf16[48,640,1024]{2,1,0:T(8,128)(2,1)} %get-tuple-element.33.refs_1_, bf16[640,512]{1,0:T(8,128)(2,1)S(1)} %pad_maximum_fusion.refs_0_.refs_2_.refs_8_, ...), custom_call_target="tpu_custom_call", output_to_operand_aliasing={{0}: (8, {})} | custom-call | flops 1000 | bytes 1000 | tf_op jit(solution)/shard_map/products/pallas_call | solution.py:392
  117.7 10.1 %products.3 = f32[4,1280,1280]{2,1,0:T(8,128)} custom-call(s32[6]{0:T(128)S(1)} %stack.95.refs_0_, bf16[8,640,1024]{2,1,0:T(8,128)(2,1)S(1)} %get-tuple-element.37.refs_1_, bf16[384,512]{1,0:T(8,128)(2,1)S(1)} %collective-permute-done.9.refs_4_.refs_2_, ...), custom_call_target="tpu_custom_call", output_to_operand_aliasing={{}: (12, {})} | custom-call | flops 1000 | bytes 1000 | tf_op jit(solution)/shard_map/products/pallas_call | solution.py:392
  (46 shorter events, 2.7 us)
Async XLA Ops:
  0.1 0.7 copy-start.2
  9.2 15.1 %collective-permute-start = (bf16[384,512]{1,0:T(8,128)(2,1)S(1)}, bf16[384,512]{1,0:T(8,128)(2,1)S(1)}, u32[]{:S(2)}, u32[]{:S(2)}) collective-permute-start(bf16[384,512]{1,0:T(8,128)(2,1)S(1)} %get-tuple-element.22), channel_id=1, source_target_pairs={{0,4},{4,8},{8,12},{12,0},{1,5},{5,9},{9,13},{13,1},{2,6},{6,10},{... | collective-permute-start | bytes 1179656 | tf_op jit(solution)/shard_map/ppermute | solution.py:491
  12.3 16.4 %collective-permute-start.2 = (bf16[256,512]{1,0:T(8,128)(2,1)S(1)}, bf16[256,512]{1,0:T(8,128)(2,1)S(1)}, u32[]{:S(2)}, u32[]{:S(2)}) collective-permute-start(bf16[256,512]{1,0:T(8,128)(2,1)S(1)} %get-tuple-element.25), channel_id=1, source_target_pairs={{0,12},{4,0},{8,4},{12,8},{1,13},{5,1},{9,5},{13,9},{2,14},{6,2},{... | collective-permute-start | bytes 786440 | tf_op jit(solution)/shard_map/ppermute | solution.py:492
  24.4 15.9 %collective-permute-start.1 = (bf16[384,512]{1,0:T(8,128)(2,1)S(1)}, bf16[384,512]{1,0:T(8,128)(2,1)}, u32[]{:S(2)}, u32[]{:S(2)}) collective-permute-start(bf16[384,512]{1,0:T(8,128)(2,1)S(1)} %add_convert_fusion.1), channel_id=1, source_target_pairs={{0,4},{4,8},{8,12},{12,0},{1,5},{5,9},{9,13},{13,1},{2,6},{6,10},{... | collective-permute-start | bytes 1179656 | tf_op jit(solution)/shard_map/ppermute | solution.py:491
  28.8 14.4 %collective-permute-start.4 = (bf16[256,512]{1,0:T(8,128)(2,1)S(1)}, bf16[256,512]{1,0:T(8,128)(2,1)S(1)}, u32[]{:S(2)}, u32[]{:S(2)}) collective-permute-start(bf16[256,512]{1,0:T(8,128)(2,1)S(1)} %add_convert_fusion.3), channel_id=1, source_target_pairs={{0,12},{4,0},{8,4},{12,8},{1,13},{5,1},{9,5},{13,9},{2,14},{6,2},{... | collective-permute-start | bytes 786440 | tf_op jit(solution)/shard_map/ppermute | solution.py:492
  40.3 40.1 %copy-start.3 = (s32[128]{0:T(128)S(1)}, s32[128]{0:T(128)}, u32[]{:S(2)}) copy-start(s32[128]{0:T(128)} %param.6) | copy-start | bytes 1540
  40.4 40.1 %copy-start.4 = (s32[4]{0:T(128)S(1)}, s32[4]{0:T(128)}, u32[]{:S(2)}) copy-start(s32[4]{0:T(128)} %constant.125.clone) | copy-start | bytes 52
  42.3 16.4 %collective-permute-start.3 = (bf16[384,512]{1,0:T(8,128)(2,1)}, bf16[384,512]{1,0:T(8,128)(2,1)S(1)}, u32[]{:S(2)}, u32[]{:S(2)}) collective-permute-start(bf16[384,512]{1,0:T(8,128)(2,1)} %add_convert_fusion), channel_id=1, source_target_pairs={{0,4},{4,8},{8,12},{12,0},{1,5},{5,9},{9,13},{13,1},{2,6},{6,10},{... | collective-permute-start | bytes 1179656 | tf_op jit(solution)/shard_map/ppermute | solution.py:491
  43.2 15.2 %collective-permute-start.5 = (bf16[256,512]{1,0:T(8,128)(2,1)S(1)}, bf16[256,512]{1,0:T(8,128)(2,1)S(1)}, u32[]{:S(2)}, u32[]{:S(2)}) collective-permute-start(bf16[256,512]{1,0:T(8,128)(2,1)S(1)} %add_convert_fusion.2), channel_id=1, source_target_pairs={{0,12},{4,0},{8,4},{12,8},{1,13},{5,1},{9,5},{13,9},{2,14},{6,2},{... | collective-permute-start | bytes 786440 | tf_op jit(solution)/shard_map/ppermute | solution.py:492
  59.1 16.7 %collective-permute-start.7 = (bf16[640,512]{1,0:T(8,128)(2,1)S(1)}, bf16[640,512]{1,0:T(8,128)(2,1)S(1)}, u32[]{:S(2)}, u32[]{:S(2)}) collective-permute-start(bf16[640,512]{1,0:T(8,128)(2,1)S(1)} %pad_maximum_fusion.refs_0_.refs_2_.refs_8_), channel_id=1, source_target_pairs={{0,2},{2,0},{1,3},{3,1},{4,6},{6,4},{5,7},{7,5},{8,10},{10,8},{9,1... | collective-permute-start | bytes 1966088 | tf_op jit(solution)/shard_map/ppermute | solution.py:517
  60.6 16.5 %collective-permute-start.11 = (bf16[256,512]{1,0:T(8,128)(2,1)S(1)}, bf16[256,512]{1,0:T(8,128)(2,1)}, u32[]{:S(2)}, u32[]{:S(2)}) collective-permute-start(bf16[256,512]{1,0:T(8,128)(2,1)S(1)} %whiten.3), channel_id=1, source_target_pairs={{0,12},{4,0},{8,4},{12,8},{1,13},{5,1},{9,5},{13,9},{2,14},{6,2},{... | collective-permute-start | bytes 786440 | tf_op jit(solution)/shard_map/ppermute | solution.py:515
  62.3 14.8 %collective-permute-start.9 = (bf16[384,512]{1,0:T(8,128)(2,1)S(1)}, bf16[384,512]{1,0:T(8,128)(2,1)S(1)}, u32[]{:S(2)}, u32[]{:S(2)}) collective-permute-start(bf16[384,512]{1,0:T(8,128)(2,1)S(1)} %whiten.2), channel_id=1, source_target_pairs={{0,4},{4,8},{8,12},{12,0},{1,5},{5,9},{9,13},{13,1},{2,6},{6,10},{... | collective-permute-start | bytes 1179656 | tf_op jit(solution)/shard_map/ppermute | solution.py:514
  62.6 17.9 %collective-permute-start.6 = (bf16[640,512]{1,0:T(8,128)(2,1)S(1)}, bf16[640,512]{1,0:T(8,128)(2,1)S(1)}, u32[]{:S(2)}, u32[]{:S(2)}) collective-permute-start(bf16[640,512]{1,0:T(8,128)(2,1)S(1)} %pad_maximum_fusion.refs_0_.refs_2_.refs_8_), channel_id=1, source_target_pairs={{0,1},{1,0},{2,3},{3,2},{4,5},{5,4},{6,7},{7,6},{8,9},{9,8},{10,11... | collective-permute-start | bytes 1966088 | tf_op jit(solution)/shard_map/ppermute | solution.py:516
  75.8 4.8 %collective-permute-start.8 = (bf16[640,512]{1,0:T(8,128)(2,1)S(1)}, bf16[640,512]{1,0:T(8,128)(2,1)}, u32[]{:S(2)}, u32[]{:S(2)}) collective-permute-start(bf16[640,512]{1,0:T(8,128)(2,1)S(1)} %collective-permute-done.7.refs_2_), channel_id=1, source_target_pairs={{0,1},{1,0},{2,3},{3,2},{4,5},{5,4},{6,7},{7,6},{8,9},{9,8},{10,11... | collective-permute-start | bytes 1966088 | tf_op jit(solution)/shard_map/ppermute | solution.py:522
  77.1 2.0 %collective-permute-start.12 = (bf16[256,512]{1,0:T(8,128)(2,1)}, bf16[256,512]{1,0:T(8,128)(2,1)S(1)}, u32[]{:S(2)}, u32[]{:S(2)}) collective-permute-start(bf16[256,512]{1,0:T(8,128)(2,1)} %collective-permute-done.11.refs_6_), channel_id=1, source_target_pairs={{0,1},{1,0},{2,3},{3,2},{4,5},{5,4},{6,7},{7,6},{8,9},{9,8},{10,11... | collective-permute-start | bytes 786440 | tf_op jit(solution)/shard_map/ppermute | solution.py:521
  77.1 3.5 %collective-permute-start.10 = (bf16[384,512]{1,0:T(8,128)(2,1)S(1)}, bf16[384,512]{1,0:T(8,128)(2,1)S(1)}, u32[]{:S(2)}, u32[]{:S(2)}) collective-permute-start(bf16[384,512]{1,0:T(8,128)(2,1)S(1)} %collective-permute-done.9.refs_4_.refs_2_), channel_id=1, source_target_pairs={{0,1},{1,0},{2,3},{3,2},{4,5},{5,4},{6,7},{7,6},{8,9},{9,8},{10,11... | collective-permute-start | bytes 1179656 | tf_op jit(solution)/shard_map/ppermute | solution.py:520
  77.6 13.8 %collective-permute-start.15 = (bf16[256,512]{1,0:T(8,128)(2,1)}, bf16[256,512]{1,0:T(8,128)(2,1)S(1)}, u32[]{:S(2)}, u32[]{:S(2)}) collective-permute-start(bf16[256,512]{1,0:T(8,128)(2,1)} %collective-permute-done.11.refs_6_), channel_id=1, source_target_pairs={{0,12},{4,0},{8,4},{12,8},{1,13},{5,1},{9,5},{13,9},{2,14},{6,2},{... | collective-permute-start | bytes 786440 | tf_op jit(solution)/shard_map/ppermute | solution.py:519
  79.1 0.7 copy-start
  79.8 15.1 %collective-permute-start.13 = (bf16[384,512]{1,0:T(8,128)(2,1)S(1)}, bf16[384,512]{1,0:T(8,128)(2,1)S(1)}, u32[]{:S(2)}, u32[]{:S(2)}) collective-permute-start(bf16[384,512]{1,0:T(8,128)(2,1)S(1)} %collective-permute-done.9.refs_4_.refs_2_), channel_id=1, source_target_pairs={{0,4},{4,8},{8,12},{12,0},{1,5},{5,9},{9,13},{13,1},{2,6},{6,10},{... | collective-permute-start | bytes 1179656 | tf_op jit(solution)/shard_map/ppermute | solution.py:518
  80.6 1.0 copy-start.1
  91.4 10.7 %collective-permute-start.16 = (bf16[256,512]{1,0:T(8,128)(2,1)S(1)}, bf16[256,512]{1,0:T(8,128)(2,1)S(1)}, u32[]{:S(2)}, u32[]{:S(2)}) collective-permute-start(bf16[256,512]{1,0:T(8,128)(2,1)S(1)} %collective-permute-done.15.refs_6_.refs_10_), channel_id=1, source_target_pairs={{0,1},{1,0},{2,3},{3,2},{4,5},{5,4},{6,7},{7,6},{8,9},{9,8},{10,11... | collective-permute-start | bytes 786440 | tf_op jit(solution)/shard_map/ppermute | solution.py:550
  95.0 11.6 %collective-permute-start.14 = (bf16[384,512]{1,0:T(8,128)(2,1)S(1)}, bf16[384,512]{1,0:T(8,128)(2,1)}, u32[]{:S(2)}, u32[]{:S(2)}) collective-permute-start(bf16[384,512]{1,0:T(8,128)(2,1)S(1)} %collective-permute-done.13.refs_4_), channel_id=1, source_target_pairs={{0,1},{1,0},{2,3},{3,2},{4,5},{5,4},{6,7},{7,6},{8,9},{9,8},{10,11... | collective-permute-start | bytes 1179656 | tf_op jit(solution)/shard_map/ppermute | solution.py:549
  95.0 22.7 %collective-permute-start.17 = (bf16[384,512]{1,0:T(8,128)(2,1)S(1)}, bf16[384,512]{1,0:T(8,128)(2,1)S(1)}, u32[]{:S(2)}, u32[]{:S(2)}) collective-permute-start(bf16[384,512]{1,0:T(8,128)(2,1)S(1)} %collective-permute-done.13.refs_4_), channel_id=1, source_target_pairs={{1,5},{5,9},{8,12},{12,0},{3,7},{7,11},{10,14},{14,2},{17,21},{21,... | collective-permute-start | bytes 1179656 | tf_op jit(solution)/shard_map/ppermute | solution.py:510
  96.3 21.4 %collective-permute-start.18 = (bf16[384,512]{1,0:T(8,128)(2,1)S(1)}, bf16[384,512]{1,0:T(8,128)(2,1)}, u32[]{:S(2)}, u32[]{:S(2)}) collective-permute-start(bf16[384,512]{1,0:T(8,128)(2,1)S(1)} %collective-permute-done.13.refs_4_), channel_id=1, source_target_pairs={{0,5},{4,9},{9,12},{13,0},{2,7},{6,11},{11,14},{15,2},{16,21},{20,... | collective-permute-start | bytes 1179656 | tf_op jit(solution)/shard_map/ppermute | solution.py:510
  100.7 16.9 %collective-permute-start.19 = (bf16[256,512]{1,0:T(8,128)(2,1)S(1)}, bf16[256,512]{1,0:T(8,128)(2,1)}, u32[]{:S(2)}, u32[]{:S(2)}) collective-permute-start(bf16[256,512]{1,0:T(8,128)(2,1)S(1)} %collective-permute-done.15.refs_6_.refs_10_), channel_id=1, source_target_pairs={{1,13},{5,1},{8,4},{12,8},{3,15},{7,3},{10,6},{14,10},{17,29},{21,... | collective-permute-start | bytes 786440 | tf_op jit(solution)/shard_map/ppermute | solution.py:510
  102.1 15.6 %collective-permute-start.20 = (bf16[256,512]{1,0:T(8,128)(2,1)S(1)}, bf16[256,512]{1,0:T(8,128)(2,1)}, u32[]{:S(2)}, u32[]{:S(2)}) collective-permute-start(bf16[256,512]{1,0:T(8,128)(2,1)S(1)} %collective-permute-done.15.refs_6_.refs_10_), channel_id=1, source_target_pairs={{0,13},{4,1},{9,4},{13,8},{2,15},{6,3},{11,6},{15,10},{16,29},{20,... | collective-permute-start | bytes 786440 | tf_op jit(solution)/shard_map/ppermute | solution.py:510

commit v5 on v4

--- a/solution.py
+++ b/solution.py
@@ -20,7 +20,8 @@
 SMALL_VMEM = 8 * MIB
 PRODUCT_VMEM = 16 * MIB
 SMALL = pl.CostEstimate(flops=1000, bytes_accessed=1000, transcendentals=0)
-AHEAD = 3
+TILES = 3
+AHEAD = 5
 ROWS_KEPT = 48
 FINE = 64
 
@@ -222,7 +223,7 @@
 
 def place_tile(tiles, sems, out, index, sides, starts):
     block = tiles.shape[1]
-    slot = index % 2
+    slot = index % tiles.shape[0]
     first = pl.multiple_of(sides[index // LAGS] * block, 128)
     return [
         pltpu.make_async_copy(
@@ -354,23 +355,23 @@
 
             bring(step).wait()
 
-        @pl.when(step >= 2)
+        @pl.when(step >= TILES)
         def _():
-            end_placing(step - 2)
-
-        tiles[lax.rem(step, 2)] = times_columns(scale, held[step], columns[...])
+            end_placing(step - TILES)
+
+        tiles[lax.rem(step, TILES)] = times_columns(scale, held[step], columns[...])
         start_placing(step)
 
     if fetch:
         pl.loop(0, steps)(run)
     else:
         for step in range(steps):
-            if step >= 2:
-                end_placing(step - 2)
-            tiles[step % 2] = times_columns(scale, held[step], columns[...])
+            if step >= TILES:
+                end_placing(step - TILES)
+            tiles[step % TILES] = times_columns(scale, held[step], columns[...])
             start_placing(step)
-    end_placing(steps - 2)
-    end_placing(steps - 1)
+    for step in range(steps - TILES, steps):
+        end_placing(step)
 
 
 def product_call(info, rows, parts, gather, widths, scale, base, fetch):
@@ -382,8 +383,8 @@
     out_specs = [hbm]
     scratch = [
         pltpu.VMEM((width, depth), BF16),
-        pltpu.VMEM((2, block, width), F32),
-        pltpu.SemaphoreType.DMA((2, len(widths))),
+        pltpu.VMEM((TILES, block, width), F32),
+        pltpu.SemaphoreType.DMA((TILES, len(widths))),
     ]
     if fetch:
         out_shape.append(jax.ShapeDtypeStruct((2 * LAGS, block, depth), rows.dtype))

time: 128 us -> 127 us (level)
  no operation moved by 1% of the time
where the time goes in v5:
time: 127 us
  Pallas kernels  64.2 us (51%)
  starting transfers between devices  28.9 us (23%)
  waiting for transfers between devices  27 us (21%)
  other arithmetic  3.47 us (3%)
  local copies, waits for them, and re-layouts  2.65 us (2%)
    pallas_call x4, Pallas kernels, spectra_call(): pl.pallas_call(functools.partial(spectra_kernel, with_table, firsts, size...  33.8 us
    pallas_call x2, Pallas kernels, product_call(): pl.pallas_call(functools.partial(product_kernel, gather, widths, scale, f...  20 us
    ppermute x1, waiting for transfers between devices, local_rings(): far = lax.ppermute(white, 'col', swap)  13.1 us
    ppermute x4, starting transfers between devices, last_step(): lax.ppermute(part, axes, pairs(n - 2, move, cross))  11.4 us
    pallas_call x1, Pallas kernels, first_call(): pl.pallas_call(functools.partial(first_kernel, gather, scale, len(parts))...  9.84 us
    ppermute x3, starting transfers between devices, local_rings(): left = lax.ppermute(left, 'row', to_left)  9.11 us
    ppermute x3, waiting for transfers between devices, local_rings(): left = lax.ppermute(left, 'row', to_left)  6.67 us
    ppermute x1, waiting for transfers between devices, local_rings(): right1 = lax.ppermute(right0, 'row', to_right)  3.5 us
  transfers between devices with their start and end apart: 21, of which 8 were waited for; matrix products, arithmetic and copies ran while one was open for 3% of the time, Pallas kernels for 36%

profile of v5, /device:TPU:0, one launch (start us, length us, event | category | flops | bytes accessed | tf_op | source)
XLA Modules:
  0.0 126.7 jit_solution(16004472584871431405)
XLA Ops:
  0.1 0.7 copy-done.2
  0.7 8.5 %spectra.4 = (bf16[384,512]{1,0:T(8,128)(2,1)S(1)}, bf16[256,512]{1,0:T(8,128)(2,1)S(1)}, bf16[4096,256]{1,0:T(8,128)(2,1)S(1)}) custom-call(s32[3]{0:T(128)S(1)} %get-tuple-element.41.where_ref, s32[1,128]{1,0:T(1,128)S(1)} %bitcast.19, bf16[2,2560,4096]{2,1,0:T(8,128)(2,1)} %traces_ref.7), custom_call_target="tpu_custom_call" | custom-call | flops 1000 | bytes 1000 | tf_op jit(solution)/shard_map/spectra/pallas_call | solution.py:180
  9.2 3.1 %collective-permute-start = (bf16[384,512]{1,0:T(8,128)(2,1)S(1)}, bf16[384,512]{1,0:T(8,128)(2,1)S(1)}, u32[]{:S(2)}, u32[]{:S(2)}) collective-permute-start(bf16[384,512]{1,0:T(8,128)(2,1)S(1)} %get-tuple-element.22), channel_id=1, source_target_pairs={{0,4},{4,8},{8,12},{12,0},{1,5},{5,9},{9,13},{13,1},{2,6},{6,10},{... | collective-permute-start | bytes 1179656 | tf_op jit(solution)/shard_map/ppermute | solution.py:492
  12.3 2.1 %collective-permute-start.2 = (bf16[256,512]{1,0:T(8,128)(2,1)S(1)}, bf16[256,512]{1,0:T(8,128)(2,1)S(1)}, u32[]{:S(2)}, u32[]{:S(2)}) collective-permute-start(bf16[256,512]{1,0:T(8,128)(2,1)S(1)} %get-tuple-element.25), channel_id=1, source_target_pairs={{0,12},{4,0},{8,4},{12,8},{1,13},{5,1},{9,5},{13,9},{2,14},{6,2},{... | collective-permute-start | bytes 786440 | tf_op jit(solution)/shard_map/ppermute | solution.py:493
  14.4 8.5 %spectra.5 = (f32[384,512]{1,0:T(8,128)S(1)}, f32[256,512]{1,0:T(8,128)S(1)}) custom-call(s32[3]{0:T(128)S(1)} %get-tuple-element.42.where_ref, bf16[4096,256]{1,0:T(8,128)(2,1)S(1)} %get-tuple-element.23.bins_or_table, bf16[2,2560,4096]{2,1,0:T(8,128)(2,1)} %traces_ref.7), custom_call_target="tpu_custom_call" | custom-call | flops 1000 | bytes 1000 | tf_op jit(solution)/shard_map/spectra/pallas_call | solution.py:180
  22.8 1.5 %collective-permute-done = bf16[384,512]{1,0:T(8,128)(2,1)S(1)} collective-permute-done((bf16[384,512]{1,0:T(8,128)(2,1)S(1)}, bf16[384,512]{1,0:T(8,128)(2,1)S(1)}, u32[]{:S(2)}, u32[]{:S(2)}) %collective-permute-start) | collective-permute-done | bytes 393248 | tf_op jit(solution)/shard_map/ppermute | solution.py:492
  24.6 4.1 %collective-permute-done.2 = bf16[256,512]{1,0:T(8,128)(2,1)S(1)} collective-permute-done((bf16[256,512]{1,0:T(8,128)(2,1)S(1)}, bf16[256,512]{1,0:T(8,128)(2,1)S(1)}, u32[]{:S(2)}, u32[]{:S(2)}) %collective-permute-start.2) | collective-permute-done | bytes 262176 | tf_op jit(solution)/shard_map/ppermute | solution.py:493
  28.8 3.1 %collective-permute-start.4 = (bf16[256,512]{1,0:T(8,128)(2,1)S(1)}, bf16[256,512]{1,0:T(8,128)(2,1)S(1)}, u32[]{:S(2)}, u32[]{:S(2)}) collective-permute-start(bf16[256,512]{1,0:T(8,128)(2,1)S(1)} %add_convert_fusion.3), channel_id=1, source_target_pairs={{0,12},{4,0},{8,4},{12,8},{1,13},{5,1},{9,5},{13,9},{2,14},{6,2},{... | collective-permute-start | bytes 786440 | tf_op jit(solution)/shard_map/ppermute | solution.py:493
  31.9 8.5 %spectra.6 = (f32[384,512]{1,0:T(8,128)S(1)}, f32[256,512]{1,0:T(8,128)S(1)}) custom-call(s32[3]{0:T(128)S(1)} %pad_add_fusion.5.where_ref, bf16[4096,256]{1,0:T(8,128)(2,1)S(1)} %get-tuple-element.23.bins_or_table, bf16[2,2560,4096]{2,1,0:T(8,128)(2,1)} %traces_ref.7), custom_call_target="tpu_custom_call" | custom-call | flops 1000 | bytes 1000 | tf_op jit(solution)/shard_map/spectra/pallas_call | solution.py:180
  40.4 1.9 %add_convert_fusion = bf16[384,512]{1,0:T(8,128)(2,1)} fusion(f32[384,512]{1,0:T(8,128)S(1)} %get-tuple-element.28, bf16[384,512]{1,0:T(8,128)(2,1)} %collective-permute-done.1), kind=kLoop, calls=%fused_computation | loop fusion | flops 589824 | bytes 1572864 | tf_op jit(solution)/shard_map/convert_element_type | solution.py:495
  42.3 0.9 collective-permute-done.4
  43.2 3.9 %collective-permute-start.5 = (bf16[256,512]{1,0:T(8,128)(2,1)S(1)}, bf16[256,512]{1,0:T(8,128)(2,1)S(1)}, u32[]{:S(2)}, u32[]{:S(2)}) collective-permute-start(bf16[256,512]{1,0:T(8,128)(2,1)S(1)} %add_convert_fusion.2), channel_id=1, source_target_pairs={{0,12},{4,0},{8,4},{12,8},{1,13},{5,1},{9,5},{13,9},{2,14},{6,2},{... | collective-permute-start | bytes 786440 | tf_op jit(solution)/shard_map/ppermute | solution.py:493
  47.1 0.8 dynamic-slice_convert_fusion
  48.3 8.5 %spectra.7 = (f32[384,512]{1,0:T(8,128)S(1)}, f32[256,512]{1,0:T(8,128)S(1)}) custom-call(s32[3]{0:T(128)S(1)} %pad_add_fusion.6.where_ref, bf16[4096,256]{1,0:T(8,128)(2,1)S(1)} %get-tuple-element.23.bins_or_table, bf16[2,2560,4096]{2,1,0:T(8,128)(2,1)} %traces_ref.7), custom_call_target="tpu_custom_call" | custom-call | flops 1000 | bytes 1000 | tf_op jit(solution)/shard_map/spectra/pallas_call | solution.py:180
  56.7 1.7 %collective-permute-done.5.got = bf16[256,512]{1,0:T(8,128)(2,1)S(1)} collective-permute-done((bf16[256,512]{1,0:T(8,128)(2,1)S(1)}, bf16[256,512]{1,0:T(8,128)(2,1)S(1)}, u32[]{:S(2)}, u32[]{:S(2)}) %collective-permute-start.5) | collective-permute-done | bytes 262176 | tf_op jit(solution)/shard_map/ppermute | solution.py:493
  59.1 1.6 %collective-permute-start.7 = (bf16[640,512]{1,0:T(8,128)(2,1)S(1)}, bf16[640,512]{1,0:T(8,128)(2,1)S(1)}, u32[]{:S(2)}, u32[]{:S(2)}) collective-permute-start(bf16[640,512]{1,0:T(8,128)(2,1)S(1)} %pad_maximum_fusion.refs_0_.refs_2_.refs_8_), channel_id=1, source_target_pairs={{0,2},{2,0},{1,3},{3,1},{4,6},{6,4},{5,7},{7,5},{8,10},{10,8},{9,1... | collective-permute-start | bytes 1966088 | tf_op jit(solution)/shard_map/ppermute | solution.py:518
  60.6 1.7 %collective-permute-start.11 = (bf16[256,512]{1,0:T(8,128)(2,1)S(1)}, bf16[256,512]{1,0:T(8,128)(2,1)}, u32[]{:S(2)}, u32[]{:S(2)}) collective-permute-start(bf16[256,512]{1,0:T(8,128)(2,1)S(1)} %whiten.3), channel_id=1, source_target_pairs={{0,12},{4,0},{8,4},{12,8},{1,13},{5,1},{9,5},{13,9},{2,14},{6,2},{... | collective-permute-start | bytes 786440 | tf_op jit(solution)/shard_map/ppermute | solution.py:516
  62.6 13.1 %collective-permute-done.7.refs_2_ = bf16[640,512]{1,0:T(8,128)(2,1)S(1)} collective-permute-done((bf16[640,512]{1,0:T(8,128)(2,1)S(1)}, bf16[640,512]{1,0:T(8,128)(2,1)S(1)}, u32[]{:S(2)}, u32[]{:S(2)}) %collective-permute-start.7) | collective-permute-done | bytes 655392 | tf_op jit(solution)/shard_map/ppermute | solution.py:518
  75.8 1.3 %collective-permute-done.11.refs_6_ = bf16[256,512]{1,0:T(8,128)(2,1)} collective-permute-done((bf16[256,512]{1,0:T(8,128)(2,1)S(1)}, bf16[256,512]{1,0:T(8,128)(2,1)}, u32[]{:S(2)}, u32[]{:S(2)}) %collective-permute-start.11) | collective-permute-done | bytes 262176 | tf_op jit(solution)/shard_map/ppermute | solution.py:516
  77.1 0.5 collective-permute-start.10
  77.6 0.6 collective-permute-start.15
  78.2 0.9 collective-permute-done.12.refs_7_
  79.1 0.7 copy-done
  80.6 0.9 copy-done.1
  81.5 9.8 %turn_products.1 = (f32[4,1280,1280]{2,1,0:T(8,128)}, bf16[48,640,1024]{2,1,0:T(8,128)(2,1)}) custom-call(s32[4]{0:T(128)S(1)} %pad_add_fusion.2.info, f32[4,128]{1,0:T(4,128)S(1)} %get-tuple-element.40.cos_ref, f32[4,128]{1,0:T(4,128)S(1)} %get-tuple-element.39.sin_ref, bf16[640,512]{1,0:T(8,128)(2,1)S(1)} %pad_maximum_fusion.refs_0_.refs_2_.refs_8_, ...), custom_call_target="tpu_custom_call" | custom-call | flops 1000 | bytes 1000 | tf_op jit(solution)/shard_map/turn_products/pallas_call | solution.py:301
  91.5 3.5 %collective-permute-done.13.refs_4_ = bf16[384,512]{1,0:T(8,128)(2,1)S(1)} collective-permute-done((bf16[384,512]{1,0:T(8,128)(2,1)S(1)}, bf16[384,512]{1,0:T(8,128)(2,1)S(1)}, u32[]{:S(2)}, u32[]{:S(2)}) %collective-permute-start.13) | collective-permute-done | bytes 393248 | tf_op jit(solution)/shard_map/ppermute | solution.py:519
  95.0 1.3 %collective-permute-start.17 = (bf16[384,512]{1,0:T(8,128)(2,1)S(1)}, bf16[384,512]{1,0:T(8,128)(2,1)S(1)}, u32[]{:S(2)}, u32[]{:S(2)}) collective-permute-start(bf16[384,512]{1,0:T(8,128)(2,1)S(1)} %collective-permute-done.13.refs_4_), channel_id=1, source_target_pairs={{1,5},{5,9},{8,12},{12,0},{3,7},{7,11},{10,14},{14,2},{17,21},{21,... | collective-permute-start | bytes 1179656 | tf_op jit(solution)/shard_map/ppermute | solution.py:511
  96.3 4.4 %collective-permute-start.18 = (bf16[384,512]{1,0:T(8,128)(2,1)S(1)}, bf16[384,512]{1,0:T(8,128)(2,1)}, u32[]{:S(2)}, u32[]{:S(2)}) collective-permute-start(bf16[384,512]{1,0:T(8,128)(2,1)S(1)} %collective-permute-done.13.refs_4_), channel_id=1, source_target_pairs={{0,5},{4,9},{9,12},{13,0},{2,7},{6,11},{11,14},{15,2},{16,21},{20,... | collective-permute-start | bytes 1179656 | tf_op jit(solution)/shard_map/ppermute | solution.py:511
  100.7 1.4 %collective-permute-start.19 = (bf16[256,512]{1,0:T(8,128)(2,1)S(1)}, bf16[256,512]{1,0:T(8,128)(2,1)}, u32[]{:S(2)}, u32[]{:S(2)}) collective-permute-start(bf16[256,512]{1,0:T(8,128)(2,1)S(1)} %collective-permute-done.15.refs_6_.refs_10_), channel_id=1, source_target_pairs={{1,13},{5,1},{8,4},{12,8},{3,15},{7,3},{10,6},{14,10},{17,29},{21,... | collective-permute-start | bytes 786440 | tf_op jit(solution)/shard_map/ppermute | solution.py:511
  102.1 4.3 %collective-permute-start.20 = (bf16[256,512]{1,0:T(8,128)(2,1)S(1)}, bf16[256,512]{1,0:T(8,128)(2,1)}, u32[]{:S(2)}, u32[]{:S(2)}) collective-permute-start(bf16[256,512]{1,0:T(8,128)(2,1)S(1)} %collective-permute-done.15.refs_6_.refs_10_), channel_id=1, source_target_pairs={{0,13},{4,1},{9,4},{13,8},{2,15},{6,3},{11,6},{15,10},{16,29},{20,... | collective-permute-start | bytes 786440 | tf_op jit(solution)/shard_map/ppermute | solution.py:511
  106.5 10.7 %products.2 = (f32[4,1280,1280]{2,1,0:T(8,128)}, bf16[8,640,1024]{2,1,0:T(8,128)(2,1)S(1)}) custom-call(s32[4]{0:T(128)S(1)} %pad_add_fusion.refs_0_, bf16[48,640,1024]{2,1,0:T(8,128)(2,1)} %get-tuple-element.33.refs_1_, bf16[640,512]{1,0:T(8,128)(2,1)S(1)} %pad_maximum_fusion.refs_0_.refs_2_.refs_8_, ...), custom_call_target="tpu_custom_call", output_to_operand_aliasing={{0}: (8, {})} | custom-call | flops 1000 | bytes 1000 | tf_op jit(solution)/shard_map/products/pallas_call | solution.py:393
  117.3 9.3 %products.3 = f32[4,1280,1280]{2,1,0:T(8,128)} custom-call(s32[6]{0:T(128)S(1)} %stack.95.refs_0_, bf16[8,640,1024]{2,1,0:T(8,128)(2,1)S(1)} %get-tuple-element.37.refs_1_, bf16[384,512]{1,0:T(8,128)(2,1)S(1)} %collective-permute-done.9.refs_4_.refs_2_, ...), custom_call_target="tpu_custom_call", output_to_operand_aliasing={{}: (12, {})} | custom-call | flops 1000 | bytes 1000 | tf_op jit(solution)/shard_map/products/pallas_call | solution.py:393
  (46 shorter events, 2.7 us)
Async XLA Ops:
  0.1 0.7 copy-start.2
  9.2 15.1 %collective-permute-start = (bf16[384,512]{1,0:T(8,128)(2,1)S(1)}, bf16[384,512]{1,0:T(8,128)(2,1)S(1)}, u32[]{:S(2)}, u32[]{:S(2)}) collective-permute-start(bf16[384,512]{1,0:T(8,128)(2,1)S(1)} %get-tuple-element.22), channel_id=1, source_target_pairs={{0,4},{4,8},{8,12},{12,0},{1,5},{5,9},{9,13},{13,1},{2,6},{6,10},{... | collective-permute-start | bytes 1179656 | tf_op jit(solution)/shard_map/ppermute | solution.py:492
  12.3 16.4 %collective-permute-start.2 = (bf16[256,512]{1,0:T(8,128)(2,1)S(1)}, bf16[256,512]{1,0:T(8,128)(2,1)S(1)}, u32[]{:S(2)}, u32[]{:S(2)}) collective-permute-start(bf16[256,512]{1,0:T(8,128)(2,1)S(1)} %get-tuple-element.25), channel_id=1, source_target_pairs={{0,12},{4,0},{8,4},{12,8},{1,13},{5,1},{9,5},{13,9},{2,14},{6,2},{... | collective-permute-start | bytes 786440 | tf_op jit(solution)/shard_map/ppermute | solution.py:493
  24.4 15.9 %collective-permute-start.1 = (bf16[384,512]{1,0:T(8,128)(2,1)S(1)}, bf16[384,512]{1,0:T(8,128)(2,1)}, u32[]{:S(2)}, u32[]{:S(2)}) collective-permute-start(bf16[384,512]{1,0:T(8,128)(2,1)S(1)} %add_convert_fusion.1), channel_id=1, source_target_pairs={{0,4},{4,8},{8,12},{12,0},{1,5},{5,9},{9,13},{13,1},{2,6},{6,10},{... | collective-permute-start | bytes 1179656 | tf_op jit(solution)/shard_map/ppermute | solution.py:492
  28.8 14.4 %collective-permute-start.4 = (bf16[256,512]{1,0:T(8,128)(2,1)S(1)}, bf16[256,512]{1,0:T(8,128)(2,1)S(1)}, u32[]{:S(2)}, u32[]{:S(2)}) collective-permute-start(bf16[256,512]{1,0:T(8,128)(2,1)S(1)} %add_convert_fusion.3), channel_id=1, source_target_pairs={{0,12},{4,0},{8,4},{12,8},{1,13},{5,1},{9,5},{13,9},{2,14},{6,2},{... | collective-permute-start | bytes 786440 | tf_op jit(solution)/shard_map/ppermute | solution.py:493
  40.3 40.1 %copy-start.3 = (s32[128]{0:T(128)S(1)}, s32[128]{0:T(128)}, u32[]{:S(2)}) copy-start(s32[128]{0:T(128)} %param.6) | copy-start | bytes 1540
  40.4 40.1 %copy-start.4 = (s32[4]{0:T(128)S(1)}, s32[4]{0:T(128)}, u32[]{:S(2)}) copy-start(s32[4]{0:T(128)} %constant.125.clone) | copy-start | bytes 52
  42.3 16.4 %collective-permute-start.3 = (bf16[384,512]{1,0:T(8,128)(2,1)}, bf16[384,512]{1,0:T(8,128)(2,1)S(1)}, u32[]{:S(2)}, u32[]{:S(2)}) collective-permute-start(bf16[384,512]{1,0:T(8,128)(2,1)} %add_convert_fusion), channel_id=1, source_target_pairs={{0,4},{4,8},{8,12},{12,0},{1,5},{5,9},{9,13},{13,1},{2,6},{6,10},{... | collective-permute-start | bytes 1179656 | tf_op jit(solution)/shard_map/ppermute | solution.py:492
  43.2 15.2 %collective-permute-start.5 = (bf16[256,512]{1,0:T(8,128)(2,1)S(1)}, bf16[256,512]{1,0:T(8,128)(2,1)S(1)}, u32[]{:S(2)}, u32[]{:S(2)}) collective-permute-start(bf16[256,512]{1,0:T(8,128)(2,1)S(1)} %add_convert_fusion.2), channel_id=1, source_target_pairs={{0,12},{4,0},{8,4},{12,8},{1,13},{5,1},{9,5},{13,9},{2,14},{6,2},{... | collective-permute-start | bytes 786440 | tf_op jit(solution)/shard_map/ppermute | solution.py:493
  59.1 16.7 %collective-permute-start.7 = (bf16[640,512]{1,0:T(8,128)(2,1)S(1)}, bf16[640,512]{1,0:T(8,128)(2,1)S(1)}, u32[]{:S(2)}, u32[]{:S(2)}) collective-permute-start(bf16[640,512]{1,0:T(8,128)(2,1)S(1)} %pad_maximum_fusion.refs_0_.refs_2_.refs_8_), channel_id=1, source_target_pairs={{0,2},{2,0},{1,3},{3,1},{4,6},{6,4},{5,7},{7,5},{8,10},{10,8},{9,1... | collective-permute-start | bytes 1966088 | tf_op jit(solution)/shard_map/ppermute | solution.py:518
  60.6 16.5 %collective-permute-start.11 = (bf16[256,512]{1,0:T(8,128)(2,1)S(1)}, bf16[256,512]{1,0:T(8,128)(2,1)}, u32[]{:S(2)}, u32[]{:S(2)}) collective-permute-start(bf16[256,512]{1,0:T(8,128)(2,1)S(1)} %whiten.3), channel_id=1, source_target_pairs={{0,12},{4,0},{8,4},{12,8},{1,13},{5,1},{9,5},{13,9},{2,14},{6,2},{... | collective-permute-start | bytes 786440 | tf_op jit(solution)/shard_map/ppermute | solution.py:516
  62.3 14.8 %collective-permute-start.9 = (bf16[384,512]{1,0:T(8,128)(2,1)S(1)}, bf16[384,512]{1,0:T(8,128)(2,1)S(1)}, u32[]{:S(2)}, u32[]{:S(2)}) collective-permute-start(bf16[384,512]{1,0:T(8,128)(2,1)S(1)} %whiten.2), channel_id=1, source_target_pairs={{0,4},{4,8},{8,12},{12,0},{1,5},{5,9},{9,13},{13,1},{2,6},{6,10},{... | collective-permute-start | bytes 1179656 | tf_op jit(solution)/shard_map/ppermute | solution.py:515
  62.6 17.9 %collective-permute-start.6 = (bf16[640,512]{1,0:T(8,128)(2,1)S(1)}, bf16[640,512]{1,0:T(8,128)(2,1)S(1)}, u32[]{:S(2)}, u32[]{:S(2)}) collective-permute-start(bf16[640,512]{1,0:T(8,128)(2,1)S(1)} %pad_maximum_fusion.refs_0_.refs_2_.refs_8_), channel_id=1, source_target_pairs={{0,1},{1,0},{2,3},{3,2},{4,5},{5,4},{6,7},{7,6},{8,9},{9,8},{10,11... | collective-permute-start | bytes 1966088 | tf_op jit(solution)/shard_map/ppermute | solution.py:517
  75.8 4.8 %collective-permute-start.8 = (bf16[640,512]{1,0:T(8,128)(2,1)S(1)}, bf16[640,512]{1,0:T(8,128)(2,1)}, u32[]{:S(2)}, u32[]{:S(2)}) collective-permute-start(bf16[640,512]{1,0:T(8,128)(2,1)S(1)} %collective-permute-done.7.refs_2_), channel_id=1, source_target_pairs={{0,1},{1,0},{2,3},{3,2},{4,5},{5,4},{6,7},{7,6},{8,9},{9,8},{10,11... | collective-permute-start | bytes 1966088 | tf_op jit(solution)/shard_map/ppermute | solution.py:523
  77.1 2.0 %collective-permute-start.12 = (bf16[256,512]{1,0:T(8,128)(2,1)}, bf16[256,512]{1,0:T(8,128)(2,1)S(1)}, u32[]{:S(2)}, u32[]{:S(2)}) collective-permute-start(bf16[256,512]{1,0:T(8,128)(2,1)} %collective-permute-done.11.refs_6_), channel_id=1, source_target_pairs={{0,1},{1,0},{2,3},{3,2},{4,5},{5,4},{6,7},{7,6},{8,9},{9,8},{10,11... | collective-permute-start | bytes 786440 | tf_op jit(solution)/shard_map/ppermute | solution.py:522
  77.1 3.5 %collective-permute-start.10 = (bf16[384,512]{1,0:T(8,128)(2,1)S(1)}, bf16[384,512]{1,0:T(8,128)(2,1)S(1)}, u32[]{:S(2)}, u32[]{:S(2)}) collective-permute-start(bf16[384,512]{1,0:T(8,128)(2,1)S(1)} %collective-permute-done.9.refs_4_.refs_2_), channel_id=1, source_target_pairs={{0,1},{1,0},{2,3},{3,2},{4,5},{5,4},{6,7},{7,6},{8,9},{9,8},{10,11... | collective-permute-start | bytes 1179656 | tf_op jit(solution)/shard_map/ppermute | solution.py:521
  77.6 13.8 %collective-permute-start.15 = (bf16[256,512]{1,0:T(8,128)(2,1)}, bf16[256,512]{1,0:T(8,128)(2,1)S(1)}, u32[]{:S(2)}, u32[]{:S(2)}) collective-permute-start(bf16[256,512]{1,0:T(8,128)(2,1)} %collective-permute-done.11.refs_6_), channel_id=1, source_target_pairs={{0,12},{4,0},{8,4},{12,8},{1,13},{5,1},{9,5},{13,9},{2,14},{6,2},{... | collective-permute-start | bytes 786440 | tf_op jit(solution)/shard_map/ppermute | solution.py:520
  79.1 0.7 copy-start
  79.8 15.1 %collective-permute-start.13 = (bf16[384,512]{1,0:T(8,128)(2,1)S(1)}, bf16[384,512]{1,0:T(8,128)(2,1)S(1)}, u32[]{:S(2)}, u32[]{:S(2)}) collective-permute-start(bf16[384,512]{1,0:T(8,128)(2,1)S(1)} %collective-permute-done.9.refs_4_.refs_2_), channel_id=1, source_target_pairs={{0,4},{4,8},{8,12},{12,0},{1,5},{5,9},{9,13},{13,1},{2,6},{6,10},{... | collective-permute-start | bytes 1179656 | tf_op jit(solution)/shard_map/ppermute | solution.py:519
  80.6 1.0 copy-start.1
  91.4 10.7 %collective-permute-start.16 = (bf16[256,512]{1,0:T(8,128)(2,1)S(1)}, bf16[256,512]{1,0:T(8,128)(2,1)S(1)}, u32[]{:S(2)}, u32[]{:S(2)}) collective-permute-start(bf16[256,512]{1,0:T(8,128)(2,1)S(1)} %collective-permute-done.15.refs_6_.refs_10_), channel_id=1, source_target_pairs={{0,1},{1,0},{2,3},{3,2},{4,5},{5,4},{6,7},{7,6},{8,9},{9,8},{10,11... | collective-permute-start | bytes 786440 | tf_op jit(solution)/shard_map/ppermute | solution.py:551
  95.0 11.6 %collective-permute-start.14 = (bf16[384,512]{1,0:T(8,128)(2,1)S(1)}, bf16[384,512]{1,0:T(8,128)(2,1)}, u32[]{:S(2)}, u32[]{:S(2)}) collective-permute-start(bf16[384,512]{1,0:T(8,128)(2,1)S(1)} %collective-permute-done.13.refs_4_), channel_id=1, source_target_pairs={{0,1},{1,0},{2,3},{3,2},{4,5},{5,4},{6,7},{7,6},{8,9},{9,8},{10,11... | collective-permute-start | bytes 1179656 | tf_op jit(solution)/shard_map/ppermute | solution.py:550
  95.0 22.3 %collective-permute-start.17 = (bf16[384,512]{1,0:T(8,128)(2,1)S(1)}, bf16[384,512]{1,0:T(8,128)(2,1)S(1)}, u32[]{:S(2)}, u32[]{:S(2)}) collective-permute-start(bf16[384,512]{1,0:T(8,128)(2,1)S(1)} %collective-permute-done.13.refs_4_), channel_id=1, source_target_pairs={{1,5},{5,9},{8,12},{12,0},{3,7},{7,11},{10,14},{14,2},{17,21},{21,... | collective-permute-start | bytes 1179656 | tf_op jit(solution)/shard_map/ppermute | solution.py:511
  96.3 21.0 %collective-permute-start.18 = (bf16[384,512]{1,0:T(8,128)(2,1)S(1)}, bf16[384,512]{1,0:T(8,128)(2,1)}, u32[]{:S(2)}, u32[]{:S(2)}) collective-permute-start(bf16[384,512]{1,0:T(8,128)(2,1)S(1)} %collective-permute-done.13.refs_4_), channel_id=1, source_target_pairs={{0,5},{4,9},{9,12},{13,0},{2,7},{6,11},{11,14},{15,2},{16,21},{20,... | collective-permute-start | bytes 1179656 | tf_op jit(solution)/shard_map/ppermute | solution.py:511
  100.7 16.5 %collective-permute-start.19 = (bf16[256,512]{1,0:T(8,128)(2,1)S(1)}, bf16[256,512]{1,0:T(8,128)(2,1)}, u32[]{:S(2)}, u32[]{:S(2)}) collective-permute-start(bf16[256,512]{1,0:T(8,128)(2,1)S(1)} %collective-permute-done.15.refs_6_.refs_10_), channel_id=1, source_target_pairs={{1,13},{5,1},{8,4},{12,8},{3,15},{7,3},{10,6},{14,10},{17,29},{21,... | collective-permute-start | bytes 786440 | tf_op jit(solution)/shard_map/ppermute | solution.py:511
  102.1 15.1 %collective-permute-start.20 = (bf16[256,512]{1,0:T(8,128)(2,1)S(1)}, bf16[256,512]{1,0:T(8,128)(2,1)}, u32[]{:S(2)}, u32[]{:S(2)}) collective-permute-start(bf16[256,512]{1,0:T(8,128)(2,1)S(1)} %collective-permute-done.15.refs_6_.refs_10_), channel_id=1, source_target_pairs={{0,13},{4,1},{9,4},{13,8},{2,15},{6,3},{11,6},{15,10},{16,29},{20,... | collective-permute-start | bytes 786440 | tf_op jit(solution)/shard_map/ppermute | solution.py:511

commit v6 on v5

--- a/solution.py
+++ b/solution.py
@@ -18,9 +18,9 @@
 MIB = 1024 * 1024
 SPECTRA_VMEM = 18 * MIB
 SMALL_VMEM = 8 * MIB
-PRODUCT_VMEM = 16 * MIB
+PRODUCT_VMEM = 20 * MIB
 SMALL = pl.CostEstimate(flops=1000, bytes_accessed=1000, transcendentals=0)
-TILES = 3
+TILES = 4
 AHEAD = 5
 ROWS_KEPT = 48
 FINE = 64

time: 127 us -> 127 us (level)
  no operation moved by 1% of the time
where the time goes in v6:
time: 127 us
  Pallas kernels  64 us (50%)
  starting transfers between devices  28.9 us (23%)
  waiting for transfers between devices  27 us (21%)
  other arithmetic  3.47 us (3%)
  local copies, waits for them, and re-layouts  2.65 us (2%)
    pallas_call x4, Pallas kernels, spectra_call(): pl.pallas_call(functools.partial(spectra_kernel, with_table, firsts, size...  33.8 us
    pallas_call x2, Pallas kernels, product_call(): pl.pallas_call(functools.partial(product_kernel, gather, widths, scale, f...  19.7 us
    ppermute x1, waiting for transfers between devices, local_rings(): far = lax.ppermute(white, 'col', swap)  13.1 us
    ppermute x4, starting transfers between devices, last_step(): lax.ppermute(part, axes, pairs(n - 2, move, cross))  11.4 us
    pallas_call x1, Pallas kernels, first_call(): pl.pallas_call(functools.partial(first_kernel, gather, scale, len(parts))...  9.84 us
    ppermute x3, starting transfers between devices, local_rings(): left = lax.ppermute(left, 'row', to_left)  9.11 us
    ppermute x3, waiting for transfers between devices, local_rings(): left = lax.ppermute(left, 'row', to_left)  6.67 us
    ppermute x1, waiting for transfers between devices, local_rings(): right1 = lax.ppermute(right0, 'row', to_right)  3.5 us
  transfers between devices with their start and end apart: 21, of which 8 were waited for; matrix products, arithmetic and copies ran while one was open for 3% of the time, Pallas kernels for 36%

profile of v6, /device:TPU:0, one launch (start us, length us, event | category | flops | bytes accessed | tf_op | source)
XLA Modules:
  0.0 126.5 jit_solution(11367484459677397353)
XLA Ops:
  0.1 0.7 copy-done.2
  0.7 8.5 %spectra.4 = (bf16[384,512]{1,0:T(8,128)(2,1)S(1)}, bf16[256,512]{1,0:T(8,128)(2,1)S(1)}, bf16[4096,256]{1,0:T(8,128)(2,1)S(1)}) custom-call(s32[3]{0:T(128)S(1)} %get-tuple-element.41.where_ref, s32[1,128]{1,0:T(1,128)S(1)} %bitcast.19, bf16[2,2560,4096]{2,1,0:T(8,128)(2,1)} %traces_ref.7), custom_call_target="tpu_custom_call" | custom-call | flops 1000 | bytes 1000 | tf_op jit(solution)/shard_map/spectra/pallas_call | solution.py:180
  9.2 3.1 %collective-permute-start = (bf16[384,512]{1,0:T(8,128)(2,1)S(1)}, bf16[384,512]{1,0:T(8,128)(2,1)S(1)}, u32[]{:S(2)}, u32[]{:S(2)}) collective-permute-start(bf16[384,512]{1,0:T(8,128)(2,1)S(1)} %get-tuple-element.22), channel_id=1, source_target_pairs={{0,4},{4,8},{8,12},{12,0},{1,5},{5,9},{9,13},{13,1},{2,6},{6,10},{... | collective-permute-start | bytes 1179656 | tf_op jit(solution)/shard_map/ppermute | solution.py:492
  12.3 2.1 %collective-permute-start.2 = (bf16[256,512]{1,0:T(8,128)(2,1)S(1)}, bf16[256,512]{1,0:T(8,128)(2,1)S(1)}, u32[]{:S(2)}, u32[]{:S(2)}) collective-permute-start(bf16[256,512]{1,0:T(8,128)(2,1)S(1)} %get-tuple-element.25), channel_id=1, source_target_pairs={{0,12},{4,0},{8,4},{12,8},{1,13},{5,1},{9,5},{13,9},{2,14},{6,2},{... | collective-permute-start | bytes 786440 | tf_op jit(solution)/shard_map/ppermute | solution.py:493
  14.4 8.5 %spectra.5 = (f32[384,512]{1,0:T(8,128)S(1)}, f32[256,512]{1,0:T(8,128)S(1)}) custom-call(s32[3]{0:T(128)S(1)} %get-tuple-element.42.where_ref, bf16[4096,256]{1,0:T(8,128)(2,1)S(1)} %get-tuple-element.23.bins_or_table, bf16[2,2560,4096]{2,1,0:T(8,128)(2,1)} %traces_ref.7), custom_call_target="tpu_custom_call" | custom-call | flops 1000 | bytes 1000 | tf_op jit(solution)/shard_map/spectra/pallas_call | solution.py:180
  22.8 1.5 %collective-permute-done = bf16[384,512]{1,0:T(8,128)(2,1)S(1)} collective-permute-done((bf16[384,512]{1,0:T(8,128)(2,1)S(1)}, bf16[384,512]{1,0:T(8,128)(2,1)S(1)}, u32[]{:S(2)}, u32[]{:S(2)}) %collective-permute-start) | collective-permute-done | bytes 393248 | tf_op jit(solution)/shard_map/ppermute | solution.py:492
  24.6 4.1 %collective-permute-done.2 = bf16[256,512]{1,0:T(8,128)(2,1)S(1)} collective-permute-done((bf16[256,512]{1,0:T(8,128)(2,1)S(1)}, bf16[256,512]{1,0:T(8,128)(2,1)S(1)}, u32[]{:S(2)}, u32[]{:S(2)}) %collective-permute-start.2) | collective-permute-done | bytes 262176 | tf_op jit(solution)/shard_map/ppermute | solution.py:493
  28.8 3.1 %collective-permute-start.4 = (bf16[256,512]{1,0:T(8,128)(2,1)S(1)}, bf16[256,512]{1,0:T(8,128)(2,1)S(1)}, u32[]{:S(2)}, u32[]{:S(2)}) collective-permute-start(bf16[256,512]{1,0:T(8,128)(2,1)S(1)} %add_convert_fusion.3), channel_id=1, source_target_pairs={{0,12},{4,0},{8,4},{12,8},{1,13},{5,1},{9,5},{13,9},{2,14},{6,2},{... | collective-permute-start | bytes 786440 | tf_op jit(solution)/shard_map/ppermute | solution.py:493
  31.9 8.5 %spectra.6 = (f32[384,512]{1,0:T(8,128)S(1)}, f32[256,512]{1,0:T(8,128)S(1)}) custom-call(s32[3]{0:T(128)S(1)} %pad_add_fusion.5.where_ref, bf16[4096,256]{1,0:T(8,128)(2,1)S(1)} %get-tuple-element.23.bins_or_table, bf16[2,2560,4096]{2,1,0:T(8,128)(2,1)} %traces_ref.7), custom_call_target="tpu_custom_call" | custom-call | flops 1000 | bytes 1000 | tf_op jit(solution)/shard_map/spectra/pallas_call | solution.py:180
  40.4 1.9 %add_convert_fusion = bf16[384,512]{1,0:T(8,128)(2,1)} fusion(f32[384,512]{1,0:T(8,128)S(1)} %get-tuple-element.28, bf16[384,512]{1,0:T(8,128)(2,1)} %collective-permute-done.1), kind=kLoop, calls=%fused_computation | loop fusion | flops 589824 | bytes 1572864 | tf_op jit(solution)/shard_map/convert_element_type | solution.py:495
  42.3 0.9 collective-permute-done.4
  43.2 3.9 %collective-permute-start.5 = (bf16[256,512]{1,0:T(8,128)(2,1)S(1)}, bf16[256,512]{1,0:T(8,128)(2,1)S(1)}, u32[]{:S(2)}, u32[]{:S(2)}) collective-permute-start(bf16[256,512]{1,0:T(8,128)(2,1)S(1)} %add_convert_fusion.2), channel_id=1, source_target_pairs={{0,12},{4,0},{8,4},{12,8},{1,13},{5,1},{9,5},{13,9},{2,14},{6,2},{... | collective-permute-start | bytes 786440 | tf_op jit(solution)/shard_map/ppermute | solution.py:493
  47.1 0.8 dynamic-slice_convert_fusion
  48.3 8.5 %spectra.7 = (f32[384,512]{1,0:T(8,128)S(1)}, f32[256,512]{1,0:T(8,128)S(1)}) custom-call(s32[3]{0:T(128)S(1)} %pad_add_fusion.6.where_ref, bf16[4096,256]{1,0:T(8,128)(2,1)S(1)} %get-tuple-element.23.bins_or_table, bf16[2,2560,4096]{2,1,0:T(8,128)(2,1)} %traces_ref.7), custom_call_target="tpu_custom_call" | custom-call | flops 1000 | bytes 1000 | tf_op jit(solution)/shard_map/spectra/pallas_call | solution.py:180
  56.7 1.7 %collective-permute-done.5.got = bf16[256,512]{1,0:T(8,128)(2,1)S(1)} collective-permute-done((bf16[256,512]{1,0:T(8,128)(2,1)S(1)}, bf16[256,512]{1,0:T(8,128)(2,1)S(1)}, u32[]{:S(2)}, u32[]{:S(2)}) %collective-permute-start.5) | collective-permute-done | bytes 262176 | tf_op jit(solution)/shard_map/ppermute | solution.py:493
  59.1 1.6 %collective-permute-start.7 = (bf16[640,512]{1,0:T(8,128)(2,1)S(1)}, bf16[640,512]{1,0:T(8,128)(2,1)S(1)}, u32[]{:S(2)}, u32[]{:S(2)}) collective-permute-start(bf16[640,512]{1,0:T(8,128)(2,1)S(1)} %pad_maximum_fusion.refs_0_.refs_2_.refs_8_), channel_id=1, source_target_pairs={{0,2},{2,0},{1,3},{3,1},{4,6},{6,4},{5,7},{7,5},{8,10},{10,8},{9,1... | collective-permute-start | bytes 1966088 | tf_op jit(solution)/shard_map/ppermute | solution.py:518
  60.6 1.7 %collective-permute-start.11 = (bf16[256,512]{1,0:T(8,128)(2,1)S(1)}, bf16[256,512]{1,0:T(8,128)(2,1)}, u32[]{:S(2)}, u32[]{:S(2)}) collective-permute-start(bf16[256,512]{1,0:T(8,128)(2,1)S(1)} %whiten.3), channel_id=1, source_target_pairs={{0,12},{4,0},{8,4},{12,8},{1,13},{5,1},{9,5},{13,9},{2,14},{6,2},{... | collective-permute-start | bytes 786440 | tf_op jit(solution)/shard_map/ppermute | solution.py:516
  62.6 13.1 %collective-permute-done.7.refs_2_ = bf16[640,512]{1,0:T(8,128)(2,1)S(1)} collective-permute-done((bf16[640,512]{1,0:T(8,128)(2,1)S(1)}, bf16[640,512]{1,0:T(8,128)(2,1)S(1)}, u32[]{:S(2)}, u32[]{:S(2)}) %collective-permute-start.7) | collective-permute-done | bytes 655392 | tf_op jit(solution)/shard_map/ppermute | solution.py:518
  75.8 1.3 %collective-permute-done.11.refs_6_ = bf16[256,512]{1,0:T(8,128)(2,1)} collective-permute-done((bf16[256,512]{1,0:T(8,128)(2,1)S(1)}, bf16[256,512]{1,0:T(8,128)(2,1)}, u32[]{:S(2)}, u32[]{:S(2)}) %collective-permute-start.11) | collective-permute-done | bytes 262176 | tf_op jit(solution)/shard_map/ppermute | solution.py:516
  77.1 0.5 collective-permute-start.10
  77.6 0.6 collective-permute-start.15
  78.2 0.9 collective-permute-done.12.refs_7_
  79.1 0.7 copy-done
  80.6 0.9 copy-done.1
  81.5 9.8 %turn_products.1 = (f32[4,1280,1280]{2,1,0:T(8,128)}, bf16[48,640,1024]{2,1,0:T(8,128)(2,1)}) custom-call(s32[4]{0:T(128)S(1)} %pad_add_fusion.2.info, f32[4,128]{1,0:T(4,128)S(1)} %get-tuple-element.40.cos_ref, f32[4,128]{1,0:T(4,128)S(1)} %get-tuple-element.39.sin_ref, bf16[640,512]{1,0:T(8,128)(2,1)S(1)} %pad_maximum_fusion.refs_0_.refs_2_.refs_8_, ...), custom_call_target="tpu_custom_call" | custom-call | flops 1000 | bytes 1000 | tf_op jit(solution)/shard_map/turn_products/pallas_call | solution.py:301
  91.5 3.5 %collective-permute-done.13.refs_4_ = bf16[384,512]{1,0:T(8,128)(2,1)S(1)} collective-permute-done((bf16[384,512]{1,0:T(8,128)(2,1)S(1)}, bf16[384,512]{1,0:T(8,128)(2,1)S(1)}, u32[]{:S(2)}, u32[]{:S(2)}) %collective-permute-start.13) | collective-permute-done | bytes 393248 | tf_op jit(solution)/shard_map/ppermute | solution.py:519
  95.0 1.3 %collective-permute-start.17 = (bf16[384,512]{1,0:T(8,128)(2,1)S(1)}, bf16[384,512]{1,0:T(8,128)(2,1)S(1)}, u32[]{:S(2)}, u32[]{:S(2)}) collective-permute-start(bf16[384,512]{1,0:T(8,128)(2,1)S(1)} %collective-permute-done.13.refs_4_), channel_id=1, source_target_pairs={{1,5},{5,9},{8,12},{12,0},{3,7},{7,11},{10,14},{14,2},{17,21},{21,... | collective-permute-start | bytes 1179656 | tf_op jit(solution)/shard_map/ppermute | solution.py:511
  96.3 4.4 %collective-permute-start.18 = (bf16[384,512]{1,0:T(8,128)(2,1)S(1)}, bf16[384,512]{1,0:T(8,128)(2,1)}, u32[]{:S(2)}, u32[]{:S(2)}) collective-permute-start(bf16[384,512]{1,0:T(8,128)(2,1)S(1)} %collective-permute-done.13.refs_4_), channel_id=1, source_target_pairs={{0,5},{4,9},{9,12},{13,0},{2,7},{6,11},{11,14},{15,2},{16,21},{20,... | collective-permute-start | bytes 1179656 | tf_op jit(solution)/shard_map/ppermute | solution.py:511
  100.7 1.4 %collective-permute-start.19 = (bf16[256,512]{1,0:T(8,128)(2,1)S(1)}, bf16[256,512]{1,0:T(8,128)(2,1)}, u32[]{:S(2)}, u32[]{:S(2)}) collective-permute-start(bf16[256,512]{1,0:T(8,128)(2,1)S(1)} %collective-permute-done.15.refs_6_.refs_10_), channel_id=1, source_target_pairs={{1,13},{5,1},{8,4},{12,8},{3,15},{7,3},{10,6},{14,10},{17,29},{21,... | collective-permute-start | bytes 786440 | tf_op jit(solution)/shard_map/ppermute | solution.py:511
  102.1 4.3 %collective-permute-start.20 = (bf16[256,512]{1,0:T(8,128)(2,1)S(1)}, bf16[256,512]{1,0:T(8,128)(2,1)}, u32[]{:S(2)}, u32[]{:S(2)}) collective-permute-start(bf16[256,512]{1,0:T(8,128)(2,1)S(1)} %collective-permute-done.15.refs_6_.refs_10_), channel_id=1, source_target_pairs={{0,13},{4,1},{9,4},{13,8},{2,15},{6,3},{11,6},{15,10},{16,29},{20,... | collective-permute-start | bytes 786440 | tf_op jit(solution)/shard_map/ppermute | solution.py:511
  106.5 10.7 %products.2 = (f32[4,1280,1280]{2,1,0:T(8,128)}, bf16[8,640,1024]{2,1,0:T(8,128)(2,1)S(1)}) custom-call(s32[4]{0:T(128)S(1)} %pad_add_fusion.refs_0_, bf16[48,640,1024]{2,1,0:T(8,128)(2,1)} %get-tuple-element.33.refs_1_, bf16[640,512]{1,0:T(8,128)(2,1)S(1)} %pad_maximum_fusion.refs_0_.refs_2_.refs_8_, ...), custom_call_target="tpu_custom_call", output_to_operand_aliasing={{0}: (8, {})} | custom-call | flops 1000 | bytes 1000 | tf_op jit(solution)/shard_map/products/pallas_call | solution.py:393
  117.2 9.1 %products.3 = f32[4,1280,1280]{2,1,0:T(8,128)} custom-call(s32[6]{0:T(128)S(1)} %stack.95.refs_0_, bf16[8,640,1024]{2,1,0:T(8,128)(2,1)S(1)} %get-tuple-element.37.refs_1_, bf16[384,512]{1,0:T(8,128)(2,1)S(1)} %collective-permute-done.9.refs_4_.refs_2_, ...), custom_call_target="tpu_custom_call", output_to_operand_aliasing={{}: (12, {})} | custom-call | flops 1000 | bytes 1000 | tf_op jit(solution)/shard_map/products/pallas_call | solution.py:393
  (46 shorter events, 2.7 us)
Async XLA Ops:
  0.1 0.7 copy-start.2
  9.2 15.1 %collective-permute-start = (bf16[384,512]{1,0:T(8,128)(2,1)S(1)}, bf16[384,512]{1,0:T(8,128)(2,1)S(1)}, u32[]{:S(2)}, u32[]{:S(2)}) collective-permute-start(bf16[384,512]{1,0:T(8,128)(2,1)S(1)} %get-tuple-element.22), channel_id=1, source_target_pairs={{0,4},{4,8},{8,12},{12,0},{1,5},{5,9},{9,13},{13,1},{2,6},{6,10},{... | collective-permute-start | bytes 1179656 | tf_op jit(solution)/shard_map/ppermute | solution.py:492
  12.3 16.4 %collective-permute-start.2 = (bf16[256,512]{1,0:T(8,128)(2,1)S(1)}, bf16[256,512]{1,0:T(8,128)(2,1)S(1)}, u32[]{:S(2)}, u32[]{:S(2)}) collective-permute-start(bf16[256,512]{1,0:T(8,128)(2,1)S(1)} %get-tuple-element.25), channel_id=1, source_target_pairs={{0,12},{4,0},{8,4},{12,8},{1,13},{5,1},{9,5},{13,9},{2,14},{6,2},{... | collective-permute-start | bytes 786440 | tf_op jit(solution)/shard_map/ppermute | solution.py:493
  24.4 15.9 %collective-permute-start.1 = (bf16[384,512]{1,0:T(8,128)(2,1)S(1)}, bf16[384,512]{1,0:T(8,128)(2,1)}, u32[]{:S(2)}, u32[]{:S(2)}) collective-permute-start(bf16[384,512]{1,0:T(8,128)(2,1)S(1)} %add_convert_fusion.1), channel_id=1, source_target_pairs={{0,4},{4,8},{8,12},{12,0},{1,5},{5,9},{9,13},{13,1},{2,6},{6,10},{... | collective-permute-start | bytes 1179656 | tf_op jit(solution)/shard_map/ppermute | solution.py:492
  28.8 14.4 %collective-permute-start.4 = (bf16[256,512]{1,0:T(8,128)(2,1)S(1)}, bf16[256,512]{1,0:T(8,128)(2,1)S(1)}, u32[]{:S(2)}, u32[]{:S(2)}) collective-permute-start(bf16[256,512]{1,0:T(8,128)(2,1)S(1)} %add_convert_fusion.3), channel_id=1, source_target_pairs={{0,12},{4,0},{8,4},{12,8},{1,13},{5,1},{9,5},{13,9},{2,14},{6,2},{... | collective-permute-start | bytes 786440 | tf_op jit(solution)/shard_map/ppermute | solution.py:493
  40.3 40.1 %copy-start.3 = (s32[128]{0:T(128)S(1)}, s32[128]{0:T(128)}, u32[]{:S(2)}) copy-start(s32[128]{0:T(128)} %param.6) | copy-start | bytes 1540
  40.4 40.1 %copy-start.4 = (s32[4]{0:T(128)S(1)}, s32[4]{0:T(128)}, u32[]{:S(2)}) copy-start(s32[4]{0:T(128)} %constant.125.clone) | copy-start | bytes 52
  42.3 16.4 %collective-permute-start.3 = (bf16[384,512]{1,0:T(8,128)(2,1)}, bf16[384,512]{1,0:T(8,128)(2,1)S(1)}, u32[]{:S(2)}, u32[]{:S(2)}) collective-permute-start(bf16[384,512]{1,0:T(8,128)(2,1)} %add_convert_fusion), channel_id=1, source_target_pairs={{0,4},{4,8},{8,12},{12,0},{1,5},{5,9},{9,13},{13,1},{2,6},{6,10},{... | collective-permute-start | bytes 1179656 | tf_op jit(solution)/shard_map/ppermute | solution.py:492
  43.2 15.2 %collective-permute-start.5 = (bf16[256,512]{1,0:T(8,128)(2,1)S(1)}, bf16[256,512]{1,0:T(8,128)(2,1)S(1)}, u32[]{:S(2)}, u32[]{:S(2)}) collective-permute-start(bf16[256,512]{1,0:T(8,128)(2,1)S(1)} %add_convert_fusion.2), channel_id=1, source_target_pairs={{0,12},{4,0},{8,4},{12,8},{1,13},{5,1},{9,5},{13,9},{2,14},{6,2},{... | collective-permute-start | bytes 786440 | tf_op jit(solution)/shard_map/ppermute | solution.py:493
  59.1 16.7 %collective-permute-start.7 = (bf16[640,512]{1,0:T(8,128)(2,1)S(1)}, bf16[640,512]{1,0:T(8,128)(2,1)S(1)}, u32[]{:S(2)}, u32[]{:S(2)}) collective-permute-start(bf16[640,512]{1,0:T(8,128)(2,1)S(1)} %pad_maximum_fusion.refs_0_.refs_2_.refs_8_), channel_id=1, source_target_pairs={{0,2},{2,0},{1,3},{3,1},{4,6},{6,4},{5,7},{7,5},{8,10},{10,8},{9,1... | collective-permute-start | bytes 1966088 | tf_op jit(solution)/shard_map/ppermute | solution.py:518
  60.6 16.5 %collective-permute-start.11 = (bf16[256,512]{1,0:T(8,128)(2,1)S(1)}, bf16[256,512]{1,0:T(8,128)(2,1)}, u32[]{:S(2)}, u32[]{:S(2)}) collective-permute-start(bf16[256,512]{1,0:T(8,128)(2,1)S(1)} %whiten.3), channel_id=1, source_target_pairs={{0,12},{4,0},{8,4},{12,8},{1,13},{5,1},{9,5},{13,9},{2,14},{6,2},{... | collective-permute-start | bytes 786440 | tf_op jit(solution)/shard_map/ppermute | solution.py:516
  62.3 14.8 %collective-permute-start.9 = (bf16[384,512]{1,0:T(8,128)(2,1)S(1)}, bf16[384,512]{1,0:T(8,128)(2,1)S(1)}, u32[]{:S(2)}, u32[]{:S(2)}) collective-permute-start(bf16[384,512]{1,0:T(8,128)(2,1)S(1)} %whiten.2), channel_id=1, source_target_pairs={{0,4},{4,8},{8,12},{12,0},{1,5},{5,9},{9,13},{13,1},{2,6},{6,10},{... | collective-permute-start | bytes 1179656 | tf_op jit(solution)/shard_map/ppermute | solution.py:515
  62.6 17.9 %collective-permute-start.6 = (bf16[640,512]{1,0:T(8,128)(2,1)S(1)}, bf16[640,512]{1,0:T(8,128)(2,1)S(1)}, u32[]{:S(2)}, u32[]{:S(2)}) collective-permute-start(bf16[640,512]{1,0:T(8,128)(2,1)S(1)} %pad_maximum_fusion.refs_0_.refs_2_.refs_8_), channel_id=1, source_target_pairs={{0,1},{1,0},{2,3},{3,2},{4,5},{5,4},{6,7},{7,6},{8,9},{9,8},{10,11... | collective-permute-start | bytes 1966088 | tf_op jit(solution)/shard_map/ppermute | solution.py:517
  75.8 4.8 %collective-permute-start.8 = (bf16[640,512]{1,0:T(8,128)(2,1)S(1)}, bf16[640,512]{1,0:T(8,128)(2,1)}, u32[]{:S(2)}, u32[]{:S(2)}) collective-permute-start(bf16[640,512]{1,0:T(8,128)(2,1)S(1)} %collective-permute-done.7.refs_2_), channel_id=1, source_target_pairs={{0,1},{1,0},{2,3},{3,2},{4,5},{5,4},{6,7},{7,6},{8,9},{9,8},{10,11... | collective-permute-start | bytes 1966088 | tf_op jit(solution)/shard_map/ppermute | solution.py:523
  77.1 2.0 %collective-permute-start.12 = (bf16[256,512]{1,0:T(8,128)(2,1)}, bf16[256,512]{1,0:T(8,128)(2,1)S(1)}, u32[]{:S(2)}, u32[]{:S(2)}) collective-permute-start(bf16[256,512]{1,0:T(8,128)(2,1)} %collective-permute-done.11.refs_6_), channel_id=1, source_target_pairs={{0,1},{1,0},{2,3},{3,2},{4,5},{5,4},{6,7},{7,6},{8,9},{9,8},{10,11... | collective-permute-start | bytes 786440 | tf_op jit(solution)/shard_map/ppermute | solution.py:522
  77.1 3.5 %collective-permute-start.10 = (bf16[384,512]{1,0:T(8,128)(2,1)S(1)}, bf16[384,512]{1,0:T(8,128)(2,1)S(1)}, u32[]{:S(2)}, u32[]{:S(2)}) collective-permute-start(bf16[384,512]{1,0:T(8,128)(2,1)S(1)} %collective-permute-done.9.refs_4_.refs_2_), channel_id=1, source_target_pairs={{0,1},{1,0},{2,3},{3,2},{4,5},{5,4},{6,7},{7,6},{8,9},{9,8},{10,11... | collective-permute-start | bytes 1179656 | tf_op jit(solution)/shard_map/ppermute | solution.py:521
  77.6 13.8 %collective-permute-start.15 = (bf16[256,512]{1,0:T(8,128)(2,1)}, bf16[256,512]{1,0:T(8,128)(2,1)S(1)}, u32[]{:S(2)}, u32[]{:S(2)}) collective-permute-start(bf16[256,512]{1,0:T(8,128)(2,1)} %collective-permute-done.11.refs_6_), channel_id=1, source_target_pairs={{0,12},{4,0},{8,4},{12,8},{1,13},{5,1},{9,5},{13,9},{2,14},{6,2},{... | collective-permute-start | bytes 786440 | tf_op jit(solution)/shard_map/ppermute | solution.py:520
  79.1 0.7 copy-start
  79.8 15.1 %collective-permute-start.13 = (bf16[384,512]{1,0:T(8,128)(2,1)S(1)}, bf16[384,512]{1,0:T(8,128)(2,1)S(1)}, u32[]{:S(2)}, u32[]{:S(2)}) collective-permute-start(bf16[384,512]{1,0:T(8,128)(2,1)S(1)} %collective-permute-done.9.refs_4_.refs_2_), channel_id=1, source_target_pairs={{0,4},{4,8},{8,12},{12,0},{1,5},{5,9},{9,13},{13,1},{2,6},{6,10},{... | collective-permute-start | bytes 1179656 | tf_op jit(solution)/shard_map/ppermute | solution.py:519
  80.6 1.0 copy-start.1
  91.4 10.7 %collective-permute-start.16 = (bf16[256,512]{1,0:T(8,128)(2,1)S(1)}, bf16[256,512]{1,0:T(8,128)(2,1)S(1)}, u32[]{:S(2)}, u32[]{:S(2)}) collective-permute-start(bf16[256,512]{1,0:T(8,128)(2,1)S(1)} %collective-permute-done.15.refs_6_.refs_10_), channel_id=1, source_target_pairs={{0,1},{1,0},{2,3},{3,2},{4,5},{5,4},{6,7},{7,6},{8,9},{9,8},{10,11... | collective-permute-start | bytes 786440 | tf_op jit(solution)/shard_map/ppermute | solution.py:551
  95.0 11.6 %collective-permute-start.14 = (bf16[384,512]{1,0:T(8,128)(2,1)S(1)}, bf16[384,512]{1,0:T(8,128)(2,1)}, u32[]{:S(2)}, u32[]{:S(2)}) collective-permute-start(bf16[384,512]{1,0:T(8,128)(2,1)S(1)} %collective-permute-done.13.refs_4_), channel_id=1, source_target_pairs={{0,1},{1,0},{2,3},{3,2},{4,5},{5,4},{6,7},{7,6},{8,9},{9,8},{10,11... | collective-permute-start | bytes 1179656 | tf_op jit(solution)/shard_map/ppermute | solution.py:550
  95.0 22.2 %collective-permute-start.17 = (bf16[384,512]{1,0:T(8,128)(2,1)S(1)}, bf16[384,512]{1,0:T(8,128)(2,1)S(1)}, u32[]{:S(2)}, u32[]{:S(2)}) collective-permute-start(bf16[384,512]{1,0:T(8,128)(2,1)S(1)} %collective-permute-done.13.refs_4_), channel_id=1, source_target_pairs={{1,5},{5,9},{8,12},{12,0},{3,7},{7,11},{10,14},{14,2},{17,21},{21,... | collective-permute-start | bytes 1179656 | tf_op jit(solution)/shard_map/ppermute | solution.py:511
  96.3 21.0 %collective-permute-start.18 = (bf16[384,512]{1,0:T(8,128)(2,1)S(1)}, bf16[384,512]{1,0:T(8,128)(2,1)}, u32[]{:S(2)}, u32[]{:S(2)}) collective-permute-start(bf16[384,512]{1,0:T(8,128)(2,1)S(1)} %collective-permute-done.13.refs_4_), channel_id=1, source_target_pairs={{0,5},{4,9},{9,12},{13,0},{2,7},{6,11},{11,14},{15,2},{16,21},{20,... | collective-permute-start | bytes 1179656 | tf_op jit(solution)/shard_map/ppermute | solution.py:511
  100.7 16.5 %collective-permute-start.19 = (bf16[256,512]{1,0:T(8,128)(2,1)S(1)}, bf16[256,512]{1,0:T(8,128)(2,1)}, u32[]{:S(2)}, u32[]{:S(2)}) collective-permute-start(bf16[256,512]{1,0:T(8,128)(2,1)S(1)} %collective-permute-done.15.refs_6_.refs_10_), channel_id=1, source_target_pairs={{1,13},{5,1},{8,4},{12,8},{3,15},{7,3},{10,6},{14,10},{17,29},{21,... | collective-permute-start | bytes 786440 | tf_op jit(solution)/shard_map/ppermute | solution.py:511
  102.1 15.1 %collective-permute-start.20 = (bf16[256,512]{1,0:T(8,128)(2,1)S(1)}, bf16[256,512]{1,0:T(8,128)(2,1)}, u32[]{:S(2)}, u32[]{:S(2)}) collective-permute-start(bf16[256,512]{1,0:T(8,128)(2,1)S(1)} %collective-permute-done.15.refs_6_.refs_10_), channel_id=1, source_target_pairs={{0,13},{4,1},{9,4},{13,8},{2,15},{6,3},{11,6},{15,10},{16,29},{20,... | collective-permute-start | bytes 786440 | tf_op jit(solution)/shard_map/ppermute | solution.py:511
